TPU v7x, 256 devices: a whole 4x4x8 slice. The times are simulated.
256 devices in a mesh: fsdp: 64 (over z, x, y_lo), tp: 4 (over y_hi, core).
Axes of the slice: x: 4, y: 4 (y_hi: 2, y_lo: 2; y = y_hi * 2 + y_lo), z: 8, core: 2. Of those that a mesh axis runs over, the one named last changes fastest.
Arguments:
- grad: bfloat16 [4096, 8192], P('fsdp', 'tp'), may hold values from -6 to 6
- left_codes: bfloat16 [2, 2048, 2048], P(None, 'fsdp', 'tp'), may hold values from -0.125 to 0.125
- left_scale: bfloat16 [2, 2048], P(None, 'fsdp'), may hold values from 0.5 to 2
- right_codes: bfloat16 [4, 2048, 2048], P('tp', 'fsdp'), may hold values from -0.125 to 0.125
- right_scale: bfloat16 [4, 2048], P('tp', 'fsdp'), may hold values from 0.5 to 2
- moment1: float32 [4096, 8192], P('fsdp', 'tp'), may hold values from -3 to 3
- moment2: float32 [4096, 8192], P('fsdp', 'tp'), may hold values from 0.002 to 0.02
Outputs:
- update: float32 [4096, 8192], P('fsdp', 'tp')
- moment1_new: float32 [4096, 8192], P('fsdp', 'tp')
- moment2_new: float32 [4096, 8192], P('fsdp', 'tp')
All inputs are finite; a program needn't handle non-finite values.
Results may differ from a plain program's by a relative error of at most 0.00045.
Values may be sent and summed in bfloat16 or wider, within the bound.
No kernel may reach another device: no remote copies, remote signals or barrier semaphores. Data moves between devices by JAX's collectives and lax.ppermute only.
A program may use at most 128 MiB of HBM per device.

v0:
```python
import jax
import jax.numpy as jnp
from jax import lax
from jax.sharding import PartitionSpec as P

beta_one = 0.9
beta_two = 0.999
corr_one = 1.0 - 0.9**10
corr_two = 1.0 - 0.999**10
epsilon = 1e-08


def dequant(codes, scales):
    return codes.astype(jnp.float32) * scales.astype(jnp.float32)[..., None]


def body(grad, left_codes, left_scale, right_codes, right_scale, moment1, moment2):
    highest = lax.Precision.HIGHEST
    rows_dev, width = grad.shape
    fsdp_count = lax.axis_size("fsdp")
    total_rows = rows_dev * fsdp_count
    blocks = total_rows // width
    col_count = width // fsdp_count
    contract_last = (((1,), (1,)), ((), ()))
    copies = 1
    columns = lax.all_to_all(
        jnp.tile(grad.T, (copies, 1)), "fsdp", split_axis=0, concat_axis=1, tiled=True
    )
    full_codes = lax.all_gather(left_codes, "tp", axis=2, tiled=True)
    codes_all, scale_all = (
        lax.all_gather(full_codes, "fsdp", axis=1, tiled=True),
        lax.all_gather(left_scale, "fsdp", axis=1, tiled=True),
    )
    left_basis = dequant(codes_all, scale_all)
    col_data = columns.astype(jnp.float32).reshape(col_count, blocks, width)
    half_cols = jnp.einsum("cbi,bio->cbo", col_data, left_basis, precision=highest).reshape(
        col_count, total_rows
    )
    received = lax.all_to_all(half_cols, "fsdp", split_axis=1, concat_axis=0, tiled=True)
    half_rows = received.T
    right_all, right_scales = (
        lax.all_gather(right_codes[0], "fsdp", axis=0, tiled=True),
        lax.all_gather(right_scale[0], "fsdp", axis=0, tiled=True),
    )
    right_basis = dequant(right_all, right_scales)
    rotated = jnp.dot(half_rows, right_basis, precision=highest)
    first_new = beta_one * moment1 + (1.0 - beta_one) * rotated
    second_new = beta_two * moment2 + (1.0 - beta_two) * rotated * rotated
    direction = first_new / corr_one / (jnp.sqrt(second_new / corr_two) + epsilon)
    back_rows = lax.dot_general(direction, right_basis, contract_last, precision=highest)
    back_cols = lax.all_to_all(
        jnp.tile(back_rows.T, (copies, 1)), "fsdp", split_axis=0, concat_axis=1, tiled=True
    )
    update_cols = jnp.einsum(
        "cbo,bio->cbi", back_cols.reshape(col_count, blocks, width), left_basis, precision=highest
    ).reshape(col_count, total_rows)
    update_back = lax.all_to_all(update_cols, "fsdp", split_axis=1, concat_axis=0, tiled=True)
    update = update_back.T
    return (update, first_new, second_new)


def solution(mesh):
    return jax.shard_map(
        body,
        mesh=mesh,
        in_specs=(
            P("fsdp", "tp"),
            P(None, "fsdp", "tp"),
            P(None, "fsdp"),
            P("tp", "fsdp", None),
            P("tp", "fsdp"),
            P("fsdp", "tp"),
            P("fsdp", "tp"),
        ),
        out_specs=(P("fsdp", "tp"), P("fsdp", "tp"), P("fsdp", "tp")),
        check_vma=False,
    )
```

profile of v0, /device:TPU:8, one launch (start us, length us, event | category | flops | bytes accessed | tf_op | source)
XLA Modules:
  0.0 833.4 jit_solution(16503532091710669579)
XLA Ops:
  7.2 0.0 all-gather.6.cloned.1.call-start
  7.2 8.2 all_gather.15
  15.4 0.0 all-gather.6.cloned.1.call-update
  15.4 0.0 all-gather.8.cloned.1.call-start
  15.5 0.7 all-gather.8.cloned.1.call-update
  16.2 1.2 copy.36
  17.4 1.0 reshape.48
  18.4 12.9 %all-to-all-start = ((bf16[64,2,1024]{2,1,0:T(2,128)(2,1)}), bf16[64,2,1024]{2,1,0:T(2,128)(2,1)S(1)}, u32[]{:S(2)}, u32[]{:S(2)}) async-start(bf16[64,2,1024]{2,1,0:T(2,128)(2,1)} %reshape.48), calls=%async_computation | async-start | bytes 524288 | tf_op jit(solution)/shard_map/all_to_all | solution.py:26
  31.4 156.0 %all-gather.2 = bf16[64,32,2]{1,2,0:T(2,128)(2,1)S(1)} all-gather(bf16[1,32,2]{1,2,0:T(2,128)(2,1)} %bitcast.57), channel_id=1, replica_groups=mesh['fsdp'=64,'tp'=4] {'fsdp'}, dimensions={0}, use_global_device_ids=true | all-gather | bytes 8320 | tf_op jit(solution)/shard_map/all_gather | solution.py:32
  187.4 0.1 copy.34
  187.4 0.1 copy.35
  187.5 0.1 reshape.47
  187.7 0.3 reshape.49
  188.0 0.2 copy.37
  188.2 0.4 reshape.32
  188.6 204.7 %all-gather.6.cloned.1.call-done = bf16[2,2048,2048]{2,1,0:T(8,128)(2,1)} async-done(((bf16[2,32,2048]{2,1,0:T(8,128)(2,1)}), bf16[2,2048,2048]{2,1,0:T(8,128)(2,1)}) %all-gather.6.cloned.1.call-update) | async-done | bytes 16777232 | tf_op jit(solution)/shard_map/all_gather | solution.py:31
  393.3 17.1 %fusion.11 = f32[32,2,2048]{2,0,1:T(8,128)S(1)} fusion(bf16[2,2048,2048]{2,1,0:T(8,128)(2,1)} %all-gather.6.cloned.1.call-done, f32[2,2048]{1,0:T(2,128)S(1)} %bitcast.55, bf16[32,2,2048]{2,1,0:T(2,128)(2,1)S(1)} %reshape.32), kind=kOutput, calls=%fused_computation.13 | convolution fusion | flops 3238002688 | bytes 17580032 | tf_op jit(solution)/shard_map/cbi,bio->cbo/dot_general | solution.py:36
  410.5 0.4 copy.39
  410.9 0.6 all_to_all.55
  411.5 0.6 copy.55
  412.1 1.4 reshape.50
  413.6 10.4 %all-to-all-start.1 = ((f32[64,1,2048]{2,1,0:T(1,128)}), f32[64,1,2048]{2,1,0:T(1,128)S(1)}, u32[]{:S(2)}, u32[]{:S(2)}) async-start(f32[64,1,2048]{2,1,0:T(1,128)} %reshape.50), calls=%async_computation.1 | async-start | bytes 1048576 | tf_op jit(solution)/shard_map/all_to_all | solution.py:39
  424.0 0.6 dynamic-slice
  425.2 0.2 dynamic-update-slice
  425.5 160.2 %all-reduce = bf16[2048]{0:T(1024)(128)(2,1)S(1)} all-reduce(bf16[2048]{0:T(1024)(128)(2,1)S(1)} %dynamic-update-slice), channel_id=3, replica_groups=mesh['fsdp'=64,'tp'=4] {'fsdp'}, use_global_device_ids=true, to_apply=%add | all-reduce | flops 2048 | bytes 8192
  585.7 0.5 broadcast.6
  586.2 1.9 reduce
  588.1 0.4 reshape.51
  588.6 120.9 %all-gather.8.cloned.1.call-done = bf16[1,2048,2048]{2,1,0:T(8,128)(2,1)} async-done(((bf16[1,32,2048]{2,1,0:T(8,128)(2,1)}), bf16[1,2048,2048]{2,1,0:T(8,128)(2,1)}) %all-gather.8.cloned.1.call-update) | async-done | bytes 8388624 | tf_op jit(solution)/shard_map/all_gather | solution.py:42
  709.4 14.3 %multiply_add_fusion = (f32[64,2048]{1,0:T(8,128)S(1)}, f32[64,2048]{1,0:T(8,128)S(1)}) fusion(f32[64,2048]{1,0:T(8,128)S(1)} %copy-done, f32[64,2048]{1,0:T(8,128)S(1)} %copy-done.1, f32[2048,64]{1,0:T(8,128)S(1)} %bitcast.47, bf16[1,2048,2048]{2,1,0:T(8,128)(2,1)} %all-gather.8.cloned.1.call-done, f32[2048]{0:T(1024)S(1)} %convert_element_type.20), kind=kOutput, calls=%fused_computation.22 | convolution fusion | flops 3230531584 | bytes 11018240 | tf_op jit(solution)/shard_map/dot_general | solution.py:46
  723.7 0.0 copy-start.3
  723.8 0.0 copy-start.2
  723.8 16.2 %fusion.2 = f32[2048,64]{1,0:T(8,128)S(1)} fusion(bf16[1,2048,2048]{2,1,0:T(8,128)(2,1)} %all-gather.8.cloned.1.call-done, f32[2048]{0:T(1024)S(1)} %convert_element_type.20, f32[64,2048]{1,0:T(8,128)S(1)} %get-tuple-element.13, f32[64,2048]{1,0:T(8,128)S(1)} %get-tuple-element.12), kind=kOutput, calls=%fused_computation.4 | convolution fusion | flops 3230138368 | bytes 9969664 | tf_op jit(solution)/shard_map/dot_general | solution.py:50
  740.0 0.7 reshape.52
  740.7 21.2 %all_to_all.70 = f32[64,1,2048]{2,1,0:T(1,128)S(1)} all-to-all(f32[64,1,2048]{2,1,0:T(1,128)S(1)} %reshape.52), channel_id=1, replica_groups=mesh['fsdp'=64,'tp'=4] {'fsdp'}, dimensions={0} | all-to-all | bytes 1048576 | tf_op jit(solution)/shard_map/all_to_all | solution.py:51
  761.9 1.9 reduce.1
  763.8 0.4 reshape.53
  764.3 0.6 copy.42
  764.9 0.5 reshape.33
  765.4 35.6 %fusion.10 = f32[32,2,2048]{2,0,1:T(8,128)S(1)} fusion(bf16[2,2048,2048]{2,1,0:T(8,128)(2,1)} %all-gather.6.cloned.1.call-done, f32[2,2048]{1,0:T(2,128)S(1)} %bitcast.56, f32[32,2,2048]{2,1,0:T(2,128)S(1)} %reshape.33), kind=kOutput, calls=%fused_computation.12 | convolution fusion | flops 3238002688 | bytes 17842176 | tf_op jit(solution)/shard_map/cbo,bio->cbi/dot_general | solution.py:54
  801.0 0.4 copy.44
  801.4 0.6 all_to_all.62
  802.1 0.6 copy.54
  802.7 0.7 reshape.54
  803.3 19.4 %all_to_all.71 = f32[64,1,2048]{2,1,0:T(1,128)S(1)} all-to-all(f32[64,1,2048]{2,1,0:T(1,128)S(1)} %reshape.54), channel_id=1, replica_groups=mesh['fsdp'=64,'tp'=4] {'fsdp'}, dimensions={0} | all-to-all | bytes 1048576 | tf_op jit(solution)/shard_map/all_to_all | solution.py:57
  822.7 1.9 reduce.2
  824.6 0.4 reshape.55
  825.0 1.1 copy.46
  (14 shorter events, 0.0 us)
Async XLA Ops:
  7.2 386.2 %all-gather.6.cloned.1.call-start = ((), (), s32[]{:S(2)}) async-start(), calls=%async_computation.4 | async-start | bytes 17039360 | tf_op jit(solution)/shard_map/all_gather | solution.py:31
  15.4 694.0 %all-gather.8.cloned.1.call-start = ((), (), s32[]{:S(2)}) async-start(), calls=%async_computation.5 | async-start | bytes 8519680 | tf_op jit(solution)/shard_map/all_gather | solution.py:42
  18.4 169.2 %all-to-all-start = ((bf16[64,2,1024]{2,1,0:T(2,128)(2,1)}), bf16[64,2,1024]{2,1,0:T(2,128)(2,1)S(1)}, u32[]{:S(2)}, u32[]{:S(2)}) async-start(bf16[64,2,1024]{2,1,0:T(2,128)(2,1)} %reshape.48), calls=%async_computation | async-start | bytes 524288 | tf_op jit(solution)/shard_map/all_to_all | solution.py:26
  393.3 30.7 %copy-start.5 = (u32[256]{0:T(256)S(1)}, u32[256]{0:T(256)}, u32[]{:S(2)}) copy-start(u32[256]{0:T(256)} %constant.22) | copy-start | bytes 3076
  393.3 31.9 %copy-start.4 = (bf16[1,32]{1,0:T(2,128)(2,1)S(1)}, bf16[1,32]{1,0:T(2,128)(2,1)}, u32[]{:S(2)}) copy-start(bf16[1,32]{1,0:T(2,128)(2,1)} %param.11) | copy-start | bytes 196
  393.3 316.1 %copy-start = (f32[64,2048]{1,0:T(8,128)S(1)}, f32[64,2048]{1,0:T(8,128)}, u32[]{:S(2)}) copy-start(f32[64,2048]{1,0:T(8,128)} %param.12) | copy-start | bytes 1572868
  393.3 316.1 %copy-start.1 = (f32[64,2048]{1,0:T(8,128)S(1)}, f32[64,2048]{1,0:T(8,128)}, u32[]{:S(2)}) copy-start(f32[64,2048]{1,0:T(8,128)} %param.13) | copy-start | bytes 1572868
  413.6 172.1 %all-to-all-start.1 = ((f32[64,1,2048]{2,1,0:T(1,128)}), f32[64,1,2048]{2,1,0:T(1,128)S(1)}, u32[]{:S(2)}, u32[]{:S(2)}) async-start(f32[64,1,2048]{2,1,0:T(1,128)} %reshape.50), calls=%async_computation.1 | async-start | bytes 1048576 | tf_op jit(solution)/shard_map/all_to_all | solution.py:39
  723.7 16.3 %copy-start.3 = (f32[64,2048]{1,0:T(8,128)}, f32[64,2048]{1,0:T(8,128)S(1)}, u32[]{:S(2)}) copy-start(f32[64,2048]{1,0:T(8,128)S(1)} %get-tuple-element.13) | copy-start | bytes 1572868
  723.8 40.5 %copy-start.2 = (f32[64,2048]{1,0:T(8,128)}, f32[64,2048]{1,0:T(8,128)S(1)}, u32[]{:S(2)}) copy-start(f32[64,2048]{1,0:T(8,128)S(1)} %get-tuple-element.12) | copy-start | bytes 1572868
Sparse Core Ops, SparseCore 0:
  15.6 377.7 all-gather.5
  395.1 314.2 all-gather.7
where the time goes:
time: 842 us; the launch traced here: 833 us
  blocking collectives  365 us (43%)
  waiting for transfers between devices  326 us (39%)
  matrix products  83.3 us (10%)
  starting transfers between devices  23.4 us (3%)
  between operations  15.4 us (2%)
  local copies, waits for them, and re-layouts  14.3 us (2%)
    all_gather x1, waiting for transfers between devices, body(): lax.all_gather(full_codes, 'fsdp', axis=1, tiled=True)  205 us
    unnamed x1, blocking collectives  160 us
    all_gather x1, blocking collectives, body(): lax.all_gather(left_scale, 'fsdp', axis=1, tiled=True)  156 us
    all_gather x1, waiting for transfers between devices, body(): lax.all_gather(right_codes[0], 'fsdp', axis=0, tiled=True)  121 us
    dot_general x1, matrix products, body(): jnp.einsum('cbo,bio->cbi', back_cols.reshape(col_count, blocks, width), l...  35.6 us
    all_to_all x1, blocking collectives, body(): lax.all_to_all(jnp.tile(back_rows.T, (copies, 1)), 'fsdp', split_axis=0,...  21.2 us
    all_to_all x1, blocking collectives, body(): lax.all_to_all(update_cols, 'fsdp', split_axis=1, concat_axis=0, tiled=True)  19.4 us
    dot_general x1, matrix products, body(): jnp.einsum('cbi,bio->cbo', col_data, left_basis, precision=highest)  17.1 us
  transfers between devices with their start and end apart: 4, of which 2 were waited for; matrix products, arithmetic and copies ran while one was open for 3% of the time, Pallas kernels for 0%

commit v1 on v0

v1 whole, which is shorter than its diff:
```python
import jax
import jax.numpy as jnp
from jax import lax
from jax.sharding import Mesh, PartitionSpec as P

beta_one = 0.9
beta_two = 0.999
corr_one = 1.0 - 0.9**10
corr_two = 1.0 - 0.999**10
epsilon = 1e-08

AXES = ("zh", "zl", "x", "l", "h", "c")
SIZES = (2, 4, 4, 2, 2, 2)
F32, BF16, F16 = jnp.float32, jnp.bfloat16, jnp.float16
WIDTH = 2048
SLICE = 256
PLANE = 512
LANES = 128


def linear(zh, zl, x, l, h, c):
    index = 0
    for size, value in zip(SIZES, (zh, zl, x, l, h, c)):
        index = index * size + value
    return index


def left_perms():
    first, second = [], []
    for z in range(8):
        for x in range(4):
            for l in range(2):
                for t in range(4):
                    src = linear(z // 4, z % 4, x, l, t // 2, t % 2)
                    for perm, b in ((first, l), (second, 1 - l)):
                        perm.append((src, linear(b, t, x, z % 2, z // 2 % 2, z // 4)))
    return first, second


def split(value):
    high = lax.reduce_precision(value, 8, 7)
    return high.astype(BF16), (value - high).astype(BF16)


def exponent(bound):
    return jnp.ceil(jnp.log2(jnp.maximum(bound, 1e-30))) + 1.0


def dot(a, b, dims):
    return lax.dot_general(a, b, ((dims[:1], dims[1:]), ((), ())), preferred_element_type=F32)


def with_lanes(value, lane):
    return jnp.concatenate([value, jnp.broadcast_to(lane, lane.shape[:-1] + (LANES,)).astype(value.dtype)], -1)


def body(grad, left_codes, left_scale, right_codes, right_scale, moment1, moment2):
    zh, zl, l = (lax.axis_index(a) for a in ("zh", "zl", "l"))
    rows = grad.shape[0]
    right = lax.all_gather(with_lanes(right_codes[0], right_scale[0][:, None]), ("zh", "zl"), axis=0, tiled=True)

    pieces = with_lanes(left_codes, left_scale[..., None])
    first, second = left_perms()
    got1 = lax.ppermute(jnp.where(l == 0, pieces[0], pieces[1]), AXES, first)
    got2 = lax.ppermute(jnp.where(l == 0, pieces[1], pieces[0]), AXES, second)

    slices = grad.reshape(rows, 8, 8, 32).transpose(2, 0, 1, 3).reshape(1, 8, rows, SLICE)
    columns = lax.all_to_all(
        jnp.broadcast_to(slices, (4, 8, rows, SLICE)).reshape(32, rows, SLICE), ("zl", "x", "l"), 0, 0, tiled=True
    ).reshape(WIDTH, SLICE)

    chunk = jnp.where(zh == 0, jnp.concatenate([got1, got2]), jnp.concatenate([got2, got1]))
    part = lax.all_to_all(
        jnp.broadcast_to(chunk[None], (16,) + chunk.shape), ("h", "l", "x"), 0, 0, tiled=True
    ).reshape(1, WIDTH // 2, -1)
    left = lax.all_to_all(jnp.concatenate([part, part]), ("c",), 0, 0, tiled=True).reshape(WIDTH, -1)
    left_rows = left[:, PLANE].astype(F32)[:, None]
    left = left[:, :PLANE]

    high, low = split(columns.astype(F32) * left_rows)
    half = dot(left, jnp.concatenate([high, low], 1), (0, 0))
    half = half[:, :SLICE] + half[:, SLICE:]
    right_rows = right[:, WIDTH].astype(F32)[None, :]
    right = right[:, :WIDTH]
    half = half * right_rows
    power = exponent(0.125 * jnp.sum(jnp.abs(half), axis=1, keepdims=True))
    high, low = split(half * jnp.exp2(15.0 - power))
    partial = dot(high, right, (1, 0)) + dot(low, right, (1, 0))
    message = with_lanes(partial.astype(F16), power)
    got = lax.all_to_all(message.reshape(8, rows, -1), ("x", "l"), 0, 0, tiled=True)
    rotated = jnp.sum(got[..., :WIDTH].astype(F32) * jnp.exp2(got[..., WIDTH:WIDTH + 1].astype(F32) - 15.0), axis=0)

    first_new = beta_one * moment1 + (1.0 - beta_one) * rotated
    second_new = beta_two * moment2 + (1.0 - beta_two) * rotated * rotated
    direction = first_new / corr_one / (jnp.sqrt(second_new / corr_two) + epsilon)

    power = exponent(jnp.max(jnp.abs(direction), axis=1, keepdims=True))
    message = with_lanes((direction * jnp.exp2(15.0 - power)).astype(F16), power)
    got = lax.all_to_all(jnp.broadcast_to(message[None], (8,) + message.shape), ("x", "l"), 0, 0, tiled=True)
    got = got.reshape(PLANE, -1)
    power = got[:, WIDTH:WIDTH + 1].astype(F32)
    top = jnp.max(power)
    tops = jnp.where(jnp.arange(4)[:, None] == zl, top, 0.0) * jnp.ones((1, LANES), F32)
    for shift in range(1, 4):
        other = lax.ppermute(jnp.full((8, LANES), top, F32), ("zl",), [(i, (i + shift) % 4) for i in range(4)])
        tops = tops + jnp.where(jnp.arange(4)[:, None] == (zl - shift) % 4, other[:1], 0.0)
    high, low = split(got[:, :WIDTH].astype(F32))
    back = dot(high, right, (1, 1)) + dot(low, right, (1, 1))
    back = back * right_rows * jnp.exp2(power - 15.0 - 1.0 - top)
    high, low = split(back)
    update = dot(left, jnp.concatenate([high, low], 1), (1, 0))
    update = (update[:, :SLICE] + update[:, SLICE:]) * left_rows
    got = lax.all_to_all(update.astype(F16).reshape(32, rows, SLICE), ("zl", "x", "l"), 0, 0, tiled=True)
    scales = jnp.exp2(tops[:, 0] + 1.0)
    update = jnp.sum(got.reshape(4, 8, rows, SLICE).astype(F32) * scales[:, None, None, None], axis=0)
    update = update.reshape(8, rows, 8, 32).transpose(1, 2, 0, 3).reshape(rows, WIDTH)
    return update, first_new, second_new


def solution(mesh):
    fine = Mesh(mesh.devices.reshape(SIZES), AXES)
    fsdp, tp = ("zh", "zl", "x", "l"), ("h", "c")
    return jax.shard_map(
        body,
        mesh=fine,
        in_specs=(P(fsdp, tp), P(None, fsdp, tp), P(None, fsdp), P(tp, fsdp, None), P(tp, fsdp), P(fsdp, tp), P(fsdp, tp)),
        out_specs=(P(fsdp, tp), P(fsdp, tp), P(fsdp, tp)),
        check_vma=False,
    )
```

time: 842 us -> 229 us (0.27)
  blocking collectives: 365 us -> 37.2 us
  waiting for transfers between devices: 326 us -> 84.5 us
  matrix products: 83.3 us -> 7.69 us
  starting transfers between devices: 23.4 us -> 47.6 us
  other arithmetic: 5.69 us -> 16.7 us
    all_gather x2 -> x1, waiting for transfers between devices: 326 us -> 4.48 us  [body(): lax.all_gather(with_lanes(right_codes[0], right_scale[0][:, None]), ('zh'...]
    all_gather x2 -> x0, blocking collectives: 164 us -> none  [the longest x1 156 us: body(): lax.all_gather(left_scale, 'fsdp', axis=1, tiled=True)]
    unnamed x1 -> x0, blocking collectives: 160 us -> none
    dot_general x4 -> x6, matrix products: 83.3 us -> 7.69 us  [dot(): lax.dot_general(a, b, ((dims[:1], dims[1:]), ((), ())), preferred_element...]
    all_to_all x2 -> x4, waiting for transfers between devices: 0.01 us -> 60.3 us  [the longest x1 25.1 us: body(): lax.all_to_all(message.reshape(8, rows, -1), ('x', 'l'), 0, 0, tiled=True)]
    ppermute x0 -> x5, waiting for transfers between devices: none -> 19.7 us  [the longest x3 15.5 us: body(): lax.ppermute(jnp.full((8, LANES), top, F32), ('zl',), [(i, (i + shift) %...]
    ppermute x0 -> x5, starting transfers between devices: none -> 13.5 us  [the longest x1 8.98 us: body(): got1 = lax.ppermute(jnp.where(l == 0, pieces[0], pieces[1]), AXES, first)]
    all_to_all x2 -> x4, starting transfers between devices: 23.3 us -> 34 us  [the longest x1 11 us: body(): lax.all_to_all(jnp.broadcast_to(slices, (4, 8, rows, SLICE)).reshape(32,...]
  transfers between devices with their start and end apart: 4 -> 10, of which waited for: 2 -> 9; matrix products, arithmetic and copies ran while one was open for 3% -> 6% of each run, Pallas kernels for 0% -> 0%
where the time goes in v1:
time: 229 us; the launch traced here: 228 us
  waiting for transfers between devices  84.5 us (37%)
  starting transfers between devices  47.6 us (21%)
  blocking collectives  37.2 us (16%)
  local copies, waits for them, and re-layouts  20.3 us (9%)
  other arithmetic  16.7 us (7%)
  between operations  14.4 us (6%)
  matrix products  7.69 us (3%)
    all_to_all x1, blocking collectives, body(): lax.all_to_all(jnp.broadcast_to(message[None], (8,) + message.shape), ('x...  31.3 us
    all_to_all x1, waiting for transfers between devices, body(): lax.all_to_all(message.reshape(8, rows, -1), ('x', 'l'), 0, 0, tiled=True)  25.1 us
    all_to_all x1, waiting for transfers between devices, body(): lax.all_to_all(jnp.broadcast_to(slices, (4, 8, rows, SLICE)).reshape(32,...  19.3 us
    ppermute x3, waiting for transfers between devices, body(): lax.ppermute(jnp.full((8, LANES), top, F32), ('zl',), [(i, (i + shift) %...  15.5 us
    all_to_all x1, waiting for transfers between devices, body(): lax.all_to_all(jnp.broadcast_to(chunk[None], (16,) + chunk.shape), ('h',...  14.7 us
    unnamed x34, local copies, waits for them, and re-layouts  14 us
    all_to_all x1, starting transfers between devices, body(): lax.all_to_all(jnp.broadcast_to(slices, (4, 8, rows, SLICE)).reshape(32,...  11 us
    all_to_all x1, starting transfers between devices, body(): lax.all_to_all(jnp.broadcast_to(chunk[None], (16,) + chunk.shape), ('h',...  10 us
  transfers between devices with their start and end apart: 10, of which 9 were waited for; matrix products, arithmetic and copies ran while one was open for 6% of the time, Pallas kernels for 0%

profile of v1, /device:TPU:8, one launch (start us, length us, event | category | flops | bytes accessed | tf_op | source)
XLA Modules:
  0.0 228.4 jit_solution(8876219308719921238)
XLA Ops:
  7.2 0.7 broadcast_in_dim.112
  7.9 0.9 select_bitcast_fusion.1
  8.8 9.0 %collective-permute-start = (bf16[32,640]{1,0:T(8,128)(2,1)S(1)}, bf16[32,640]{1,0:T(8,128)(2,1)S(1)}, u32[]{:S(2)}, u32[]{:S(2)}) collective-permute-start(bf16[32,640]{1,0:T(8,128)(2,1)S(1)} %get-tuple-element.24), channel_id=1, source_target_pairs={{0,0},{1,32},{2,64},{3,96},{4,128},{5,160},{6,192},{7,224},{8,8},{... | collective-permute-start | bytes 122888 | tf_op jit(solution)/shard_map/ppermute | solution.py:64
  17.9 1.5 collective-permute-done
  19.4 2.7 %collective-permute-done.1 = bf16[32,640]{1,0:T(8,128)(2,1)S(1)} collective-permute-done((bf16[32,640]{1,0:T(8,128)(2,1)S(1)}, bf16[32,640]{1,0:T(8,128)(2,1)S(1)}, u32[]{:S(2)}, u32[]{:S(2)}) %collective-permute-start.1) | collective-permute-done | bytes 40992 | tf_op jit(solution)/shard_map/ppermute | solution.py:65
  22.2 1.2 broadcast_in_dim.113
  23.4 10.0 %all-to-all-start = ((bf16[16,64,640]{2,1,0:T(8,128)(2,1)}), bf16[16,64,640]{2,1,0:T(8,128)(2,1)S(1)}, u32[]{:S(2)}, u32[]{:S(2)}) async-start(bf16[16,64,640]{2,1,0:T(8,128)(2,1)} %broadcast_in_dim.113), calls=%async_computation | async-start | bytes 2621440 | tf_op jit(solution)/shard_map/all_to_all | solution.py:73
  33.6 0.7 pad_maximum_fusion.3
  34.8 14.7 %all-to-all-done = bf16[16,64,640]{2,1,0:T(8,128)(2,1)S(1)} async-done(((bf16[16,64,640]{2,1,0:T(8,128)(2,1)}), bf16[16,64,640]{2,1,0:T(8,128)(2,1)S(1)}, u32[]{:S(2)}, u32[]{:S(2)}) %all-to-all-start) | async-done | bytes 1310752 | tf_op jit(solution)/shard_map/all_to_all | solution.py:73
  49.8 5.8 %all_to_all.30 = bf16[2,1024,640]{2,1,0:T(8,128)(2,1)S(1)} all-to-all(bf16[2,1024,640]{2,1,0:T(8,128)(2,1)S(1)} %pad_maximum_fusion), channel_id=1, replica_groups=mesh['zh'=2,'zl'=4,'x'=4,'l'=2,'h'=2,'c'=2] {'c'}, dimensions={0} | all-to-all | bytes 5242880 | tf_op jit(solution)/shard_map/all_to_all | solution.py:76
  55.6 1.1 broadcast_in_dim.115
  56.7 11.0 %all-to-all-start.2 = ((bf16[32,64,256]{2,1,0:T(8,128)(2,1)}), bf16[32,64,256]{2,1,0:T(8,128)(2,1)}, u32[]{:S(2)}, u32[]{:S(2)}) async-start(bf16[32,64,256]{2,1,0:T(8,128)(2,1)} %bitcast.46), calls=%async_computation.2 | async-start | bytes 2097152 | tf_op jit(solution)/shard_map/all_to_all | solution.py:68
  67.7 1.0 slice_convert_fusion
  68.8 1.6 copy.58
  70.3 4.5 %all-gather.2.cloned.1.call-done = bf16[256,2176]{1,0:T(8,128)(2,1)} async-done(((bf16[32,2176]{1,0:T(8,128)(2,1)}), bf16[256,2176]{1,0:T(8,128)(2,1)}) %all-gather.2.cloned.1.call-update) | async-done | bytes 1114128 | tf_op jit(solution)/shard_map/all_gather | solution.py:60
  74.8 0.9 convert_reduce_fusion
  75.7 19.3 %all-to-all-done.2 = bf16[32,64,256]{2,1,0:T(8,128)(2,1)} async-done(((bf16[32,64,256]{2,1,0:T(8,128)(2,1)}), bf16[32,64,256]{2,1,0:T(8,128)(2,1)}, u32[]{:S(2)}, u32[]{:S(2)}) %all-to-all-start.2) | async-done | bytes 1048608 | tf_op jit(solution)/shard_map/all_to_all | solution.py:68
  95.1 1.6 reduce-precision_convert_fusion.1
  96.7 1.3 fusion.7
  98.2 1.1 copy-done.4
  99.3 0.7 fusion.24
  100.0 0.8 add_convert_fusion
  100.9 1.9 pad_maximum_fusion.1
  102.9 4.9 %all-to-all-start.3 = ((f16[8,64,2176]{2,1,0:T(8,128)(2,1)}), f16[8,64,2176]{2,1,0:T(8,128)(2,1)}, u32[]{:S(2)}, u32[]{:S(2)}) async-start(f16[8,64,2176]{2,1,0:T(8,128)(2,1)} %bitcast.44), calls=%async_computation.3 | async-start | bytes 4456448 | tf_op jit(solution)/shard_map/all_to_all | solution.py:90
  107.8 1.3 copy.39
  109.1 2.3 %copy.46 = f32[64,2048]{0,1:T(8,128)} copy(f32[64,2048]{1,0:T(8,128)} %param.13) | data formatting | bytes 1048576 | tf_op args[6]
  111.5 25.1 %all-to-all-done.3 = f16[8,64,2176]{2,1,0:T(8,128)(2,1)} async-done(((f16[8,64,2176]{2,1,0:T(8,128)(2,1)}), f16[8,64,2176]{2,1,0:T(8,128)(2,1)}, u32[]{:S(2)}, u32[]{:S(2)}) %all-to-all-start.3) | async-done | bytes 2228256 | tf_op jit(solution)/shard_map/all_to_all | solution.py:90
  136.6 0.9 slice.83
  137.7 2.1 multiply_reduce_fusion
  139.8 1.3 copy.54
  141.1 2.6 %abs_reduce_fusion = (f32[64]{0:T(128)S(1)}, f32[64,2048]{0,1:T(8,128)S(1)}, f32[64,2048]{0,1:T(8,128)S(1)}) fusion(f32[64,2048]{0,1:T(8,128)} %copy.54, f32[64,2048]{0,1:T(8,128)} %copy.39, f32[64,2048]{0,1:T(8,128)} %copy.46), kind=kLoop, calls=%fused_computation.33 | loop fusion | flops 1703872 | bytes 2621696 | tf_op jit(solution)/shard_map/reduce_max | solution.py:97
  143.8 0.9 copy-done
  146.2 31.3 %all_to_all.31 = f16[8,64,2176]{2,1,0:T(8,128)(2,1)S(1)} all-to-all(f16[8,64,2176]{2,1,0:T(8,128)(2,1)S(1)} %broadcast_in_dim.120), channel_id=1, replica_groups=mesh['zh'=2,'zl'=4,'x'=4,'l'=2,'h'=2,'c'=2] {'x','l'}, dimensions={0} | all-to-all | bytes 4456448 | tf_op jit(solution)/shard_map/all_to_all | solution.py:99
  177.5 1.4 copy-done.6
  179.7 0.7 multiply_exponential_fusion
  180.3 2.8 %fusion.2 = f32[512,256]{0,1:T(8,128)S(1)} fusion(f16[512,2176]{1,0:T(8,128)(2,1)} %bitcast.51, bf16[256,2176]{1,0:T(8,128)(2,1)} %all-gather.2.cloned.1.call-done), kind=kOutput, calls=%fused_computation.10 | convolution fusion | flops 541065216 | bytes 3670016 | tf_op jit(solution)/shard_map/dot_general | solution.py:50
  183.2 0.8 reduce-precision_convert_fusion.9
  184.0 1.3 fusion.14
  185.4 1.3 fusion.6
  186.7 8.1 %all-to-all-start.5 = ((f16[32,64,256]{2,1,0:T(8,128)(2,1)}), f16[32,64,256]{2,1,0:T(8,128)(2,1)S(1)}, u32[]{:S(2)}, u32[]{:S(2)}) async-start(f16[32,64,256]{2,1,0:T(8,128)(2,1)} %bitcast.16), calls=%async_computation.5 | async-start | bytes 2097152 | tf_op jit(solution)/shard_map/all_to_all | solution.py:113
  194.9 1.1 copy.52
  196.0 1.1 copy.53
  197.7 3.4 %collective-permute-start.4 = (f32[8,128]{1,0:T(8,128)S(1)}, f32[8,128]{1,0:T(8,128)S(1)}, u32[]{:S(2)}, u32[]{:S(2)}) collective-permute-start(f32[8,128]{1,0:T(8,128)S(1)} %broadcast_in_dim.124), channel_id=1, source_target_pairs={{0,96},{32,0},{64,32},{96,64},{1,97},{33,1},{65,33},{97,65},{2,98}... | collective-permute-start | bytes 12296 | tf_op jit(solution)/shard_map/ppermute | solution.py:105
  201.1 1.1 collective-permute-start.2
  202.9 6.9 %collective-permute-done.4 = f32[8,128]{1,0:T(8,128)S(1)} collective-permute-done((f32[8,128]{1,0:T(8,128)S(1)}, f32[8,128]{1,0:T(8,128)S(1)}, u32[]{:S(2)}, u32[]{:S(2)}) %collective-permute-start.4) | collective-permute-done | bytes 4128 | tf_op jit(solution)/shard_map/ppermute | solution.py:105
  209.8 8.6 %collective-permute-done.3 = f32[8,128]{1,0:T(8,128)S(1)} collective-permute-done((f32[8,128]{1,0:T(8,128)S(1)}, f32[8,128]{1,0:T(8,128)S(1)}, u32[]{:S(2)}, u32[]{:S(2)}) %collective-permute-start.3) | collective-permute-done | bytes 4128 | tf_op jit(solution)/shard_map/ppermute | solution.py:105
  218.4 1.2 all-to-all-done.5
  220.4 1.1 copy.51
  (57 shorter events, 6.0 us)
Async XLA Ops:
  8.8 24.7 %copy-start.11 = (bf16[1,32]{1,0:T(2,128)(2,1)S(1)}, bf16[1,32]{1,0:T(2,128)(2,1)}, u32[]{:S(2)}) copy-start(bf16[1,32]{1,0:T(2,128)(2,1)} %param.11) | copy-start | bytes 196
  8.8 10.6 %collective-permute-start = (bf16[32,640]{1,0:T(8,128)(2,1)S(1)}, bf16[32,640]{1,0:T(8,128)(2,1)S(1)}, u32[]{:S(2)}, u32[]{:S(2)}) collective-permute-start(bf16[32,640]{1,0:T(8,128)(2,1)S(1)} %get-tuple-element.24), channel_id=1, source_target_pairs={{0,0},{1,32},{2,64},{3,96},{4,128},{5,160},{6,192},{7,224},{8,8},{... | collective-permute-start | bytes 122888 | tf_op jit(solution)/shard_map/ppermute | solution.py:64
  17.8 4.4 %collective-permute-start.1 = (bf16[32,640]{1,0:T(8,128)(2,1)S(1)}, bf16[32,640]{1,0:T(8,128)(2,1)S(1)}, u32[]{:S(2)}, u32[]{:S(2)}) collective-permute-start(bf16[32,640]{1,0:T(8,128)(2,1)S(1)} %get-tuple-element.25), channel_id=1, source_target_pairs={{0,128},{1,160},{2,192},{3,224},{4,0},{5,32},{6,64},{7,96},{8,136}... | collective-permute-start | bytes 122888 | tf_op jit(solution)/shard_map/ppermute | solution.py:65
  17.9 15.7 %copy-start.10 = (bf16[1,32,2048]{2,1,0:T(8,128)(2,1)S(1)}, bf16[1,32,2048]{2,1,0:T(8,128)(2,1)}, u32[]{:S(2)}) copy-start(bf16[1,32,2048]{2,1,0:T(8,128)(2,1)} %param.10) | copy-start | bytes 393220
  22.1 12.1 %copy-start.9 = (bf16[64,2048]{1,0:T(8,128)(2,1)S(1)}, bf16[64,2048]{1,0:T(8,128)(2,1)}, u32[]{:S(2)}) copy-start(bf16[64,2048]{1,0:T(8,128)(2,1)} %param.7) | copy-start | bytes 786436
  23.4 26.1 %all-to-all-start = ((bf16[16,64,640]{2,1,0:T(8,128)(2,1)}), bf16[16,64,640]{2,1,0:T(8,128)(2,1)S(1)}, u32[]{:S(2)}, u32[]{:S(2)}) async-start(bf16[16,64,640]{2,1,0:T(8,128)(2,1)} %broadcast_in_dim.113), calls=%async_computation | async-start | bytes 2621440 | tf_op jit(solution)/shard_map/all_to_all | solution.py:73
  33.4 41.4 %all-gather.2.cloned.1.call-start = ((), (), s32[]{:S(2)}) async-start(), calls=%async_computation.6 | async-start | bytes 1253376 | tf_op jit(solution)/shard_map/all_gather | solution.py:60
  56.7 38.3 %all-to-all-start.2 = ((bf16[32,64,256]{2,1,0:T(8,128)(2,1)}), bf16[32,64,256]{2,1,0:T(8,128)(2,1)}, u32[]{:S(2)}, u32[]{:S(2)}) async-start(bf16[32,64,256]{2,1,0:T(8,128)(2,1)} %bitcast.46), calls=%async_computation.2 | async-start | bytes 2097152 | tf_op jit(solution)/shard_map/all_to_all | solution.py:68
  98.0 1.2 copy-start.4
  102.9 4.9 %copy-start.8 = (f32[64,2048]{1,0:T(8,128)S(1)}, f32[64,2048]{1,0:T(8,128)}, u32[]{:S(2)}) copy-start(f32[64,2048]{1,0:T(8,128)} %param.12) | copy-start | bytes 1572868
  102.9 33.7 %all-to-all-start.3 = ((f16[8,64,2176]{2,1,0:T(8,128)(2,1)}), f16[8,64,2176]{2,1,0:T(8,128)(2,1)}, u32[]{:S(2)}, u32[]{:S(2)}) async-start(f16[8,64,2176]{2,1,0:T(8,128)(2,1)} %bitcast.44), calls=%async_computation.3 | async-start | bytes 4456448 | tf_op jit(solution)/shard_map/all_to_all | solution.py:90
  143.8 1.0 copy-start
  143.8 1.5 copy-start.2
  177.5 1.4 copy-start.6
  180.3 2.8 %copy-start.5 = (bf16[256,2176]{1,0:T(8,128)(2,1)S(1)}, bf16[256,2176]{1,0:T(8,128)(2,1)}, u32[]{:S(2)}) copy-start(bf16[256,2176]{1,0:T(8,128)(2,1)} %all-gather.2.cloned.1.call-done) | copy-start | bytes 3342340
  180.3 2.9 %copy-start.7 = (f16[8,64,2176]{2,1,0:T(8,128)(2,1)S(1)}, f16[8,64,2176]{2,1,0:T(8,128)(2,1)}, u32[]{:S(2)}) copy-start(f16[8,64,2176]{2,1,0:T(8,128)(2,1)} %copy-done.6) | copy-start | bytes 6684676
  186.7 8.2 %copy-start.3 = (f32[64,2048]{0,1:T(8,128)S(1)}, f32[64,2048]{0,1:T(8,128)}, u32[]{:S(2)}) copy-start(f32[64,2048]{0,1:T(8,128)} %copy-done.2) | copy-start | bytes 1572868
  186.7 9.3 %copy-start.1 = (f32[64,2048]{0,1:T(8,128)S(1)}, f32[64,2048]{0,1:T(8,128)}, u32[]{:S(2)}) copy-start(f32[64,2048]{0,1:T(8,128)} %copy-done) | copy-start | bytes 1572868
  186.7 32.9 %all-to-all-start.5 = ((f16[32,64,256]{2,1,0:T(8,128)(2,1)}), f16[32,64,256]{2,1,0:T(8,128)(2,1)S(1)}, u32[]{:S(2)}, u32[]{:S(2)}) async-start(f16[32,64,256]{2,1,0:T(8,128)(2,1)} %bitcast.16), calls=%async_computation.5 | async-start | bytes 2097152 | tf_op jit(solution)/shard_map/all_to_all | solution.py:113
  197.7 12.0 %collective-permute-start.4 = (f32[8,128]{1,0:T(8,128)S(1)}, f32[8,128]{1,0:T(8,128)S(1)}, u32[]{:S(2)}, u32[]{:S(2)}) collective-permute-start(f32[8,128]{1,0:T(8,128)S(1)} %broadcast_in_dim.124), channel_id=1, source_target_pairs={{0,96},{32,0},{64,32},{96,64},{1,97},{33,1},{65,33},{97,65},{2,98}... | collective-permute-start | bytes 12296 | tf_op jit(solution)/shard_map/ppermute | solution.py:105
  201.1 17.2 %collective-permute-start.3 = (f32[8,128]{1,0:T(8,128)S(1)}, f32[8,128]{1,0:T(8,128)S(1)}, u32[]{:S(2)}, u32[]{:S(2)}) collective-permute-start(f32[8,128]{1,0:T(8,128)S(1)} %broadcast_in_dim.124), channel_id=1, source_target_pairs={{0,64},{32,96},{64,0},{96,32},{1,65},{33,97},{65,1},{97,33},{2,66}... | collective-permute-start | bytes 12296 | tf_op jit(solution)/shard_map/ppermute | solution.py:105
  201.1 17.2 %collective-permute-start.2 = (f32[8,128]{1,0:T(8,128)S(1)}, f32[8,128]{1,0:T(8,128)S(1)}, u32[]{:S(2)}, u32[]{:S(2)}) collective-permute-start(f32[8,128]{1,0:T(8,128)S(1)} %broadcast_in_dim.124), channel_id=1, source_target_pairs={{0,32},{32,64},{64,96},{96,0},{1,33},{33,65},{65,97},{97,1},{2,34}... | collective-permute-start | bytes 12296 | tf_op jit(solution)/shard_map/ppermute | solution.py:105
Sparse Core Ops, SparseCore 0:
  36.6 38.1 all-gather.1

commit v2 on v1

v2 whole, which is shorter than its diff:
```python
import jax
import jax.numpy as jnp
from jax import lax
from jax.experimental import pallas as pl
from jax.experimental.pallas import tpu as pltpu
from jax.sharding import Mesh, PartitionSpec as P

beta_one = 0.9
beta_two = 0.999
corr_one = 1.0 - 0.9**10
corr_two = 1.0 - 0.999**10
epsilon = 1e-08

AXES = ("zh", "zl", "x", "l", "h", "c")
SIZES = (2, 4, 4, 2, 2, 2)
F32, BF16, F16 = jnp.float32, jnp.bfloat16, jnp.float16
WIDTH = 2048
SLICE = 256
PLANE = 512
ROWS = 64
LANES = 128
SWAP = [(0, 1), (1, 0)]


def linear(zh, zl, x, l, h, c):
    index = 0
    for size, value in zip(SIZES, (zh, zl, x, l, h, c)):
        index = index * size + value
    return index


def left_perms():
    first, second = [], []
    for z in range(8):
        for x in range(4):
            for l in range(2):
                for t in range(4):
                    src = linear(z // 4, z % 4, x, l, t // 2, t % 2)
                    for perm, b in ((first, l), (second, 1 - l)):
                        perm.append((src, linear(b, t, x, z % 2, z // 2 % 2, z // 4)))
    return first, second


def split(value):
    high = value.astype(BF16)
    return high, (value - high.astype(F32)).astype(BF16)


def exponent(bound):
    return jnp.ceil(jnp.log2(jnp.maximum(bound, 1e-30))) + 1.0


def dot(a, b, dims):
    return lax.dot_general(a, b, ((dims[:1], dims[1:]), ((), ())), preferred_element_type=F32)


def with_lanes(value, lane):
    return jnp.concatenate([value, jnp.broadcast_to(lane, lane.shape[:-1] + (LANES,)).astype(value.dtype)], -1)


def call(kernel, out, scratch=(), smem=0, operands=()):
    specs = [pl.BlockSpec(memory_space=pltpu.SMEM)] * smem
    specs += [pl.BlockSpec(memory_space=pltpu.VMEM)] * (len(operands) - smem)
    return pl.pallas_call(
        kernel,
        out_shape=tuple(jax.ShapeDtypeStruct(shape, F32) for shape in out),
        in_specs=specs,
        out_specs=tuple(pl.BlockSpec(memory_space=pltpu.VMEM) for _ in out),
        scratch_shapes=list(scratch),
        compiler_params=pltpu.CompilerParams(vmem_limit_bytes=28 * 1024 * 1024),
    )(*operands)


def block_starts(place):
    c, y, x = place[0], place[1], place[2]
    for part in range(2):
        core = c if part == 0 else 1 - c
        for s in range(4):
            for t in range(4):
                block = core * 16 + lax.rem(y - s + 4, 4) * 4 + lax.rem(x - t + 4, 4)
                yield part, (s * 4 + t) * ROWS, pl.multiple_of(block * ROWS, ROWS)


def left_kernel(place, own, other, columns, mine, theirs, scaled, total):
    tiles = (own, other)
    for part, row, start in block_starts(place):
        scale = tiles[part][row:row + ROWS, PLANE:].astype(F32)
        here = part * 1024 + row
        for lane in range(0, SLICE, LANES):
            value = columns[pl.ds(start, ROWS), lane:lane + LANES].astype(F32) * scale
            high, low = split(value)
            scaled[here:here + ROWS, lane:lane + LANES] = high
            scaled[here:here + ROWS, SLICE + lane:SLICE + lane + LANES] = low
    half = dot(own[:, :PLANE], scaled[:1024], (0, 0)) + dot(other[:, :PLANE], scaled[1024:], (0, 0))
    total[...] = half[:, :SLICE] + half[:, SLICE:]
    l = lax.rem(place[1], 2)
    for x in range(4):
        mine[x * ROWS:(x + 1) * ROWS, :] = total[pl.ds(pl.multiple_of((2 * x + l) * ROWS, ROWS), ROWS), :]
        theirs[x * ROWS:(x + 1) * ROWS, :] = total[pl.ds(pl.multiple_of((2 * x + 1 - l) * ROWS, ROWS), ROWS), :]


def right_kernel(mine, theirs, scales, right, message):
    own_half = mine[...] * scales[0:1, :]
    other_half = theirs[...] * scales[1:2, :]
    bound = jnp.sum(jnp.abs(own_half) + jnp.abs(other_half), axis=1, keepdims=True)
    power = exponent(0.125 * bound)
    factor = jnp.exp2(15.0 - power)
    high, low = split(own_half * factor)
    high2, low2 = split(other_half * factor)
    for lane in range(0, WIDTH, 512):
        near, far = right[0, :, lane:lane + 512], right[1, :, lane:lane + 512]
        message[:, lane:lane + 512] = (
            dot(high, near, (1, 0)) + dot(low, near, (1, 0)) + dot(high2, far, (1, 0)) + dot(low2, far, (1, 0))
        )
    message[:, WIDTH:] = jnp.broadcast_to(power, (4 * ROWS, LANES))


def moment_kernel(got, moment1, moment2, first_new, second_new, message):
    rotated = jnp.zeros((ROWS, WIDTH), F32)
    for source in range(4):
        rotated += got[source, :, :WIDTH] * jnp.exp2(got[source, :, WIDTH:WIDTH + 1] - 15.0)
    first = beta_one * moment1[...] + (1.0 - beta_one) * rotated
    second = beta_two * moment2[...] + (1.0 - beta_two) * rotated * rotated
    first_new[...] = first
    second_new[...] = second
    direction = first / corr_one / (jnp.sqrt(second / corr_two) + epsilon)
    power = exponent(jnp.max(jnp.abs(direction), axis=1, keepdims=True))
    message[:, :WIDTH] = direction * jnp.exp2(15.0 - power)
    message[:, WIDTH:] = jnp.broadcast_to(power, (ROWS, LANES))


def back_kernel(got, scales, right, mine, theirs):
    power = got[:, WIDTH:WIDTH + 1]
    high, low = split(got[:, :WIDTH])
    factor = jnp.exp2(power - 15.0)
    near, far = right[0, :, :WIDTH], right[1, :, :WIDTH]
    mine[...] = (dot(high, near, (1, 1)) + dot(low, near, (1, 1))) * factor * scales[0:1, :]
    theirs[:4 * ROWS, :] = (dot(high, far, (1, 1)) + dot(low, far, (1, 1))) * factor * scales[1:2, :]
    theirs[4 * ROWS:, :] = jnp.broadcast_to(jnp.max(power, axis=0, keepdims=True), (8, SLICE))


def update_kernel(place, factor, own, other, mine, theirs, update, parts):
    l = lax.rem(place[1], 2)
    for x in range(4):
        for values, side in ((mine, l), (theirs, 1 - l)):
            high, low = split(values[x * ROWS:(x + 1) * ROWS, :] * factor[0])
            rows = pl.ds(pl.multiple_of((2 * x + side) * ROWS, ROWS), ROWS)
            parts[rows, :SLICE] = high
            parts[rows, SLICE:] = low
    tiles = (own, other)
    values = [dot(tile[:, :PLANE], parts[...], (1, 0)) for tile in tiles]
    values = [value[:, :SLICE] + value[:, SLICE:] for value in values]
    for part, row, start in block_starts(place):
        scale = tiles[part][row:row + ROWS, PLANE:].astype(F32)
        for lane in range(0, SLICE, LANES):
            update[pl.ds(start, ROWS), lane:lane + LANES] = values[part][row:row + ROWS, lane:lane + LANES] * scale


def ring_gather(value, axes, names):
    size = len(names)
    blocks = [value]
    for shift in range(1, size):
        blocks.append(lax.ppermute(value, axes, [(names[i], names[(i + shift) % size]) for i in range(size)]))
    return jnp.concatenate(blocks)


def body(grad, left_codes, left_scale, right_codes, right_scale, moment1, moment2):
    zh, zl, x, l, h, c = (lax.axis_index(a) for a in AXES)
    place = jnp.stack([c, 2 * h + l, x]).astype(jnp.int32)
    right = with_lanes(right_codes, right_scale[..., None])
    right = jnp.concatenate([right, lax.ppermute(right, "l", SWAP)])

    pieces = with_lanes(left_codes, left_scale[..., None])
    first, second = left_perms()
    got1 = lax.ppermute(jnp.where(l == 0, pieces[0], pieces[1]), AXES, first)
    got2 = lax.ppermute(jnp.where(l == 0, pieces[1], pieces[0]), AXES, second)

    right, got1, got2 = lax.optimization_barrier((right, got1, got2))
    right = lax.all_gather(right, ("zh", "zl"), axis=1, tiled=True)
    slices = grad.reshape(ROWS, 8, 8, 32).transpose(2, 0, 1, 3).reshape(1, 8, ROWS, SLICE)
    columns = jnp.broadcast_to(slices, (4, 8, ROWS, SLICE)).reshape(32, ROWS, SLICE)
    columns = lax.all_to_all(columns, ("zl", "x", "l"), 0, 0, tiled=True).reshape(WIDTH, SLICE)

    chunk = jnp.where(zh == 0, jnp.concatenate([got1, got2]), jnp.concatenate([got2, got1]))
    left_own = ring_gather(ring_gather(chunk, ("x",), (0, 1, 2, 3)), ("l", "h"), (0, 2, 1, 3))
    left_other = lax.ppermute(left_own, "c", SWAP)

    mine, theirs = call(
        left_kernel,
        [(4 * ROWS, SLICE)] * 2,
        [pltpu.VMEM((WIDTH, 2 * SLICE), BF16), pltpu.VMEM((PLANE, SLICE), F32)],
        1,
        (place, left_own, left_other, columns),
    )
    theirs = lax.ppermute(theirs, "l", SWAP)
    scales = right[:, :, WIDTH].astype(F32)
    (message,) = call(
        right_kernel, [(4 * ROWS, WIDTH + LANES)], operands=(mine, theirs, scales, right)
    )
    got = lax.all_to_all(message.astype(F16).reshape(4, ROWS, -1), "x", 0, 0, tiled=True)
    first_new, second_new, message = call(
        moment_kernel,
        [(ROWS, WIDTH)] * 2 + [(ROWS, WIDTH + LANES)],
        operands=(got.astype(F32), moment1, moment2),
    )
    message = message.astype(F16)
    got = lax.all_to_all(jnp.broadcast_to(message, (4,) + message.shape), "x", 0, 0, tiled=True)
    mine, theirs = call(
        back_kernel,
        [(4 * ROWS, SLICE), (4 * ROWS + 8, SLICE)],
        operands=(got.astype(F32).reshape(4 * ROWS, -1), scales, right),
    )
    top = theirs[-1, 0]
    theirs = lax.ppermute(theirs, "l", SWAP)
    top = jnp.maximum(top, theirs[-1, 0])
    lane = jnp.full((8, LANES), top)
    tops = jnp.where(jnp.arange(4) == zl, top, 0.0)
    for shift in range(1, 4):
        other = lax.ppermute(lane, "zl", [(i, (i + shift) % 4) for i in range(4)])
        tops = tops + jnp.where(jnp.arange(4) == (zl - shift) % 4, other[0, 0], 0.0)
    (update,) = call(
        update_kernel,
        [(WIDTH, SLICE)],
        [pltpu.VMEM((PLANE, 2 * SLICE), BF16)],
        2,
        (place, jnp.exp2(-1.0 - top).reshape(1), left_own, left_other, mine, theirs),
    )
    got = lax.all_to_all(update.astype(F16).reshape(32, ROWS, SLICE), ("zl", "x", "l"), 0, 0, tiled=True)
    factors = jnp.exp2(tops + 1.0)[:, None, None, None]
    update = jnp.sum(got.reshape(4, 8, ROWS, SLICE).astype(F32) * factors, axis=0)
    update = update.reshape(8, ROWS, 8, 32).transpose(1, 2, 0, 3).reshape(ROWS, WIDTH)
    return update, first_new, second_new


def solution(mesh):
    fine = Mesh(mesh.devices.reshape(SIZES), AXES)
    fsdp, tp = ("zh", "zl", "x", "l"), ("h", "c")
    return jax.shard_map(
        body,
        mesh=fine,
        in_specs=(P(fsdp, tp), P(None, fsdp, tp), P(None, fsdp), P(tp, fsdp, None), P(tp, fsdp), P(fsdp, tp), P(fsdp, tp)),
        out_specs=(P(fsdp, tp), P(fsdp, tp), P(fsdp, tp)),
        check_vma=False,
    )
```

time: 229 us -> 184 us (0.80)
  waiting for transfers between devices: 84.5 us -> 61.5 us
  Pallas kernels: 0 us -> 8.87 us
  local copies, waits for them, and re-layouts: 20.3 us -> 11.7 us
  other arithmetic: 16.7 us -> 8.5 us
  matrix products: 7.69 us -> 0 us
  starting transfers between devices: 47.6 us -> 42.3 us
    all_to_all x4 -> x2, waiting for transfers between devices: 60.3 us -> 9.58 us  [the longest x1 9.58 us: body(): lax.all_to_all(columns, ('zl', 'x', 'l'), 0, 0, tiled=True)]
    ppermute x3 -> x13, waiting for transfers between devices: 15.5 us -> 46 us  [the longest x6 19.5 us: ring_gather(): lax.ppermute(value, axes, [(names[i], names[(i + shift) % size]) for i in...]
    all_to_all x4 -> x2, starting transfers between devices: 34 us -> 14 us  [the longest x1 7.95 us: body(): lax.all_to_all(columns, ('zl', 'x', 'l'), 0, 0, tiled=True)]
    ppermute x3 -> x13, starting transfers between devices: 4.47 us -> 19.8 us  [the longest x6 10.6 us: ring_gather(): lax.ppermute(value, axes, [(names[i], names[(i + shift) % size]) for i in...]
    pallas_call x0 -> x5, Pallas kernels: none -> 8.87 us  [call(): pl.pallas_call(kernel, out_shape=tuple((jax.ShapeDtypeStruct(shape, F32)...]
    unnamed x34 -> x17, local copies, waits for them, and re-layouts: 14 us -> 5.59 us
    dot_general x6 -> x0, matrix products: 7.69 us -> none  [dot(): lax.dot_general(a, b, ((dims[:1], dims[1:]), ((), ())), preferred_element...]
    reduce_max x2 -> x0, other arithmetic: 3.26 us -> none  [the longest x1 2.64 us: body(): power = exponent(jnp.max(jnp.abs(direction), axis=1, keepdims=True))]
  transfers between devices with their start and end apart: 10 -> 18, of which waited for: 9 -> 10; matrix products, arithmetic and copies ran while one was open for 6% -> 6% of each run, Pallas kernels for 0% -> 2%
where the time goes in v2:
time: 184 us
  waiting for transfers between devices  61.5 us (33%)
  starting transfers between devices  42.3 us (23%)
  blocking collectives  35.2 us (19%)
  between operations  15.6 us (8%)
  local copies, waits for them, and re-layouts  11.7 us (6%)
  Pallas kernels  8.87 us (5%)
  other arithmetic  8.5 us (5%)
    ppermute x6, waiting for transfers between devices, ring_gather(): lax.ppermute(value, axes, [(names[i], names[(i + shift) % size]) for i in...  19.5 us
    all_to_all x1, blocking collectives, body(): lax.all_to_all(message.astype(F16).reshape(4, ROWS, -1), 'x', 0, 0, tiled...  18.9 us
    all_to_all x1, blocking collectives, body(): lax.all_to_all(jnp.broadcast_to(message, (4,) + message.shape), 'x', 0, 0...  16.3 us
    ppermute x3, waiting for transfers between devices, body(): other = lax.ppermute(lane, 'zl', [(i, (i + shift) % 4) for i in range(4)])  15.3 us
    ppermute x6, starting transfers between devices, ring_gather(): lax.ppermute(value, axes, [(names[i], names[(i + shift) % size]) for i in...  10.6 us
    all_to_all x1, waiting for transfers between devices, body(): lax.all_to_all(columns, ('zl', 'x', 'l'), 0, 0, tiled=True)  9.58 us
    pallas_call x5, Pallas kernels, call(): pl.pallas_call(kernel, out_shape=tuple((jax.ShapeDtypeStruct(shape, F32)...  8.87 us
    ppermute x1, starting transfers between devices, body(): got1 = lax.ppermute(jnp.where(l == 0, pieces[0], pieces[1]), AXES, first)  8.38 us
  transfers between devices with their start and end apart: 18, of which 10 were waited for; matrix products, arithmetic and copies ran while one was open for 6% of the time, Pallas kernels for 2%

profile of v2, /device:TPU:8, one launch (start us, length us, event | category | flops | bytes accessed | tf_op | source)
XLA Modules:
  0.0 183.5 jit_solution(2779263651001682449)
XLA Ops:
  7.2 0.8 broadcast_in_dim.49
  8.0 0.9 pad_maximum_fusion.2
  8.9 2.3 %collective-permute-start = (bf16[1,32,2176]{2,1,0:T(8,128)(2,1)S(1)}, bf16[1,32,2176]{2,1,0:T(8,128)(2,1)S(1)}, u32[]{:S(2)}, u32[]{:S(2)}) collective-permute-start(bf16[1,32,2176]{2,1,0:T(8,128)(2,1)S(1)} %pad_maximum_fusion.2), channel_id=1, source_target_pairs={{0,4},{4,0},{1,5},{5,1},{2,6},{6,2},{3,7},{7,3},{8,12},{12,8},{9,1... | collective-permute-start | bytes 417800 | tf_op jit(solution)/shard_map/ppermute | solution.py:171
  11.2 0.7 broadcast_in_dim.50
  11.9 0.9 select_bitcast_fusion
  12.8 8.4 %collective-permute-start.1 = (bf16[32,640]{1,0:T(8,128)(2,1)S(1)}, bf16[32,640]{1,0:T(8,128)(2,1)S(1)}, u32[]{:S(2)}, u32[]{:S(2)}) collective-permute-start(bf16[32,640]{1,0:T(8,128)(2,1)S(1)} %get-tuple-element.32), channel_id=1, source_target_pairs={{0,0},{1,32},{2,64},{3,96},{4,128},{5,160},{6,192},{7,224},{8,8},{... | collective-permute-start | bytes 122888 | tf_op jit(solution)/shard_map/ppermute | solution.py:175
  21.2 1.6 pad_maximum_fusion.1
  22.9 2.5 %collective-permute-done.2 = bf16[32,640]{1,0:T(8,128)(2,1)S(1)} collective-permute-done((bf16[32,640]{1,0:T(8,128)(2,1)S(1)}, bf16[32,640]{1,0:T(8,128)(2,1)S(1)}, u32[]{:S(2)}, u32[]{:S(2)}) %collective-permute-start.2) | collective-permute-done | bytes 40992 | tf_op jit(solution)/shard_map/ppermute | solution.py:176
  25.4 1.6 collective-permute-start.3
  27.0 2.7 %collective-permute-start.4 = (bf16[64,640]{1,0:T(8,128)(2,1)S(1)}, bf16[64,640]{1,0:T(8,128)(2,1)S(1)}, u32[]{:S(2)}, u32[]{:S(2)}) collective-permute-start(bf16[64,640]{1,0:T(8,128)(2,1)S(1)} %get-tuple-element.30), channel_id=1, source_target_pairs={{0,16},{8,24},{16,0},{24,8},{1,17},{9,25},{17,1},{25,9},{2,18},{10... | collective-permute-start | bytes 245768 | tf_op jit(solution)/shard_map/ppermute | solution.py:163
  29.7 1.4 collective-permute-start.5
  31.7 1.1 broadcast_in_dim.52
  32.8 7.9 %all-to-all-start = ((bf16[32,64,256]{2,1,0:T(8,128)(2,1)}), bf16[32,64,256]{2,1,0:T(8,128)(2,1)}, u32[]{:S(2)}, u32[]{:S(2)}) async-start(bf16[32,64,256]{2,1,0:T(8,128)(2,1)} %bitcast.9), calls=%async_computation | async-start | bytes 2097152 | tf_op jit(solution)/shard_map/all_to_all | solution.py:182
  41.0 2.2 %collective-permute-start.7 = (bf16[256,640]{1,0:T(8,128)(2,1)S(1)}, bf16[256,640]{1,0:T(8,128)(2,1)S(1)}, u32[]{:S(2)}, u32[]{:S(2)}) collective-permute-start(bf16[256,640]{1,0:T(8,128)(2,1)S(1)} %pad_maximum_fusion), channel_id=1, source_target_pairs={{0,2},{4,6},{2,0},{6,4},{1,3},{5,7},{3,1},{7,5},{8,10},{12,14},{10... | collective-permute-start | bytes 983048 | tf_op jit(solution)/shard_map/ppermute | solution.py:163
  43.3 2.5 %collective-permute-start.8 = (bf16[256,640]{1,0:T(8,128)(2,1)S(1)}, bf16[256,640]{1,0:T(8,128)(2,1)S(1)}, u32[]{:S(2)}, u32[]{:S(2)}) collective-permute-start(bf16[256,640]{1,0:T(8,128)(2,1)S(1)} %pad_maximum_fusion), channel_id=1, source_target_pairs={{0,6},{4,0},{2,4},{6,2},{1,7},{5,1},{3,5},{7,3},{8,14},{12,8},{10,... | collective-permute-start | bytes 983048 | tf_op jit(solution)/shard_map/ppermute | solution.py:163
  45.8 11.8 %collective-permute-done.6 = bf16[256,640]{1,0:T(8,128)(2,1)S(1)} collective-permute-done((bf16[256,640]{1,0:T(8,128)(2,1)S(1)}, bf16[256,640]{1,0:T(8,128)(2,1)S(1)}, u32[]{:S(2)}, u32[]{:S(2)}) %collective-permute-start.6) | collective-permute-done | bytes 327712 | tf_op jit(solution)/shard_map/ppermute | solution.py:163
  57.7 7.7 %collective-permute-done.8 = bf16[256,640]{1,0:T(8,128)(2,1)S(1)} collective-permute-done((bf16[256,640]{1,0:T(8,128)(2,1)S(1)}, bf16[256,640]{1,0:T(8,128)(2,1)S(1)}, u32[]{:S(2)}, u32[]{:S(2)}) %collective-permute-start.8) | collective-permute-done | bytes 327712 | tf_op jit(solution)/shard_map/ppermute | solution.py:163
  65.6 2.9 %collective-permute-done.9.other = bf16[1024,640]{1,0:T(8,128)(2,1)S(1)} collective-permute-done((bf16[1024,640]{1,0:T(8,128)(2,1)S(1)}, bf16[1024,640]{1,0:T(8,128)(2,1)S(1)}, u32[]{:S(2)}, u32[]{:S(2)}) %collective-permute-start.9) | collective-permute-done | bytes 1310752 | tf_op jit(solution)/shard_map/ppermute | solution.py:186
  68.5 9.6 %all-to-all-done = bf16[32,64,256]{2,1,0:T(8,128)(2,1)} async-done(((bf16[32,64,256]{2,1,0:T(8,128)(2,1)}), bf16[32,64,256]{2,1,0:T(8,128)(2,1)}, u32[]{:S(2)}, u32[]{:S(2)}) %all-to-all-start) | async-done | bytes 1048608 | tf_op jit(solution)/shard_map/all_to_all | solution.py:182
  78.1 2.8 %shard_map.94 = (f32[256,256]{1,0:T(8,128)S(1)}, f32[256,256]{1,0:T(8,128)S(1)}) custom-call(s32[3]{0:T(128)S(1)} %pad_add_fusion.place, bf16[1024,640]{1,0:T(8,128)(2,1)S(1)} %constant_dynamic-update-slice_fusion.own, bf16[1024,640]{1,0:T(8,128)(2,1)S(1)} %collective-permute-done.9.other, bf16[2048,256]{1,0:T(8,128)(2,1)} %bitcast.10.columns), custom_call_target="tpu_custom_call" | custom-call | tf_op jit(solution)/shard_map/pallas_call | solution.py:64
  80.9 0.8 collective-permute-start.10
  81.7 3.4 %all-gather.2.cloned.1.call-done.right = bf16[2,256,2176]{2,1,0:T(8,128)(2,1)} async-done(((bf16[2,32,2176]{2,1,0:T(8,128)(2,1)}), bf16[2,256,2176]{2,1,0:T(8,128)(2,1)}) %all-gather.2.cloned.1.call-update) | async-done | bytes 2228240 | tf_op jit(solution)/shard_map/all_gather | solution.py:179
  85.1 1.0 convert_reduce_fusion.scales
  86.1 2.9 %collective-permute-done.10.theirs = f32[256,256]{1,0:T(8,128)S(1)} collective-permute-done((f32[256,256]{1,0:T(8,128)S(1)}, f32[256,256]{1,0:T(8,128)S(1)}, u32[]{:S(2)}, u32[]{:S(2)}) %collective-permute-start.10) | collective-permute-done | bytes 262176 | tf_op jit(solution)/shard_map/ppermute | solution.py:195
  89.0 1.6 copy-done
  90.6 1.3 shard_map.95
  92.1 18.9 %all_to_all.20 = f16[4,64,2176]{2,1,0:T(8,128)(2,1)S(1)} all-to-all(f16[4,64,2176]{2,1,0:T(8,128)(2,1)S(1)} %bitcast.30), channel_id=1, replica_groups=mesh['zh'=2,'zl'=4,'x'=4,'l'=2,'h'=2,'c'=2] {'x'}, dimensions={0} | all-to-all | bytes 2228224 | tf_op jit(solution)/shard_map/all_to_all | solution.py:200
  111.1 0.9 copy-done.2
  112.2 1.5 shard_map.96
  113.8 16.3 %all_to_all.21 = f16[4,64,2176]{2,1,0:T(8,128)(2,1)S(1)} all-to-all(f16[4,64,2176]{2,1,0:T(8,128)(2,1)S(1)} %broadcast_in_dim.53), channel_id=1, replica_groups=mesh['zh'=2,'zl'=4,'x'=4,'l'=2,'h'=2,'c'=2] {'x'}, dimensions={0} | all-to-all | bytes 2228224 | tf_op jit(solution)/shard_map/all_to_all | solution.py:207
  130.3 1.4 copy-done.1
  131.7 1.3 shard_map.97
  133.0 0.7 collective-permute-start.11
  134.2 5.4 %collective-permute-done.11.theirs = f32[264,256]{1,0:T(8,128)S(1)} collective-permute-done((f32[264,256]{1,0:T(8,128)S(1)}, f32[264,256]{1,0:T(8,128)S(1)}, u32[]{:S(2)}, u32[]{:S(2)}) %collective-permute-start.11) | collective-permute-done | bytes 270368 | tf_op jit(solution)/shard_map/ppermute | solution.py:214
  139.6 0.5 slice.37
  141.3 1.9 %shard_map.98 = f32[2048,256]{1,0:T(8,128)S(1)} custom-call(s32[3]{0:T(128)S(1)} %pad_add_fusion.place, f32[1]{0:T(128)} %bitcast.14.factor, bf16[1024,640]{1,0:T(8,128)(2,1)S(1)} %constant_dynamic-update-slice_fusion.own, bf16[1024,640]{1,0:T(8,128)(2,1)S(1)} %collective-permute-done.9.other, f32[256,256]{1,0:T(8,128)S(1)} %get-tuple-element.20.mine, ...), custom_call_target="tpu_custom_call" | custom-call | tf_op jit(solution)/shard_map/pallas_call | solution.py:64
  143.3 1.2 convert_element_type.29
  144.5 6.0 %all-to-all-start.3 = ((f16[32,64,256]{2,1,0:T(8,128)(2,1)}), f16[32,64,256]{2,1,0:T(8,128)(2,1)S(1)}, u32[]{:S(2)}, u32[]{:S(2)}) async-start(f16[32,64,256]{2,1,0:T(8,128)(2,1)} %bitcast.15), calls=%async_computation.3 | async-start | bytes 2097152 | tf_op jit(solution)/shard_map/all_to_all | solution.py:228
  150.5 1.5 collective-permute-start.12
  152.1 2.4 %collective-permute-start.13 = (f32[8,128]{1,0:T(8,128)S(1)}, f32[8,128]{1,0:T(8,128)S(1)}, u32[]{:S(2)}, u32[]{:S(2)}) collective-permute-start(f32[8,128]{1,0:T(8,128)S(1)} %broadcast_in_dim.56), channel_id=1, source_target_pairs={{0,64},{32,96},{64,0},{96,32},{1,65},{33,97},{65,1},{97,33},{2,66}... | collective-permute-start | bytes 12296 | tf_op jit(solution)/shard_map/ppermute | solution.py:219
  154.5 1.4 collective-permute-start.14
  155.9 11.0 %collective-permute-done.12 = f32[8,128]{1,0:T(8,128)S(1)} collective-permute-done((f32[8,128]{1,0:T(8,128)S(1)}, f32[8,128]{1,0:T(8,128)S(1)}, u32[]{:S(2)}, u32[]{:S(2)}) %collective-permute-start.12) | collective-permute-done | bytes 4128 | tf_op jit(solution)/shard_map/ppermute | solution.py:219
  166.9 0.5 slice.31
  167.4 4.3 %collective-permute-done.13 = f32[8,128]{1,0:T(8,128)S(1)} collective-permute-done((f32[8,128]{1,0:T(8,128)S(1)}, f32[8,128]{1,0:T(8,128)S(1)}, u32[]{:S(2)}, u32[]{:S(2)}) %collective-permute-start.13) | collective-permute-done | bytes 4128 | tf_op jit(solution)/shard_map/ppermute | solution.py:219
  171.7 0.6 slice.32
  172.3 0.6 slice.33
  172.9 1.9 %multiply_exponential_fusion = f32[4]{0:T(128)S(1)} fusion(f32[]{:T(128)} %bitcast.19, s32[]{:T(128)S(6)} %select_n.82, f32[]{:T(128)} %bitcast.18, s32[]{:T(128)S(6)} %select_n.80, f32[]{:T(128)} %bitcast.17, s32[]{:T(128)S(6)} %select_n.78, f32[]{:T(128)} %bitcast.13, s32[]{:T(128)S(6)} %axis_index.77), kind=kLoop, calls=%fused_computation.29 | loop fusion | flops 52 | bytes 48 | tf_op jit(solution)/shard_map/exp2 | solution.py:229
  175.6 1.1 copy.20
  (42 shorter events, 3.4 us)
Async XLA Ops:
  7.2 24.0 %copy-start.4 = (bf16[64,2048]{1,0:T(8,128)(2,1)S(1)}, bf16[64,2048]{1,0:T(8,128)(2,1)}, u32[]{:S(2)}) copy-start(bf16[64,2048]{1,0:T(8,128)(2,1)} %param.7) | copy-start | bytes 786436
  7.2 77.9 %all-gather.2.cloned.1.call-start = ((), (), s32[]{:S(2)}) async-start(), calls=%async_computation.4 | async-start | bytes 2506752 | tf_op jit(solution)/shard_map/all_gather | solution.py:179
  8.9 12.3 %collective-permute-start = (bf16[1,32,2176]{2,1,0:T(8,128)(2,1)S(1)}, bf16[1,32,2176]{2,1,0:T(8,128)(2,1)S(1)}, u32[]{:S(2)}, u32[]{:S(2)}) collective-permute-start(bf16[1,32,2176]{2,1,0:T(8,128)(2,1)S(1)} %pad_maximum_fusion.2), channel_id=1, source_target_pairs={{0,4},{4,0},{1,5},{5,1},{2,6},{6,2},{3,7},{7,3},{8,12},{12,8},{9,1... | collective-permute-start | bytes 417800 | tf_op jit(solution)/shard_map/ppermute | solution.py:171
  12.8 10.1 %collective-permute-start.1 = (bf16[32,640]{1,0:T(8,128)(2,1)S(1)}, bf16[32,640]{1,0:T(8,128)(2,1)S(1)}, u32[]{:S(2)}, u32[]{:S(2)}) collective-permute-start(bf16[32,640]{1,0:T(8,128)(2,1)S(1)} %get-tuple-element.32), channel_id=1, source_target_pairs={{0,0},{1,32},{2,64},{3,96},{4,128},{5,160},{6,192},{7,224},{8,8},{... | collective-permute-start | bytes 122888 | tf_op jit(solution)/shard_map/ppermute | solution.py:175
  21.1 4.2 %collective-permute-start.2 = (bf16[32,640]{1,0:T(8,128)(2,1)S(1)}, bf16[32,640]{1,0:T(8,128)(2,1)S(1)}, u32[]{:S(2)}, u32[]{:S(2)}) collective-permute-start(bf16[32,640]{1,0:T(8,128)(2,1)S(1)} %get-tuple-element.31), channel_id=1, source_target_pairs={{0,128},{1,160},{2,192},{3,224},{4,0},{5,32},{6,64},{7,96},{8,136}... | collective-permute-start | bytes 122888 | tf_op jit(solution)/shard_map/ppermute | solution.py:176
  25.4 15.3 %collective-permute-start.3 = (bf16[64,640]{1,0:T(8,128)(2,1)S(1)}, bf16[64,640]{1,0:T(8,128)(2,1)S(1)}, u32[]{:S(2)}, u32[]{:S(2)}) collective-permute-start(bf16[64,640]{1,0:T(8,128)(2,1)S(1)} %get-tuple-element.30), channel_id=1, source_target_pairs={{0,8},{8,16},{16,24},{24,0},{1,9},{9,17},{17,25},{25,1},{2,10},{10... | collective-permute-start | bytes 245768 | tf_op jit(solution)/shard_map/ppermute | solution.py:163
  27.0 13.8 %collective-permute-start.4 = (bf16[64,640]{1,0:T(8,128)(2,1)S(1)}, bf16[64,640]{1,0:T(8,128)(2,1)S(1)}, u32[]{:S(2)}, u32[]{:S(2)}) collective-permute-start(bf16[64,640]{1,0:T(8,128)(2,1)S(1)} %get-tuple-element.30), channel_id=1, source_target_pairs={{0,16},{8,24},{16,0},{24,8},{1,17},{9,25},{17,1},{25,9},{2,18},{10... | collective-permute-start | bytes 245768 | tf_op jit(solution)/shard_map/ppermute | solution.py:163
  29.7 11.1 %collective-permute-start.5 = (bf16[64,640]{1,0:T(8,128)(2,1)S(1)}, bf16[64,640]{1,0:T(8,128)(2,1)S(1)}, u32[]{:S(2)}, u32[]{:S(2)}) collective-permute-start(bf16[64,640]{1,0:T(8,128)(2,1)S(1)} %get-tuple-element.30), channel_id=1, source_target_pairs={{0,24},{8,0},{16,8},{24,16},{1,25},{9,1},{17,9},{25,17},{2,26},{10... | collective-permute-start | bytes 245768 | tf_op jit(solution)/shard_map/ppermute | solution.py:163
  32.8 45.3 %all-to-all-start = ((bf16[32,64,256]{2,1,0:T(8,128)(2,1)}), bf16[32,64,256]{2,1,0:T(8,128)(2,1)}, u32[]{:S(2)}, u32[]{:S(2)}) async-start(bf16[32,64,256]{2,1,0:T(8,128)(2,1)} %bitcast.9), calls=%async_computation | async-start | bytes 2097152 | tf_op jit(solution)/shard_map/all_to_all | solution.py:182
  40.8 16.8 %collective-permute-start.6 = (bf16[256,640]{1,0:T(8,128)(2,1)S(1)}, bf16[256,640]{1,0:T(8,128)(2,1)S(1)}, u32[]{:S(2)}, u32[]{:S(2)}) collective-permute-start(bf16[256,640]{1,0:T(8,128)(2,1)S(1)} %pad_maximum_fusion), channel_id=1, source_target_pairs={{0,4},{4,2},{2,6},{6,0},{1,5},{5,3},{3,7},{7,1},{8,12},{12,10},{10... | collective-permute-start | bytes 983048 | tf_op jit(solution)/shard_map/ppermute | solution.py:163
  41.0 16.6 %collective-permute-start.7 = (bf16[256,640]{1,0:T(8,128)(2,1)S(1)}, bf16[256,640]{1,0:T(8,128)(2,1)S(1)}, u32[]{:S(2)}, u32[]{:S(2)}) collective-permute-start(bf16[256,640]{1,0:T(8,128)(2,1)S(1)} %pad_maximum_fusion), channel_id=1, source_target_pairs={{0,2},{4,6},{2,0},{6,4},{1,3},{5,7},{3,1},{7,5},{8,10},{12,14},{10... | collective-permute-start | bytes 983048 | tf_op jit(solution)/shard_map/ppermute | solution.py:163
  43.3 22.1 %collective-permute-start.8 = (bf16[256,640]{1,0:T(8,128)(2,1)S(1)}, bf16[256,640]{1,0:T(8,128)(2,1)S(1)}, u32[]{:S(2)}, u32[]{:S(2)}) collective-permute-start(bf16[256,640]{1,0:T(8,128)(2,1)S(1)} %pad_maximum_fusion), channel_id=1, source_target_pairs={{0,6},{4,0},{2,4},{6,2},{1,7},{5,1},{3,5},{7,3},{8,14},{12,8},{10,... | collective-permute-start | bytes 983048 | tf_op jit(solution)/shard_map/ppermute | solution.py:163
  65.4 3.1 %collective-permute-start.9 = (bf16[1024,640]{1,0:T(8,128)(2,1)S(1)}, bf16[1024,640]{1,0:T(8,128)(2,1)S(1)}, u32[]{:S(2)}, u32[]{:S(2)}) collective-permute-start(bf16[1024,640]{1,0:T(8,128)(2,1)S(1)} %constant_dynamic-update-slice_fusion.own), channel_id=1, source_target_pairs={{0,1},{1,0},{2,3},{3,2},{4,5},{5,4},{6,7},{7,6},{8,9},{9,8},{10,11... | collective-permute-start | bytes 3932168 | tf_op jit(solution)/shard_map/ppermute | solution.py:186
  80.9 8.1 %collective-permute-start.10 = (f32[256,256]{1,0:T(8,128)S(1)}, f32[256,256]{1,0:T(8,128)S(1)}, u32[]{:S(2)}, u32[]{:S(2)}) collective-permute-start(f32[256,256]{1,0:T(8,128)S(1)} %get-tuple-element.16), channel_id=1, source_target_pairs={{0,4},{4,0},{1,5},{5,1},{2,6},{6,2},{3,7},{7,3},{8,12},{12,8},{9,1... | collective-permute-start | bytes 786440 | tf_op jit(solution)/shard_map/ppermute | solution.py:195
  89.0 1.6 copy-start
  111.0 1.0 copy-start.2
  111.0 1.2 copy-start.3
  130.1 1.6 copy-start.1
  133.0 6.5 %collective-permute-start.11 = (f32[264,256]{1,0:T(8,128)S(1)}, f32[264,256]{1,0:T(8,128)S(1)}, u32[]{:S(2)}, u32[]{:S(2)}) collective-permute-start(f32[264,256]{1,0:T(8,128)S(1)} %get-tuple-element.19), channel_id=1, source_target_pairs={{0,4},{4,0},{1,5},{5,1},{2,6},{6,2},{3,7},{7,3},{8,12},{12,8},{9,1... | collective-permute-start | bytes 811016 | tf_op jit(solution)/shard_map/ppermute | solution.py:214
  144.5 30.3 %all-to-all-start.3 = ((f16[32,64,256]{2,1,0:T(8,128)(2,1)}), f16[32,64,256]{2,1,0:T(8,128)(2,1)S(1)}, u32[]{:S(2)}, u32[]{:S(2)}) async-start(f16[32,64,256]{2,1,0:T(8,128)(2,1)} %bitcast.15), calls=%async_computation.3 | async-start | bytes 2097152 | tf_op jit(solution)/shard_map/all_to_all | solution.py:228
  150.5 16.4 %collective-permute-start.12 = (f32[8,128]{1,0:T(8,128)S(1)}, f32[8,128]{1,0:T(8,128)S(1)}, u32[]{:S(2)}, u32[]{:S(2)}) collective-permute-start(f32[8,128]{1,0:T(8,128)S(1)} %broadcast_in_dim.56), channel_id=1, source_target_pairs={{0,32},{32,64},{64,96},{96,0},{1,33},{33,65},{65,97},{97,1},{2,34}... | collective-permute-start | bytes 12296 | tf_op jit(solution)/shard_map/ppermute | solution.py:219
  152.1 19.7 %collective-permute-start.13 = (f32[8,128]{1,0:T(8,128)S(1)}, f32[8,128]{1,0:T(8,128)S(1)}, u32[]{:S(2)}, u32[]{:S(2)}) collective-permute-start(f32[8,128]{1,0:T(8,128)S(1)} %broadcast_in_dim.56), channel_id=1, source_target_pairs={{0,64},{32,96},{64,0},{96,32},{1,65},{33,97},{65,1},{97,33},{2,66}... | collective-permute-start | bytes 12296 | tf_op jit(solution)/shard_map/ppermute | solution.py:219
  154.5 17.8 %collective-permute-start.14 = (f32[8,128]{1,0:T(8,128)S(1)}, f32[8,128]{1,0:T(8,128)S(1)}, u32[]{:S(2)}, u32[]{:S(2)}) collective-permute-start(f32[8,128]{1,0:T(8,128)S(1)} %broadcast_in_dim.56), channel_id=1, source_target_pairs={{0,96},{32,0},{64,32},{96,64},{1,97},{33,1},{65,33},{97,65},{2,98}... | collective-permute-start | bytes 12296 | tf_op jit(solution)/shard_map/ppermute | solution.py:219
Sparse Core Ops, SparseCore 0:
  25.5 59.5 all-gather.1

commit v3 on v2

--- a/solution.py
+++ b/solution.py
@@ -94,9 +94,10 @@
     half = dot(own[:, :PLANE], scaled[:1024], (0, 0)) + dot(other[:, :PLANE], scaled[1024:], (0, 0))
     total[...] = half[:, :SLICE] + half[:, SLICE:]
     l = lax.rem(place[1], 2)
-    for x in range(4):
-        mine[x * ROWS:(x + 1) * ROWS, :] = total[pl.ds(pl.multiple_of((2 * x + l) * ROWS, ROWS), ROWS), :]
-        theirs[x * ROWS:(x + 1) * ROWS, :] = total[pl.ds(pl.multiple_of((2 * x + 1 - l) * ROWS, ROWS), ROWS), :]
+    for s in range(4):
+        x = lax.rem(place[2] + s, 4)
+        mine[s * ROWS:(s + 1) * ROWS, :] = total[pl.ds(pl.multiple_of((2 * x + l) * ROWS, ROWS), ROWS), :]
+        theirs[s * ROWS:(s + 1) * ROWS, :] = total[pl.ds(pl.multiple_of((2 * x + 1 - l) * ROWS, ROWS), ROWS), :]
 
 
 def right_kernel(mine, theirs, scales, right, message):
@@ -115,10 +116,10 @@
     message[:, WIDTH:] = jnp.broadcast_to(power, (4 * ROWS, LANES))
 
 
-def moment_kernel(got, moment1, moment2, first_new, second_new, message):
-    rotated = jnp.zeros((ROWS, WIDTH), F32)
-    for source in range(4):
-        rotated += got[source, :, :WIDTH] * jnp.exp2(got[source, :, WIDTH:WIDTH + 1] - 15.0)
+def moment_kernel(own, got1, got2, got3, moment1, moment2, first_new, second_new, message):
+    rotated = own[:ROWS, :WIDTH] * jnp.exp2(own[:ROWS, WIDTH:WIDTH + 1] - 15.0)
+    for got in (got1, got2, got3):
+        rotated += got[:, :WIDTH] * jnp.exp2(got[:, WIDTH:WIDTH + 1] - 15.0)
     first = beta_one * moment1[...] + (1.0 - beta_one) * rotated
     second = beta_two * moment2[...] + (1.0 - beta_two) * rotated * rotated
     first_new[...] = first
@@ -129,21 +130,31 @@
     message[:, WIDTH:] = jnp.broadcast_to(power, (ROWS, LANES))
 
 
-def back_kernel(got, scales, right, mine, theirs):
-    power = got[:, WIDTH:WIDTH + 1]
-    high, low = split(got[:, :WIDTH])
-    factor = jnp.exp2(power - 15.0)
+def back_kernel(own, got1, got2, got3, scales, right, mine, theirs, top, high, low):
     near, far = right[0, :, :WIDTH], right[1, :, :WIDTH]
-    mine[...] = (dot(high, near, (1, 1)) + dot(low, near, (1, 1))) * factor * scales[0:1, :]
-    theirs[:4 * ROWS, :] = (dot(high, far, (1, 1)) + dot(low, far, (1, 1))) * factor * scales[1:2, :]
-    theirs[4 * ROWS:, :] = jnp.broadcast_to(jnp.max(power, axis=0, keepdims=True), (8, SLICE))
-
-
-def update_kernel(place, factor, own, other, mine, theirs, update, parts):
+    best = jnp.zeros((1, 1), F32) - 200.0
+    factors = []
+    for s, got in enumerate((own, got1, got2, got3)):
+        power = got[:, WIDTH:WIDTH + 1]
+        best = jnp.maximum(best, jnp.max(power, axis=0, keepdims=True))
+        factors.append(jnp.exp2(power - 15.0))
+        high[s * ROWS:(s + 1) * ROWS, :], low[s * ROWS:(s + 1) * ROWS, :] = split(got[:, :WIDTH])
+    factor = jnp.concatenate(factors)
+    mine[...] = (dot(high[...], near, (1, 1)) + dot(low[...], near, (1, 1))) * factor * scales[0:1, :]
+    theirs[:4 * ROWS, :] = (dot(high[...], far, (1, 1)) + dot(low[...], far, (1, 1))) * factor * scales[1:2, :]
+    top[...] = jnp.broadcast_to(best, (8, SLICE))
+    theirs[4 * ROWS:, :] = jnp.broadcast_to(best, (8, SLICE))
+
+
+def update_kernel(place, own, other, mine, theirs, top, update, tops, parts):
     l = lax.rem(place[1], 2)
-    for x in range(4):
+    best = jnp.maximum(top[...], theirs[4 * ROWS:, :])
+    tops[...] = best
+    factor = jnp.exp2(-1.0 - best[0:1, :])
+    for s in range(4):
+        x = lax.rem(place[2] - s + 4, 4)
         for values, side in ((mine, l), (theirs, 1 - l)):
-            high, low = split(values[x * ROWS:(x + 1) * ROWS, :] * factor[0])
+            high, low = split(values[s * ROWS:(s + 1) * ROWS, :] * factor)
             rows = pl.ds(pl.multiple_of((2 * x + side) * ROWS, ROWS), ROWS)
             parts[rows, :SLICE] = high
             parts[rows, SLICE:] = low
@@ -156,6 +167,10 @@
             update[pl.ds(start, ROWS), lane:lane + LANES] = values[part][row:row + ROWS, lane:lane + LANES] * scale
 
 
+def shifted(value, axis, shift):
+    return lax.ppermute(value, axis, [(i, (i + shift) % 4) for i in range(4)])
+
+
 def ring_gather(value, axes, names):
     size = len(names)
     blocks = [value]
@@ -197,37 +212,34 @@
     (message,) = call(
         right_kernel, [(4 * ROWS, WIDTH + LANES)], operands=(mine, theirs, scales, right)
     )
-    got = lax.all_to_all(message.astype(F16).reshape(4, ROWS, -1), "x", 0, 0, tiled=True)
+    got = [shifted(message[s * ROWS:(s + 1) * ROWS].astype(F16), "x", s).astype(F32) for s in range(1, 4)]
     first_new, second_new, message = call(
         moment_kernel,
         [(ROWS, WIDTH)] * 2 + [(ROWS, WIDTH + LANES)],
-        operands=(got.astype(F32), moment1, moment2),
-    )
-    message = message.astype(F16)
-    got = lax.all_to_all(jnp.broadcast_to(message, (4,) + message.shape), "x", 0, 0, tiled=True)
-    mine, theirs = call(
+        operands=(message, *got, moment1, moment2),
+    )
+    narrow = message.astype(F16)
+    got = [shifted(narrow, "x", s).astype(F32) for s in range(1, 4)]
+    mine, theirs, top = call(
         back_kernel,
-        [(4 * ROWS, SLICE), (4 * ROWS + 8, SLICE)],
-        operands=(got.astype(F32).reshape(4 * ROWS, -1), scales, right),
-    )
-    top = theirs[-1, 0]
+        [(4 * ROWS, SLICE), (4 * ROWS + 8, SLICE), (8, SLICE)],
+        [pltpu.VMEM((4 * ROWS, WIDTH), BF16)] * 2,
+        operands=(message, *got, scales, right),
+    )
     theirs = lax.ppermute(theirs, "l", SWAP)
-    top = jnp.maximum(top, theirs[-1, 0])
-    lane = jnp.full((8, LANES), top)
-    tops = jnp.where(jnp.arange(4) == zl, top, 0.0)
-    for shift in range(1, 4):
-        other = lax.ppermute(lane, "zl", [(i, (i + shift) % 4) for i in range(4)])
-        tops = tops + jnp.where(jnp.arange(4) == (zl - shift) % 4, other[0, 0], 0.0)
-    (update,) = call(
+    update, top = call(
         update_kernel,
-        [(WIDTH, SLICE)],
+        [(WIDTH, SLICE), (8, SLICE)],
         [pltpu.VMEM((PLANE, 2 * SLICE), BF16)],
-        2,
-        (place, jnp.exp2(-1.0 - top).reshape(1), left_own, left_other, mine, theirs),
-    )
+        1,
+        (place, left_own, left_other, mine, theirs, top),
+    )
+    planes = jnp.arange(4)[:, None, None, None]
+    tops = jnp.where(planes == zl, top[:1], 0.0)
+    for s in range(1, 4):
+        tops = tops + jnp.where(planes == (zl - s) % 4, shifted(top, "zl", s)[:1], 0.0)
     got = lax.all_to_all(update.astype(F16).reshape(32, ROWS, SLICE), ("zl", "x", "l"), 0, 0, tiled=True)
-    factors = jnp.exp2(tops + 1.0)[:, None, None, None]
-    update = jnp.sum(got.reshape(4, 8, ROWS, SLICE).astype(F32) * factors, axis=0)
+    update = jnp.sum(got.reshape(4, 8, ROWS, SLICE).astype(F32) * jnp.exp2(tops + 1.0), axis=0)
     update = update.reshape(8, ROWS, 8, 32).transpose(1, 2, 0, 3).reshape(ROWS, WIDTH)
     return update, first_new, second_new
 

time: 184 us -> 181 us (0.984)
  blocking collectives: 35.2 us -> 0 us
  waiting for transfers between devices: 61.5 us -> 88.6 us
  starting transfers between devices: 42.3 us -> 55.6 us
  local copies, waits for them, and re-layouts: 11.7 us -> 6.6 us
  other arithmetic: 8.5 us -> 6.42 us
    all_to_all x2 -> x0, blocking collectives: 35.2 us -> none  [the longest x1 18.9 us: body(): lax.all_to_all(message.astype(F16).reshape(4, ROWS, -1), 'x', 0, 0, tiled...]
    ppermute x3 -> x9, waiting for transfers between devices: 15.3 us -> 40.1 us  [shifted(): return lax.ppermute(value, axis, [(i, (i + shift) % 4) for i in range(4)])]
    ppermute x3 -> x9, starting transfers between devices: 5.37 us -> 16.4 us  [shifted(): return lax.ppermute(value, axis, [(i, (i + shift) % 4) for i in range(4)])]
    slice x5, local copies, waits for them, and re-layouts: 2.71 us -> 0.15 us  [the longest x1 0.14 us: body(): message[s * ROWS:(s + 1) * ROWS].astype(F16)]
    unnamed x17, local copies, waits for them, and re-layouts: 5.59 us -> 3.16 us
    all_to_all x1, starting transfers between devices: 6.01 us -> 8.27 us  [body(): lax.all_to_all(update.astype(F16).reshape(32, ROWS, SLICE), ('zl', 'x', '...]
  transfers between devices with their start and end apart: 18 -> 24, of which waited for: 10 -> 15; matrix products, arithmetic and copies ran while one was open for 6% -> 4% of each run, Pallas kernels for 2% -> 2%
where the time goes in v3:
time: 181 us
  waiting for transfers between devices  88.6 us (49%)
  starting transfers between devices  55.6 us (31%)
  between operations  14.4 us (8%)
  Pallas kernels  8.87 us (5%)
  local copies, waits for them, and re-layouts  6.6 us (4%)
  other arithmetic  6.42 us (4%)
    ppermute x9, waiting for transfers between devices, shifted(): return lax.ppermute(value, axis, [(i, (i + shift) % 4) for i in range(4)])  40.1 us
    ppermute x6, waiting for transfers between devices, ring_gather(): lax.ppermute(value, axes, [(names[i], names[(i + shift) % size]) for i in...  19.5 us
    ppermute x9, starting transfers between devices, shifted(): return lax.ppermute(value, axis, [(i, (i + shift) % 4) for i in range(4)])  16.4 us
    ppermute x6, starting transfers between devices, ring_gather(): lax.ppermute(value, axes, [(names[i], names[(i + shift) % size]) for i in...  10.6 us
    all_to_all x1, waiting for transfers between devices, body(): lax.all_to_all(columns, ('zl', 'x', 'l'), 0, 0, tiled=True)  9.58 us
    ppermute x2, waiting for transfers between devices, body(): theirs = lax.ppermute(theirs, 'l', SWAP)  9.31 us
    pallas_call x5, Pallas kernels, call(): pl.pallas_call(kernel, out_shape=tuple((jax.ShapeDtypeStruct(shape, F32)...  8.87 us
    ppermute x1, starting transfers between devices, body(): got1 = lax.ppermute(jnp.where(l == 0, pieces[0], pieces[1]), AXES, first)  8.38 us
  transfers between devices with their start and end apart: 24, of which 15 were waited for; matrix products, arithmetic and copies ran while one was open for 4% of the time, Pallas kernels for 2%

profile of v3, /device:TPU:8, one launch (start us, length us, event | category | flops | bytes accessed | tf_op | source)
XLA Modules:
  0.0 180.6 jit_solution(4200571581565813178)
XLA Ops:
  7.2 0.8 broadcast_in_dim.74
  8.0 0.9 pad_maximum_fusion.2
  8.9 2.3 %collective-permute-start = (bf16[1,32,2176]{2,1,0:T(8,128)(2,1)S(1)}, bf16[1,32,2176]{2,1,0:T(8,128)(2,1)S(1)}, u32[]{:S(2)}, u32[]{:S(2)}) collective-permute-start(bf16[1,32,2176]{2,1,0:T(8,128)(2,1)S(1)} %pad_maximum_fusion.2), channel_id=1, source_target_pairs={{0,4},{4,0},{1,5},{5,1},{2,6},{6,2},{3,7},{7,3},{8,12},{12,8},{9,1... | collective-permute-start | bytes 417800 | tf_op jit(solution)/shard_map/ppermute | solution.py:186
  11.9 0.9 select_bitcast_fusion
  12.8 8.4 %collective-permute-start.1 = (bf16[32,640]{1,0:T(8,128)(2,1)S(1)}, bf16[32,640]{1,0:T(8,128)(2,1)S(1)}, u32[]{:S(2)}, u32[]{:S(2)}) collective-permute-start(bf16[32,640]{1,0:T(8,128)(2,1)S(1)} %get-tuple-element.41), channel_id=1, source_target_pairs={{0,0},{1,32},{2,64},{3,96},{4,128},{5,160},{6,192},{7,224},{8,8},{... | collective-permute-start | bytes 122888 | tf_op jit(solution)/shard_map/ppermute | solution.py:190
  21.2 1.6 pad_maximum_fusion.1
  22.9 2.5 %collective-permute-done.2 = bf16[32,640]{1,0:T(8,128)(2,1)S(1)} collective-permute-done((bf16[32,640]{1,0:T(8,128)(2,1)S(1)}, bf16[32,640]{1,0:T(8,128)(2,1)S(1)}, u32[]{:S(2)}, u32[]{:S(2)}) %collective-permute-start.2) | collective-permute-done | bytes 40992 | tf_op jit(solution)/shard_map/ppermute | solution.py:191
  25.4 1.6 collective-permute-start.3
  27.0 2.7 %collective-permute-start.4 = (bf16[64,640]{1,0:T(8,128)(2,1)S(1)}, bf16[64,640]{1,0:T(8,128)(2,1)S(1)}, u32[]{:S(2)}, u32[]{:S(2)}) collective-permute-start(bf16[64,640]{1,0:T(8,128)(2,1)S(1)} %get-tuple-element.36), channel_id=1, source_target_pairs={{0,16},{8,24},{16,0},{24,8},{1,17},{9,25},{17,1},{25,9},{2,18},{10... | collective-permute-start | bytes 245768 | tf_op jit(solution)/shard_map/ppermute | solution.py:178
  29.7 1.4 collective-permute-start.5
  31.7 1.1 broadcast_in_dim.77
  32.8 7.9 %all-to-all-start = ((bf16[32,64,256]{2,1,0:T(8,128)(2,1)}), bf16[32,64,256]{2,1,0:T(8,128)(2,1)}, u32[]{:S(2)}, u32[]{:S(2)}) async-start(bf16[32,64,256]{2,1,0:T(8,128)(2,1)} %bitcast.9), calls=%async_computation | async-start | bytes 2097152 | tf_op jit(solution)/shard_map/all_to_all | solution.py:197
  41.0 2.2 %collective-permute-start.7 = (bf16[256,640]{1,0:T(8,128)(2,1)S(1)}, bf16[256,640]{1,0:T(8,128)(2,1)S(1)}, u32[]{:S(2)}, u32[]{:S(2)}) collective-permute-start(bf16[256,640]{1,0:T(8,128)(2,1)S(1)} %pad_maximum_fusion), channel_id=1, source_target_pairs={{0,2},{4,6},{2,0},{6,4},{1,3},{5,7},{3,1},{7,5},{8,10},{12,14},{10... | collective-permute-start | bytes 983048 | tf_op jit(solution)/shard_map/ppermute | solution.py:178
  43.3 2.5 %collective-permute-start.8 = (bf16[256,640]{1,0:T(8,128)(2,1)S(1)}, bf16[256,640]{1,0:T(8,128)(2,1)S(1)}, u32[]{:S(2)}, u32[]{:S(2)}) collective-permute-start(bf16[256,640]{1,0:T(8,128)(2,1)S(1)} %pad_maximum_fusion), channel_id=1, source_target_pairs={{0,6},{4,0},{2,4},{6,2},{1,7},{5,1},{3,5},{7,3},{8,14},{12,8},{10,... | collective-permute-start | bytes 983048 | tf_op jit(solution)/shard_map/ppermute | solution.py:178
  45.8 11.8 %collective-permute-done.6 = bf16[256,640]{1,0:T(8,128)(2,1)S(1)} collective-permute-done((bf16[256,640]{1,0:T(8,128)(2,1)S(1)}, bf16[256,640]{1,0:T(8,128)(2,1)S(1)}, u32[]{:S(2)}, u32[]{:S(2)}) %collective-permute-start.6) | collective-permute-done | bytes 327712 | tf_op jit(solution)/shard_map/ppermute | solution.py:178
  57.7 7.7 %collective-permute-done.8 = bf16[256,640]{1,0:T(8,128)(2,1)S(1)} collective-permute-done((bf16[256,640]{1,0:T(8,128)(2,1)S(1)}, bf16[256,640]{1,0:T(8,128)(2,1)S(1)}, u32[]{:S(2)}, u32[]{:S(2)}) %collective-permute-start.8) | collective-permute-done | bytes 327712 | tf_op jit(solution)/shard_map/ppermute | solution.py:178
  65.6 2.9 %collective-permute-done.9.other = bf16[1024,640]{1,0:T(8,128)(2,1)S(1)} collective-permute-done((bf16[1024,640]{1,0:T(8,128)(2,1)S(1)}, bf16[1024,640]{1,0:T(8,128)(2,1)S(1)}, u32[]{:S(2)}, u32[]{:S(2)}) %collective-permute-start.9) | collective-permute-done | bytes 1310752 | tf_op jit(solution)/shard_map/ppermute | solution.py:201
  68.5 9.6 %all-to-all-done = bf16[32,64,256]{2,1,0:T(8,128)(2,1)} async-done(((bf16[32,64,256]{2,1,0:T(8,128)(2,1)}), bf16[32,64,256]{2,1,0:T(8,128)(2,1)}, u32[]{:S(2)}, u32[]{:S(2)}) %all-to-all-start) | async-done | bytes 1048608 | tf_op jit(solution)/shard_map/all_to_all | solution.py:197
  78.1 2.7 %shard_map.94 = (f32[256,256]{1,0:T(8,128)S(1)}, f32[256,256]{1,0:T(8,128)S(1)}) custom-call(s32[3]{0:T(128)S(1)} %pad_add_fusion.place, bf16[1024,640]{1,0:T(8,128)(2,1)S(1)} %constant_dynamic-update-slice_fusion.own, bf16[1024,640]{1,0:T(8,128)(2,1)S(1)} %collective-permute-done.9.other, bf16[2048,256]{1,0:T(8,128)(2,1)} %bitcast.10.columns), custom_call_target="tpu_custom_call" | custom-call | tf_op jit(solution)/shard_map/pallas_call | solution.py:64
  80.9 0.8 collective-permute-start.10
  81.7 3.4 %all-gather.2.cloned.1.call-done.right = bf16[2,256,2176]{2,1,0:T(8,128)(2,1)} async-done(((bf16[2,32,2176]{2,1,0:T(8,128)(2,1)}), bf16[2,256,2176]{2,1,0:T(8,128)(2,1)}) %all-gather.2.cloned.1.call-update) | async-done | bytes 2228240 | tf_op jit(solution)/shard_map/all_gather | solution.py:194
  85.1 1.0 convert_reduce_fusion.scales
  86.1 2.8 %collective-permute-done.10.theirs = f32[256,256]{1,0:T(8,128)S(1)} collective-permute-done((f32[256,256]{1,0:T(8,128)S(1)}, f32[256,256]{1,0:T(8,128)S(1)}, u32[]{:S(2)}, u32[]{:S(2)}) %collective-permute-start.10) | collective-permute-done | bytes 262176 | tf_op jit(solution)/shard_map/ppermute | solution.py:210
  88.9 1.6 copy-done
  90.6 1.3 shard_map.95.own
  92.2 1.5 collective-permute-start.11
  93.7 2.8 %collective-permute-start.12 = (f16[64,2176]{1,0:T(8,128)(2,1)S(1)}, f16[64,2176]{1,0:T(8,128)(2,1)S(1)}, u32[]{:S(2)}, u32[]{:S(2)}) collective-permute-start(f16[64,2176]{1,0:T(8,128)(2,1)S(1)} %get-tuple-element.38), channel_id=1, source_target_pairs={{0,16},{8,24},{16,0},{24,8},{1,17},{9,25},{17,1},{25,9},{2,18},{10... | collective-permute-start | bytes 835592 | tf_op jit(solution)/shard_map/ppermute | solution.py:171
  96.5 1.4 collective-permute-start.13
  97.9 4.2 %collective-permute-done.11 = f16[64,2176]{1,0:T(8,128)(2,1)S(1)} collective-permute-done((f16[64,2176]{1,0:T(8,128)(2,1)S(1)}, f16[64,2176]{1,0:T(8,128)(2,1)S(1)}, u32[]{:S(2)}, u32[]{:S(2)}) %collective-permute-start.11) | collective-permute-done | bytes 278560 | tf_op jit(solution)/shard_map/ppermute | solution.py:171
  102.2 5.7 %collective-permute-done.12 = f16[64,2176]{1,0:T(8,128)(2,1)S(1)} collective-permute-done((f16[64,2176]{1,0:T(8,128)(2,1)S(1)}, f16[64,2176]{1,0:T(8,128)(2,1)S(1)}, u32[]{:S(2)}, u32[]{:S(2)}) %collective-permute-start.12) | collective-permute-done | bytes 278560 | tf_op jit(solution)/shard_map/ppermute | solution.py:171
  108.0 1.5 shard_map.96
  109.6 1.4 collective-permute-start.14
  111.0 2.4 %collective-permute-start.15 = (f16[64,2176]{1,0:T(8,128)(2,1)S(1)}, f16[64,2176]{1,0:T(8,128)(2,1)S(1)}, u32[]{:S(2)}, u32[]{:S(2)}) collective-permute-start(f16[64,2176]{1,0:T(8,128)(2,1)S(1)} %convert_element_type.43), channel_id=1, source_target_pairs={{0,16},{8,24},{16,0},{24,8},{1,17},{9,25},{17,1},{25,9},{2,18},{10... | collective-permute-start | bytes 835592 | tf_op jit(solution)/shard_map/ppermute | solution.py:171
  113.4 1.5 collective-permute-start.16
  114.9 3.7 %collective-permute-done.14 = f16[64,2176]{1,0:T(8,128)(2,1)S(1)} collective-permute-done((f16[64,2176]{1,0:T(8,128)(2,1)S(1)}, f16[64,2176]{1,0:T(8,128)(2,1)S(1)}, u32[]{:S(2)}, u32[]{:S(2)}) %collective-permute-start.14) | collective-permute-done | bytes 278560 | tf_op jit(solution)/shard_map/ppermute | solution.py:171
  118.6 6.9 %collective-permute-done.15 = f16[64,2176]{1,0:T(8,128)(2,1)S(1)} collective-permute-done((f16[64,2176]{1,0:T(8,128)(2,1)S(1)}, f16[64,2176]{1,0:T(8,128)(2,1)S(1)}, u32[]{:S(2)}, u32[]{:S(2)}) %collective-permute-start.15) | collective-permute-done | bytes 278560 | tf_op jit(solution)/shard_map/ppermute | solution.py:171
  125.6 1.3 shard_map.97
  127.7 6.5 %collective-permute-done.17.theirs = f32[264,256]{1,0:T(8,128)S(1)} collective-permute-done((f32[264,256]{1,0:T(8,128)S(1)}, f32[264,256]{1,0:T(8,128)S(1)}, u32[]{:S(2)}, u32[]{:S(2)}) %collective-permute-start.17) | collective-permute-done | bytes 270368 | tf_op jit(solution)/shard_map/ppermute | solution.py:229
  134.2 2.0 %shard_map.98 = (f32[2048,256]{1,0:T(8,128)S(1)}, f32[8,256]{1,0:T(8,128)S(1)}) custom-call(s32[3]{0:T(128)S(1)} %pad_add_fusion.place, bf16[1024,640]{1,0:T(8,128)(2,1)S(1)} %constant_dynamic-update-slice_fusion.own, bf16[1024,640]{1,0:T(8,128)(2,1)S(1)} %collective-permute-done.9.other, f32[256,256]{1,0:T(8,128)S(1)} %get-tuple-element.22.mine, ...), custom_call_target="tpu_custom_call" | custom-call | tf_op jit(solution)/shard_map/pallas_call | solution.py:64
  136.1 1.1 convert_element_type.47
  137.3 8.3 %all-to-all-start.1 = ((f16[32,64,256]{2,1,0:T(8,128)(2,1)}), f16[32,64,256]{2,1,0:T(8,128)(2,1)S(1)}, u32[]{:S(2)}, u32[]{:S(2)}) async-start(f16[32,64,256]{2,1,0:T(8,128)(2,1)} %bitcast.11), calls=%async_computation.1 | async-start | bytes 2097152 | tf_op jit(solution)/shard_map/all_to_all | solution.py:241
  145.6 1.5 collective-permute-start.18
  147.2 2.4 %collective-permute-start.19 = (f32[8,256]{1,0:T(8,128)S(1)}, f32[8,256]{1,0:T(8,128)S(1)}, u32[]{:S(2)}, u32[]{:S(2)}) collective-permute-start(f32[8,256]{1,0:T(8,128)S(1)} %get-tuple-element.26), channel_id=1, source_target_pairs={{0,64},{32,96},{64,0},{96,32},{1,65},{33,97},{65,1},{97,33},{2,66}... | collective-permute-start | bytes 24584 | tf_op jit(solution)/shard_map/ppermute | solution.py:171
  149.6 1.4 collective-permute-start.20
  151.0 14.7 %collective-permute-done.18 = f32[8,256]{1,0:T(8,128)S(1)} collective-permute-done((f32[8,256]{1,0:T(8,128)S(1)}, f32[8,256]{1,0:T(8,128)S(1)}, u32[]{:S(2)}, u32[]{:S(2)}) %collective-permute-start.18) | collective-permute-done | bytes 8224 | tf_op jit(solution)/shard_map/ppermute | solution.py:171
  165.7 4.8 %collective-permute-done.19 = f32[8,256]{1,0:T(8,128)S(1)} collective-permute-done((f32[8,256]{1,0:T(8,128)S(1)}, f32[8,256]{1,0:T(8,128)S(1)}, u32[]{:S(2)}, u32[]{:S(2)}) %collective-permute-start.19) | collective-permute-done | bytes 8224 | tf_op jit(solution)/shard_map/ppermute | solution.py:171
  170.7 1.2 all-to-all-done.1
  172.6 1.1 copy.20
  (56 shorter events, 4.1 us)
Async XLA Ops:
  7.2 24.0 %copy-start.4 = (bf16[64,2048]{1,0:T(8,128)(2,1)S(1)}, bf16[64,2048]{1,0:T(8,128)(2,1)}, u32[]{:S(2)}) copy-start(bf16[64,2048]{1,0:T(8,128)(2,1)} %param.7) | copy-start | bytes 786436
  7.2 77.9 %all-gather.2.cloned.1.call-start = ((), (), s32[]{:S(2)}) async-start(), calls=%async_computation.2 | async-start | bytes 2506752 | tf_op jit(solution)/shard_map/all_gather | solution.py:194
  8.9 12.3 %collective-permute-start = (bf16[1,32,2176]{2,1,0:T(8,128)(2,1)S(1)}, bf16[1,32,2176]{2,1,0:T(8,128)(2,1)S(1)}, u32[]{:S(2)}, u32[]{:S(2)}) collective-permute-start(bf16[1,32,2176]{2,1,0:T(8,128)(2,1)S(1)} %pad_maximum_fusion.2), channel_id=1, source_target_pairs={{0,4},{4,0},{1,5},{5,1},{2,6},{6,2},{3,7},{7,3},{8,12},{12,8},{9,1... | collective-permute-start | bytes 417800 | tf_op jit(solution)/shard_map/ppermute | solution.py:186
  12.8 10.1 %collective-permute-start.1 = (bf16[32,640]{1,0:T(8,128)(2,1)S(1)}, bf16[32,640]{1,0:T(8,128)(2,1)S(1)}, u32[]{:S(2)}, u32[]{:S(2)}) collective-permute-start(bf16[32,640]{1,0:T(8,128)(2,1)S(1)} %get-tuple-element.41), channel_id=1, source_target_pairs={{0,0},{1,32},{2,64},{3,96},{4,128},{5,160},{6,192},{7,224},{8,8},{... | collective-permute-start | bytes 122888 | tf_op jit(solution)/shard_map/ppermute | solution.py:190
  21.1 4.2 %collective-permute-start.2 = (bf16[32,640]{1,0:T(8,128)(2,1)S(1)}, bf16[32,640]{1,0:T(8,128)(2,1)S(1)}, u32[]{:S(2)}, u32[]{:S(2)}) collective-permute-start(bf16[32,640]{1,0:T(8,128)(2,1)S(1)} %get-tuple-element.40), channel_id=1, source_target_pairs={{0,128},{1,160},{2,192},{3,224},{4,0},{5,32},{6,64},{7,96},{8,136}... | collective-permute-start | bytes 122888 | tf_op jit(solution)/shard_map/ppermute | solution.py:191
  25.4 15.3 %collective-permute-start.3 = (bf16[64,640]{1,0:T(8,128)(2,1)S(1)}, bf16[64,640]{1,0:T(8,128)(2,1)S(1)}, u32[]{:S(2)}, u32[]{:S(2)}) collective-permute-start(bf16[64,640]{1,0:T(8,128)(2,1)S(1)} %get-tuple-element.36), channel_id=1, source_target_pairs={{0,8},{8,16},{16,24},{24,0},{1,9},{9,17},{17,25},{25,1},{2,10},{10... | collective-permute-start | bytes 245768 | tf_op jit(solution)/shard_map/ppermute | solution.py:178
  27.0 13.8 %collective-permute-start.4 = (bf16[64,640]{1,0:T(8,128)(2,1)S(1)}, bf16[64,640]{1,0:T(8,128)(2,1)S(1)}, u32[]{:S(2)}, u32[]{:S(2)}) collective-permute-start(bf16[64,640]{1,0:T(8,128)(2,1)S(1)} %get-tuple-element.36), channel_id=1, source_target_pairs={{0,16},{8,24},{16,0},{24,8},{1,17},{9,25},{17,1},{25,9},{2,18},{10... | collective-permute-start | bytes 245768 | tf_op jit(solution)/shard_map/ppermute | solution.py:178
  29.7 11.1 %collective-permute-start.5 = (bf16[64,640]{1,0:T(8,128)(2,1)S(1)}, bf16[64,640]{1,0:T(8,128)(2,1)S(1)}, u32[]{:S(2)}, u32[]{:S(2)}) collective-permute-start(bf16[64,640]{1,0:T(8,128)(2,1)S(1)} %get-tuple-element.36), channel_id=1, source_target_pairs={{0,24},{8,0},{16,8},{24,16},{1,25},{9,1},{17,9},{25,17},{2,26},{10... | collective-permute-start | bytes 245768 | tf_op jit(solution)/shard_map/ppermute | solution.py:178
  32.8 45.3 %all-to-all-start = ((bf16[32,64,256]{2,1,0:T(8,128)(2,1)}), bf16[32,64,256]{2,1,0:T(8,128)(2,1)}, u32[]{:S(2)}, u32[]{:S(2)}) async-start(bf16[32,64,256]{2,1,0:T(8,128)(2,1)} %bitcast.9), calls=%async_computation | async-start | bytes 2097152 | tf_op jit(solution)/shard_map/all_to_all | solution.py:197
  40.8 16.8 %collective-permute-start.6 = (bf16[256,640]{1,0:T(8,128)(2,1)S(1)}, bf16[256,640]{1,0:T(8,128)(2,1)S(1)}, u32[]{:S(2)}, u32[]{:S(2)}) collective-permute-start(bf16[256,640]{1,0:T(8,128)(2,1)S(1)} %pad_maximum_fusion), channel_id=1, source_target_pairs={{0,4},{4,2},{2,6},{6,0},{1,5},{5,3},{3,7},{7,1},{8,12},{12,10},{10... | collective-permute-start | bytes 983048 | tf_op jit(solution)/shard_map/ppermute | solution.py:178
  41.0 16.6 %collective-permute-start.7 = (bf16[256,640]{1,0:T(8,128)(2,1)S(1)}, bf16[256,640]{1,0:T(8,128)(2,1)S(1)}, u32[]{:S(2)}, u32[]{:S(2)}) collective-permute-start(bf16[256,640]{1,0:T(8,128)(2,1)S(1)} %pad_maximum_fusion), channel_id=1, source_target_pairs={{0,2},{4,6},{2,0},{6,4},{1,3},{5,7},{3,1},{7,5},{8,10},{12,14},{10... | collective-permute-start | bytes 983048 | tf_op jit(solution)/shard_map/ppermute | solution.py:178
  43.3 22.1 %collective-permute-start.8 = (bf16[256,640]{1,0:T(8,128)(2,1)S(1)}, bf16[256,640]{1,0:T(8,128)(2,1)S(1)}, u32[]{:S(2)}, u32[]{:S(2)}) collective-permute-start(bf16[256,640]{1,0:T(8,128)(2,1)S(1)} %pad_maximum_fusion), channel_id=1, source_target_pairs={{0,6},{4,0},{2,4},{6,2},{1,7},{5,1},{3,5},{7,3},{8,14},{12,8},{10,... | collective-permute-start | bytes 983048 | tf_op jit(solution)/shard_map/ppermute | solution.py:178
  65.4 3.1 %collective-permute-start.9 = (bf16[1024,640]{1,0:T(8,128)(2,1)S(1)}, bf16[1024,640]{1,0:T(8,128)(2,1)S(1)}, u32[]{:S(2)}, u32[]{:S(2)}) collective-permute-start(bf16[1024,640]{1,0:T(8,128)(2,1)S(1)} %constant_dynamic-update-slice_fusion.own), channel_id=1, source_target_pairs={{0,1},{1,0},{2,3},{3,2},{4,5},{5,4},{6,7},{7,6},{8,9},{9,8},{10,11... | collective-permute-start | bytes 3932168 | tf_op jit(solution)/shard_map/ppermute | solution.py:201
  80.9 8.1 %collective-permute-start.10 = (f32[256,256]{1,0:T(8,128)S(1)}, f32[256,256]{1,0:T(8,128)S(1)}, u32[]{:S(2)}, u32[]{:S(2)}) collective-permute-start(f32[256,256]{1,0:T(8,128)S(1)} %get-tuple-element.19), channel_id=1, source_target_pairs={{0,4},{4,0},{1,5},{5,1},{2,6},{6,2},{3,7},{7,3},{8,12},{12,8},{9,1... | collective-permute-start | bytes 786440 | tf_op jit(solution)/shard_map/ppermute | solution.py:210
  88.9 1.6 copy-start
  92.2 15.8 %copy-start.2 = (f32[64,2048]{1,0:T(8,128)S(1)}, f32[64,2048]{1,0:T(8,128)}, u32[]{:S(2)}) copy-start(f32[64,2048]{1,0:T(8,128)} %moment1.1) | copy-start | bytes 1572868
  92.2 15.8 %copy-start.3 = (f32[64,2048]{1,0:T(8,128)S(1)}, f32[64,2048]{1,0:T(8,128)}, u32[]{:S(2)}) copy-start(f32[64,2048]{1,0:T(8,128)} %moment2.1) | copy-start | bytes 1572868
  92.2 9.9 %collective-permute-start.11 = (f16[64,2176]{1,0:T(8,128)(2,1)S(1)}, f16[64,2176]{1,0:T(8,128)(2,1)S(1)}, u32[]{:S(2)}, u32[]{:S(2)}) collective-permute-start(f16[64,2176]{1,0:T(8,128)(2,1)S(1)} %get-tuple-element.39), channel_id=1, source_target_pairs={{0,8},{8,16},{16,24},{24,0},{1,9},{9,17},{17,25},{25,1},{2,10},{10... | collective-permute-start | bytes 835592 | tf_op jit(solution)/shard_map/ppermute | solution.py:171
  93.7 14.2 %collective-permute-start.12 = (f16[64,2176]{1,0:T(8,128)(2,1)S(1)}, f16[64,2176]{1,0:T(8,128)(2,1)S(1)}, u32[]{:S(2)}, u32[]{:S(2)}) collective-permute-start(f16[64,2176]{1,0:T(8,128)(2,1)S(1)} %get-tuple-element.38), channel_id=1, source_target_pairs={{0,16},{8,24},{16,0},{24,8},{1,17},{9,25},{17,1},{25,9},{2,18},{10... | collective-permute-start | bytes 835592 | tf_op jit(solution)/shard_map/ppermute | solution.py:171
  96.5 11.5 %collective-permute-start.13 = (f16[64,2176]{1,0:T(8,128)(2,1)S(1)}, f16[64,2176]{1,0:T(8,128)(2,1)S(1)}, u32[]{:S(2)}, u32[]{:S(2)}) collective-permute-start(f16[64,2176]{1,0:T(8,128)(2,1)S(1)} %get-tuple-element.37), channel_id=1, source_target_pairs={{0,24},{8,0},{16,8},{24,16},{1,25},{9,1},{17,9},{25,17},{2,26},{10... | collective-permute-start | bytes 835592 | tf_op jit(solution)/shard_map/ppermute | solution.py:171
  109.6 16.1 %copy-start.1 = (bf16[2,256,2176]{2,1,0:T(8,128)(2,1)S(1)}, bf16[2,256,2176]{2,1,0:T(8,128)(2,1)}, u32[]{:S(2)}) copy-start(bf16[2,256,2176]{2,1,0:T(8,128)(2,1)} %all-gather.2.cloned.1.call-done.right) | copy-start | bytes 6684676
  109.6 9.0 %collective-permute-start.14 = (f16[64,2176]{1,0:T(8,128)(2,1)S(1)}, f16[64,2176]{1,0:T(8,128)(2,1)S(1)}, u32[]{:S(2)}, u32[]{:S(2)}) collective-permute-start(f16[64,2176]{1,0:T(8,128)(2,1)S(1)} %convert_element_type.43), channel_id=1, source_target_pairs={{0,8},{8,16},{16,24},{24,0},{1,9},{9,17},{17,25},{25,1},{2,10},{10... | collective-permute-start | bytes 835592 | tf_op jit(solution)/shard_map/ppermute | solution.py:171
  111.0 14.5 %collective-permute-start.15 = (f16[64,2176]{1,0:T(8,128)(2,1)S(1)}, f16[64,2176]{1,0:T(8,128)(2,1)S(1)}, u32[]{:S(2)}, u32[]{:S(2)}) collective-permute-start(f16[64,2176]{1,0:T(8,128)(2,1)S(1)} %convert_element_type.43), channel_id=1, source_target_pairs={{0,16},{8,24},{16,0},{24,8},{1,17},{9,25},{17,1},{25,9},{2,18},{10... | collective-permute-start | bytes 835592 | tf_op jit(solution)/shard_map/ppermute | solution.py:171
  113.4 12.2 %collective-permute-start.16 = (f16[64,2176]{1,0:T(8,128)(2,1)S(1)}, f16[64,2176]{1,0:T(8,128)(2,1)S(1)}, u32[]{:S(2)}, u32[]{:S(2)}) collective-permute-start(f16[64,2176]{1,0:T(8,128)(2,1)S(1)} %convert_element_type.43), channel_id=1, source_target_pairs={{0,24},{8,0},{16,8},{24,16},{1,25},{9,1},{17,9},{25,17},{2,26},{10... | collective-permute-start | bytes 835592 | tf_op jit(solution)/shard_map/ppermute | solution.py:171
  126.9 7.2 %collective-permute-start.17 = (f32[264,256]{1,0:T(8,128)S(1)}, f32[264,256]{1,0:T(8,128)S(1)}, u32[]{:S(2)}, u32[]{:S(2)}) collective-permute-start(f32[264,256]{1,0:T(8,128)S(1)} %get-tuple-element.23), channel_id=1, source_target_pairs={{0,4},{4,0},{1,5},{5,1},{2,6},{6,2},{3,7},{7,3},{8,12},{12,8},{9,1... | collective-permute-start | bytes 811016 | tf_op jit(solution)/shard_map/ppermute | solution.py:229
  137.3 34.6 %all-to-all-start.1 = ((f16[32,64,256]{2,1,0:T(8,128)(2,1)}), f16[32,64,256]{2,1,0:T(8,128)(2,1)S(1)}, u32[]{:S(2)}, u32[]{:S(2)}) async-start(f16[32,64,256]{2,1,0:T(8,128)(2,1)} %bitcast.11), calls=%async_computation.1 | async-start | bytes 2097152 | tf_op jit(solution)/shard_map/all_to_all | solution.py:241
  145.6 20.1 %collective-permute-start.18 = (f32[8,256]{1,0:T(8,128)S(1)}, f32[8,256]{1,0:T(8,128)S(1)}, u32[]{:S(2)}, u32[]{:S(2)}) collective-permute-start(f32[8,256]{1,0:T(8,128)S(1)} %get-tuple-element.26), channel_id=1, source_target_pairs={{0,32},{32,64},{64,96},{96,0},{1,33},{33,65},{65,97},{97,1},{2,34}... | collective-permute-start | bytes 24584 | tf_op jit(solution)/shard_map/ppermute | solution.py:171
  147.2 23.4 %collective-permute-start.19 = (f32[8,256]{1,0:T(8,128)S(1)}, f32[8,256]{1,0:T(8,128)S(1)}, u32[]{:S(2)}, u32[]{:S(2)}) collective-permute-start(f32[8,256]{1,0:T(8,128)S(1)} %get-tuple-element.26), channel_id=1, source_target_pairs={{0,64},{32,96},{64,0},{96,32},{1,65},{33,97},{65,1},{97,33},{2,66}... | collective-permute-start | bytes 24584 | tf_op jit(solution)/shard_map/ppermute | solution.py:171
  149.6 21.0 %collective-permute-start.20 = (f32[8,256]{1,0:T(8,128)S(1)}, f32[8,256]{1,0:T(8,128)S(1)}, u32[]{:S(2)}, u32[]{:S(2)}) collective-permute-start(f32[8,256]{1,0:T(8,128)S(1)} %get-tuple-element.26), channel_id=1, source_target_pairs={{0,96},{32,0},{64,32},{96,64},{1,97},{33,1},{65,33},{97,65},{2,98}... | collective-permute-start | bytes 24584 | tf_op jit(solution)/shard_map/ppermute | solution.py:171
Sparse Core Ops, SparseCore 0:
  25.5 59.5 all-gather.1

commit v4 on v3

--- a/solution.py
+++ b/solution.py
@@ -58,17 +58,22 @@
     return jnp.concatenate([value, jnp.broadcast_to(lane, lane.shape[:-1] + (LANES,)).astype(value.dtype)], -1)
 
 
-def call(kernel, out, scratch=(), smem=0, operands=()):
+def call(kernel, out, scratch=(), smem=0, operands=(), loose=0):
     specs = [pl.BlockSpec(memory_space=pltpu.SMEM)] * smem
-    specs += [pl.BlockSpec(memory_space=pltpu.VMEM)] * (len(operands) - smem)
+    specs += [pl.BlockSpec(memory_space=pltpu.VMEM)] * (len(operands) - smem - loose)
+    specs += [pl.BlockSpec(memory_space=pl.ANY)] * loose
     return pl.pallas_call(
         kernel,
-        out_shape=tuple(jax.ShapeDtypeStruct(shape, F32) for shape in out),
+        out_shape=tuple(jax.ShapeDtypeStruct(shape, BF16 if len(shape) == 3 else F32) for shape in out),
         in_specs=specs,
         out_specs=tuple(pl.BlockSpec(memory_space=pltpu.VMEM) for _ in out),
         scratch_shapes=list(scratch),
         compiler_params=pltpu.CompilerParams(vmem_limit_bytes=28 * 1024 * 1024),
     )(*operands)
+
+
+def row_scales(right):
+    return jnp.transpose(right[:, WIDTH:].astype(F32))[0:1, :]
 
 
 def block_starts(place):
@@ -100,9 +105,18 @@
         theirs[s * ROWS:(s + 1) * ROWS, :] = total[pl.ds(pl.multiple_of((2 * x + 1 - l) * ROWS, ROWS), ROWS), :]
 
 
-def right_kernel(mine, theirs, scales, right, message):
-    own_half = mine[...] * scales[0:1, :]
-    other_half = theirs[...] * scales[1:2, :]
+def right_kernel(place, mine, theirs, here, back1, back2, back3, on1, on2, on3, far, message, right, sems):
+    z = place[3]
+    copies = []
+    for index, (block, shift) in enumerate(zip((here, on1, on2, on3, far, back3, back2, back1), range(8))):
+        rows = pl.ds(pl.multiple_of(lax.rem(z + shift, 8) * 32, 32), 32)
+        copies.append(pltpu.make_async_copy(block, right.at[:, rows, :], sems.at[index]))
+    for copy in copies:
+        copy.start()
+    for copy in copies:
+        copy.wait()
+    own_half = mine[...] * row_scales(right.at[0])
+    other_half = theirs[...] * row_scales(right.at[1])
     bound = jnp.sum(jnp.abs(own_half) + jnp.abs(other_half), axis=1, keepdims=True)
     power = exponent(0.125 * bound)
     factor = jnp.exp2(15.0 - power)
@@ -130,7 +144,7 @@
     message[:, WIDTH:] = jnp.broadcast_to(power, (ROWS, LANES))
 
 
-def back_kernel(own, got1, got2, got3, scales, right, mine, theirs, top, high, low):
+def back_kernel(own, got1, got2, got3, right, mine, theirs, top, high, low):
     near, far = right[0, :, :WIDTH], right[1, :, :WIDTH]
     best = jnp.zeros((1, 1), F32) - 200.0
     factors = []
@@ -140,8 +154,8 @@
         factors.append(jnp.exp2(power - 15.0))
         high[s * ROWS:(s + 1) * ROWS, :], low[s * ROWS:(s + 1) * ROWS, :] = split(got[:, :WIDTH])
     factor = jnp.concatenate(factors)
-    mine[...] = (dot(high[...], near, (1, 1)) + dot(low[...], near, (1, 1))) * factor * scales[0:1, :]
-    theirs[:4 * ROWS, :] = (dot(high[...], far, (1, 1)) + dot(low[...], far, (1, 1))) * factor * scales[1:2, :]
+    mine[...] = (dot(high[...], near, (1, 1)) + dot(low[...], near, (1, 1))) * factor * row_scales(right.at[0])
+    theirs[:4 * ROWS, :] = (dot(high[...], far, (1, 1)) + dot(low[...], far, (1, 1))) * factor * row_scales(right.at[1])
     top[...] = jnp.broadcast_to(best, (8, SLICE))
     theirs[4 * ROWS:, :] = jnp.broadcast_to(best, (8, SLICE))
 
@@ -171,6 +185,10 @@
     return lax.ppermute(value, axis, [(i, (i + shift) % 4) for i in range(4)])
 
 
+def around(value, shift):
+    return lax.ppermute(value, ("zh", "zl"), [(i, (i + shift) % 8) for i in range(8)])
+
+
 def ring_gather(value, axes, names):
     size = len(names)
     blocks = [value]
@@ -181,7 +199,7 @@
 
 def body(grad, left_codes, left_scale, right_codes, right_scale, moment1, moment2):
     zh, zl, x, l, h, c = (lax.axis_index(a) for a in AXES)
-    place = jnp.stack([c, 2 * h + l, x]).astype(jnp.int32)
+    place = jnp.stack([c, 2 * h + l, x, 4 * zh + zl]).astype(jnp.int32)
     right = with_lanes(right_codes, right_scale[..., None])
     right = jnp.concatenate([right, lax.ppermute(right, "l", SWAP)])
 
@@ -190,15 +208,19 @@
     got1 = lax.ppermute(jnp.where(l == 0, pieces[0], pieces[1]), AXES, first)
     got2 = lax.ppermute(jnp.where(l == 0, pieces[1], pieces[0]), AXES, second)
 
-    right, got1, got2 = lax.optimization_barrier((right, got1, got2))
-    right = lax.all_gather(right, ("zh", "zl"), axis=1, tiled=True)
     slices = grad.reshape(ROWS, 8, 8, 32).transpose(2, 0, 1, 3).reshape(1, 8, ROWS, SLICE)
     columns = jnp.broadcast_to(slices, (4, 8, ROWS, SLICE)).reshape(32, ROWS, SLICE)
     columns = lax.all_to_all(columns, ("zl", "x", "l"), 0, 0, tiled=True).reshape(WIDTH, SLICE)
 
     chunk = jnp.where(zh == 0, jnp.concatenate([got1, got2]), jnp.concatenate([got2, got1]))
-    left_own = ring_gather(ring_gather(chunk, ("x",), (0, 1, 2, 3)), ("l", "h"), (0, 2, 1, 3))
+    chunk = ring_gather(chunk, ("x",), (0, 1, 2, 3))
+    back1, on1 = around(right, 1), around(right, 7)
+    left_own = ring_gather(chunk, ("l", "h"), (0, 2, 1, 3))
+    back2, on2 = around(back1, 1), around(on1, 7)
+    back3, on3 = around(back2, 1), around(on2, 7)
+    left_own, back3, on3 = lax.optimization_barrier((left_own, back3, on3))
     left_other = lax.ppermute(left_own, "c", SWAP)
+    far = around(back3, 1)
 
     mine, theirs = call(
         left_kernel,
@@ -208,9 +230,13 @@
         (place, left_own, left_other, columns),
     )
     theirs = lax.ppermute(theirs, "l", SWAP)
-    scales = right[:, :, WIDTH].astype(F32)
-    (message,) = call(
-        right_kernel, [(4 * ROWS, WIDTH + LANES)], operands=(mine, theirs, scales, right)
+    message, right = call(
+        right_kernel,
+        [(4 * ROWS, WIDTH + LANES), (2, SLICE, WIDTH + LANES)],
+        [pltpu.SemaphoreType.DMA((8,))],
+        1,
+        (place, mine, theirs, right, back1, back2, back3, on1, on2, on3, far),
+        8,
     )
     got = [shifted(message[s * ROWS:(s + 1) * ROWS].astype(F16), "x", s).astype(F32) for s in range(1, 4)]
     first_new, second_new, message = call(
@@ -224,7 +250,7 @@
         back_kernel,
         [(4 * ROWS, SLICE), (4 * ROWS + 8, SLICE), (8, SLICE)],
         [pltpu.VMEM((4 * ROWS, WIDTH), BF16)] * 2,
-        operands=(message, *got, scales, right),
+        operands=(message, *got, right),
     )
     theirs = lax.ppermute(theirs, "l", SWAP)
     update, top = call(

time: 181 us -> 175 us (0.967)
  starting transfers between devices: 55.6 us -> 69.7 us
  between operations: 14.4 us -> 1.07 us
  waiting for transfers between devices: 88.6 us -> 82.5 us
  Pallas kernels: 8.87 us -> 10.8 us
    ppermute x0 -> x7, waiting for transfers between devices: none -> 28.5 us  [around(): lax.ppermute(value, ('zh', 'zl'), [(i, (i + shift) % 8) for i in range(8)])]
    ppermute x6, waiting for transfers between devices: 19.5 us -> 0.02 us  [ring_gather(): lax.ppermute(value, axes, [(names[i], names[(i + shift) % size]) for i in...]
    ppermute x0 -> x7, starting transfers between devices: none -> 15.5 us  [around(): lax.ppermute(value, ('zh', 'zl'), [(i, (i + shift) % 8) for i in range(8)])]
    all_to_all x1, waiting for transfers between devices: 9.58 us -> 0.01 us  [body(): lax.all_to_all(columns, ('zl', 'x', 'l'), 0, 0, tiled=True)]
    all_gather x1 -> x0, waiting for transfers between devices: 3.45 us -> none  [body(): right = lax.all_gather(right, ('zh', 'zl'), axis=1, tiled=True)]
    ppermute x1, waiting for transfers between devices: 2.47 us -> 0.01 us  [body(): got2 = lax.ppermute(jnp.where(l == 0, pieces[1], pieces[0]), AXES, second)]
    pallas_call x5, Pallas kernels: 8.87 us -> 10.8 us  [call(): pl.pallas_call(kernel, out_shape=tuple((jax.ShapeDtypeStruct(shape, BF16...]
  transfers between devices with their start and end apart: 24 -> 30, of which waited for: 15 -> 14; matrix products, arithmetic and copies ran while one was open for 4% -> 3% of each run, Pallas kernels for 2% -> 2%
where the time goes in v4:
time: 175 us
  waiting for transfers between devices  82.5 us (47%)
  starting transfers between devices  69.7 us (40%)
  Pallas kernels  10.8 us (6%)
  local copies, waits for them, and re-layouts  5.75 us (3%)
  other arithmetic  4.71 us (3%)
    ppermute x9, waiting for transfers between devices, shifted(): return lax.ppermute(value, axis, [(i, (i + shift) % 4) for i in range(4)])  40.6 us
    ppermute x7, waiting for transfers between devices, around(): lax.ppermute(value, ('zh', 'zl'), [(i, (i + shift) % 8) for i in range(8)])  28.5 us
    ppermute x9, starting transfers between devices, shifted(): return lax.ppermute(value, axis, [(i, (i + shift) % 4) for i in range(4)])  16.6 us
    ppermute x7, starting transfers between devices, around(): lax.ppermute(value, ('zh', 'zl'), [(i, (i + shift) % 8) for i in range(8)])  15.5 us
    ppermute x2, waiting for transfers between devices, body(): theirs = lax.ppermute(theirs, 'l', SWAP)  10.9 us
    pallas_call x5, Pallas kernels, call(): pl.pallas_call(kernel, out_shape=tuple((jax.ShapeDtypeStruct(shape, BF16...  10.8 us
    ppermute x6, starting transfers between devices, ring_gather(): lax.ppermute(value, axes, [(names[i], names[(i + shift) % size]) for i in...  10.7 us
    ppermute x1, starting transfers between devices, body(): got1 = lax.ppermute(jnp.where(l == 0, pieces[0], pieces[1]), AXES, first)  8.38 us
  transfers between devices with their start and end apart: 30, of which 14 were waited for; matrix products, arithmetic and copies ran while one was open for 3% of the time, Pallas kernels for 2%

profile of v4, /device:TPU:8, one launch (start us, length us, event | category | flops | bytes accessed | tf_op | source)
XLA Modules:
  0.0 174.5 jit_solution(5209358509485360488)
XLA Ops:
  1.4 0.9 pad_maximum_fusion.2
  2.3 2.3 %collective-permute-start.8 = (bf16[1,32,2176]{2,1,0:T(8,128)(2,1)S(1)}, bf16[1,32,2176]{2,1,0:T(8,128)(2,1)S(1)}, u32[]{:S(2)}, u32[]{:S(2)}) collective-permute-start(bf16[1,32,2176]{2,1,0:T(8,128)(2,1)S(1)} %pad_maximum_fusion.2), channel_id=1, source_target_pairs={{0,4},{4,0},{1,5},{5,1},{2,6},{6,2},{3,7},{7,3},{8,12},{12,8},{9,1... | collective-permute-start | bytes 417800 | tf_op jit(solution)/shard_map/ppermute | solution.py:204
  5.3 0.9 select_bitcast_fusion
  6.2 8.4 %collective-permute-start = (bf16[32,640]{1,0:T(8,128)(2,1)S(1)}, bf16[32,640]{1,0:T(8,128)(2,1)S(1)}, u32[]{:S(2)}, u32[]{:S(2)}) collective-permute-start(bf16[32,640]{1,0:T(8,128)(2,1)S(1)} %get-tuple-element.45), channel_id=1, source_target_pairs={{0,0},{1,32},{2,64},{3,96},{4,128},{5,160},{6,192},{7,224},{8,8},{... | collective-permute-start | bytes 122888 | tf_op jit(solution)/shard_map/ppermute | solution.py:208
  14.7 0.9 pad_maximum_fusion.1.here
  15.6 2.1 %collective-permute-start.9 = (bf16[2,32,2176]{2,1,0:T(8,128)(2,1)S(1)}, bf16[2,32,2176]{2,1,0:T(8,128)(2,1)S(1)}, u32[]{:S(2)}, u32[]{:S(2)}) collective-permute-start(bf16[2,32,2176]{2,1,0:T(8,128)(2,1)S(1)} %pad_maximum_fusion.1.here), channel_id=1, source_target_pairs={{0,32},{32,64},{64,96},{96,128},{128,160},{160,192},{192,224},{224... | collective-permute-start | bytes 835592 | tf_op jit(solution)/shard_map/ppermute | solution.py:189
  17.7 1.2 collective-permute-start.12
  19.0 1.6 collective-permute-start.2
  20.5 2.7 %collective-permute-start.3 = (bf16[64,640]{1,0:T(8,128)(2,1)S(1)}, bf16[64,640]{1,0:T(8,128)(2,1)S(1)}, u32[]{:S(2)}, u32[]{:S(2)}) collective-permute-start(bf16[64,640]{1,0:T(8,128)(2,1)S(1)} %get-tuple-element.40), channel_id=1, source_target_pairs={{0,16},{8,24},{16,0},{24,8},{1,17},{9,25},{17,1},{25,9},{2,18},{10... | collective-permute-start | bytes 245768 | tf_op jit(solution)/shard_map/ppermute | solution.py:196
  23.3 1.4 collective-permute-start.4
  25.2 1.1 broadcast_in_dim.77
  26.3 7.8 %all-to-all-start = ((bf16[32,64,256]{2,1,0:T(8,128)(2,1)}), bf16[32,64,256]{2,1,0:T(8,128)(2,1)}, u32[]{:S(2)}, u32[]{:S(2)}) async-start(bf16[32,64,256]{2,1,0:T(8,128)(2,1)} %bitcast.10), calls=%async_computation | async-start | bytes 2097152 | tf_op jit(solution)/shard_map/all_to_all | solution.py:213
  34.5 2.2 %collective-permute-start.6 = (bf16[256,640]{1,0:T(8,128)(2,1)S(1)}, bf16[256,640]{1,0:T(8,128)(2,1)S(1)}, u32[]{:S(2)}, u32[]{:S(2)}) collective-permute-start(bf16[256,640]{1,0:T(8,128)(2,1)S(1)} %pad_maximum_fusion), channel_id=1, source_target_pairs={{0,2},{4,6},{2,0},{6,4},{1,3},{5,7},{3,1},{7,5},{8,10},{12,14},{10... | collective-permute-start | bytes 983048 | tf_op jit(solution)/shard_map/ppermute | solution.py:196
  36.7 2.5 %collective-permute-start.7 = (bf16[256,640]{1,0:T(8,128)(2,1)S(1)}, bf16[256,640]{1,0:T(8,128)(2,1)S(1)}, u32[]{:S(2)}, u32[]{:S(2)}) collective-permute-start(bf16[256,640]{1,0:T(8,128)(2,1)S(1)} %pad_maximum_fusion), channel_id=1, source_target_pairs={{0,6},{4,0},{2,4},{6,2},{1,7},{5,1},{3,5},{7,3},{8,14},{12,8},{10,... | collective-permute-start | bytes 983048 | tf_op jit(solution)/shard_map/ppermute | solution.py:196
  39.7 2.7 %collective-permute-start.13 = (bf16[2,32,2176]{2,1,0:T(8,128)(2,1)S(1)}, bf16[2,32,2176]{2,1,0:T(8,128)(2,1)S(1)}, u32[]{:S(2)}, u32[]{:S(2)}) collective-permute-start(bf16[2,32,2176]{2,1,0:T(8,128)(2,1)S(1)} %collective-permute-done.12.on1), channel_id=1, source_target_pairs={{0,224},{32,0},{64,32},{96,64},{128,96},{160,128},{192,160},{224,1... | collective-permute-start | bytes 835592 | tf_op jit(solution)/shard_map/ppermute | solution.py:189
  42.5 15.4 %collective-permute-done.10.back2 = bf16[2,32,2176]{2,1,0:T(8,128)(2,1)S(1)} collective-permute-done((bf16[2,32,2176]{2,1,0:T(8,128)(2,1)S(1)}, bf16[2,32,2176]{2,1,0:T(8,128)(2,1)S(1)}, u32[]{:S(2)}, u32[]{:S(2)}) %collective-permute-start.10) | collective-permute-done | bytes 278560 | tf_op jit(solution)/shard_map/ppermute | solution.py:189
  57.8 7.2 %collective-permute-start.11 = (bf16[2,32,2176]{2,1,0:T(8,128)(2,1)S(1)}, bf16[2,32,2176]{2,1,0:T(8,128)(2,1)S(1)}, u32[]{:S(2)}, u32[]{:S(2)}) collective-permute-start(bf16[2,32,2176]{2,1,0:T(8,128)(2,1)S(1)} %collective-permute-done.10.back2), channel_id=1, source_target_pairs={{0,32},{32,64},{64,96},{96,128},{128,160},{160,192},{192,224},{224... | collective-permute-start | bytes 835592 | tf_op jit(solution)/shard_map/ppermute | solution.py:189
  65.2 6.0 %collective-permute-done.11.back3 = bf16[2,32,2176]{2,1,0:T(8,128)(2,1)S(1)} collective-permute-done((bf16[2,32,2176]{2,1,0:T(8,128)(2,1)S(1)}, bf16[2,32,2176]{2,1,0:T(8,128)(2,1)S(1)}, u32[]{:S(2)}, u32[]{:S(2)}) %collective-permute-start.11) | collective-permute-done | bytes 278560 | tf_op jit(solution)/shard_map/ppermute | solution.py:189
  71.2 2.9 %collective-permute-done.14.on3 = bf16[2,32,2176]{2,1,0:T(8,128)(2,1)S(1)} collective-permute-done((bf16[2,32,2176]{2,1,0:T(8,128)(2,1)S(1)}, bf16[2,32,2176]{2,1,0:T(8,128)(2,1)S(1)}, u32[]{:S(2)}, u32[]{:S(2)}) %collective-permute-start.14) | collective-permute-done | bytes 278560 | tf_op jit(solution)/shard_map/ppermute | solution.py:189
  74.9 1.7 collective-permute-start.17
  76.7 1.2 collective-permute-done.15.other
  77.9 2.8 %shard_map.94 = (f32[256,256]{1,0:T(8,128)S(1)}, f32[256,256]{1,0:T(8,128)S(1)}) custom-call(s32[4]{0:T(128)S(1)} %pad_add_fusion.place, bf16[1024,640]{1,0:T(8,128)(2,1)S(1)} %constant_dynamic-update-slice_fusion.own, bf16[1024,640]{1,0:T(8,128)(2,1)S(1)} %collective-permute-done.15.other, bf16[2048,256]{1,0:T(8,128)(2,1)} %bitcast.11.columns), custom_call_target="tpu_custom_call" | custom-call | tf_op jit(solution)/shard_map/pallas_call | solution.py:65
  81.2 4.2 %collective-permute-done.17.far = bf16[2,32,2176]{2,1,0:T(8,128)(2,1)} collective-permute-done((bf16[2,32,2176]{2,1,0:T(8,128)(2,1)}, bf16[2,32,2176]{2,1,0:T(8,128)(2,1)}, u32[]{:S(2)}, u32[]{:S(2)}) %collective-permute-start.17) | collective-permute-done | bytes 278560 | tf_op jit(solution)/shard_map/ppermute | solution.py:189
  85.5 3.7 %collective-permute-done.16.theirs = f32[256,256]{1,0:T(8,128)S(1)} collective-permute-done((f32[256,256]{1,0:T(8,128)S(1)}, f32[256,256]{1,0:T(8,128)S(1)}, u32[]{:S(2)}, u32[]{:S(2)}) %collective-permute-start.16) | collective-permute-done | bytes 262176 | tf_op jit(solution)/shard_map/ppermute | solution.py:232
  89.2 3.1 %shard_map.95 = (f32[256,2176]{1,0:T(8,128)S(1)}, bf16[2,256,2176]{2,1,0:T(8,128)(2,1)S(1)}) custom-call(s32[4]{0:T(128)S(1)} %pad_add_fusion.place, f32[256,256]{1,0:T(8,128)S(1)} %get-tuple-element.19.mine, f32[256,256]{1,0:T(8,128)S(1)} %collective-permute-done.16.theirs, bf16[2,32,2176]{2,1,0:T(8,128)(2,1)S(1)} %pad_maximum_fusion.1.here, ...), custom_call_target="tpu_custom_call" | custom-call | tf_op jit(solution)/shard_map/pallas_call | solution.py:65
  92.7 1.2 collective-permute-start.18
  93.8 3.0 %collective-permute-start.19 = (f16[64,2176]{1,0:T(8,128)(2,1)S(1)}, f16[64,2176]{1,0:T(8,128)(2,1)S(1)}, u32[]{:S(2)}, u32[]{:S(2)}) collective-permute-start(f16[64,2176]{1,0:T(8,128)(2,1)S(1)} %get-tuple-element.42), channel_id=1, source_target_pairs={{0,16},{8,24},{16,0},{24,8},{1,17},{9,25},{17,1},{25,9},{2,18},{10... | collective-permute-start | bytes 835592 | tf_op jit(solution)/shard_map/ppermute | solution.py:185
  96.8 1.5 collective-permute-start.20
  98.3 4.4 %collective-permute-done.18 = f16[64,2176]{1,0:T(8,128)(2,1)S(1)} collective-permute-done((f16[64,2176]{1,0:T(8,128)(2,1)S(1)}, f16[64,2176]{1,0:T(8,128)(2,1)S(1)}, u32[]{:S(2)}, u32[]{:S(2)}) %collective-permute-start.18) | collective-permute-done | bytes 278560 | tf_op jit(solution)/shard_map/ppermute | solution.py:185
  102.8 5.8 %collective-permute-done.19 = f16[64,2176]{1,0:T(8,128)(2,1)S(1)} collective-permute-done((f16[64,2176]{1,0:T(8,128)(2,1)S(1)}, f16[64,2176]{1,0:T(8,128)(2,1)S(1)}, u32[]{:S(2)}, u32[]{:S(2)}) %collective-permute-start.19) | collective-permute-done | bytes 278560 | tf_op jit(solution)/shard_map/ppermute | solution.py:185
  108.7 1.5 shard_map.96
  110.3 1.5 collective-permute-start.21
  111.8 2.4 %collective-permute-start.22 = (f16[64,2176]{1,0:T(8,128)(2,1)S(1)}, f16[64,2176]{1,0:T(8,128)(2,1)S(1)}, u32[]{:S(2)}, u32[]{:S(2)}) collective-permute-start(f16[64,2176]{1,0:T(8,128)(2,1)S(1)} %convert_element_type.36), channel_id=1, source_target_pairs={{0,16},{8,24},{16,0},{24,8},{1,17},{9,25},{17,1},{25,9},{2,18},{10... | collective-permute-start | bytes 835592 | tf_op jit(solution)/shard_map/ppermute | solution.py:185
  114.2 1.5 collective-permute-start.23
  115.7 3.9 %collective-permute-done.21 = f16[64,2176]{1,0:T(8,128)(2,1)S(1)} collective-permute-done((f16[64,2176]{1,0:T(8,128)(2,1)S(1)}, f16[64,2176]{1,0:T(8,128)(2,1)S(1)}, u32[]{:S(2)}, u32[]{:S(2)}) %collective-permute-start.21) | collective-permute-done | bytes 278560 | tf_op jit(solution)/shard_map/ppermute | solution.py:185
  119.6 7.1 %collective-permute-done.22 = f16[64,2176]{1,0:T(8,128)(2,1)S(1)} collective-permute-done((f16[64,2176]{1,0:T(8,128)(2,1)S(1)}, f16[64,2176]{1,0:T(8,128)(2,1)S(1)}, u32[]{:S(2)}, u32[]{:S(2)}) %collective-permute-start.22) | collective-permute-done | bytes 278560 | tf_op jit(solution)/shard_map/ppermute | solution.py:185
  126.8 1.3 shard_map.97
  128.6 7.2 %collective-permute-done.24.theirs = f32[264,256]{1,0:T(8,128)S(1)} collective-permute-done((f32[264,256]{1,0:T(8,128)S(1)}, f32[264,256]{1,0:T(8,128)S(1)}, u32[]{:S(2)}, u32[]{:S(2)}) %collective-permute-start.24) | collective-permute-done | bytes 270368 | tf_op jit(solution)/shard_map/ppermute | solution.py:255
  135.8 2.0 %shard_map.98 = (f32[2048,256]{1,0:T(8,128)S(1)}, f32[8,256]{1,0:T(8,128)S(1)}) custom-call(s32[4]{0:T(128)S(1)} %pad_add_fusion.place, bf16[1024,640]{1,0:T(8,128)(2,1)S(1)} %constant_dynamic-update-slice_fusion.own, bf16[1024,640]{1,0:T(8,128)(2,1)S(1)} %collective-permute-done.15.other, f32[256,256]{1,0:T(8,128)S(1)} %get-tuple-element.26.mine, ...), custom_call_target="tpu_custom_call" | custom-call | tf_op jit(solution)/shard_map/pallas_call | solution.py:65
  137.8 1.2 convert_element_type.40
  138.9 7.5 %all-to-all-start.1 = ((f16[32,64,256]{2,1,0:T(8,128)(2,1)}), f16[32,64,256]{2,1,0:T(8,128)(2,1)S(1)}, u32[]{:S(2)}, u32[]{:S(2)}) async-start(f16[32,64,256]{2,1,0:T(8,128)(2,1)} %bitcast.12), calls=%async_computation.1 | async-start | bytes 2097152 | tf_op jit(solution)/shard_map/all_to_all | solution.py:267
  146.4 1.8 %collective-permute-start.25 = (f32[8,256]{1,0:T(8,128)S(1)}, f32[8,256]{1,0:T(8,128)S(1)}, u32[]{:S(2)}, u32[]{:S(2)}) collective-permute-start(f32[8,256]{1,0:T(8,128)S(1)} %get-tuple-element.30), channel_id=1, source_target_pairs={{0,32},{32,64},{64,96},{96,0},{1,33},{33,65},{65,97},{97,1},{2,34}... | collective-permute-start | bytes 24584 | tf_op jit(solution)/shard_map/ppermute | solution.py:185
  148.2 2.4 %collective-permute-start.26 = (f32[8,256]{1,0:T(8,128)S(1)}, f32[8,256]{1,0:T(8,128)S(1)}, u32[]{:S(2)}, u32[]{:S(2)}) collective-permute-start(f32[8,256]{1,0:T(8,128)S(1)} %get-tuple-element.30), channel_id=1, source_target_pairs={{0,64},{32,96},{64,0},{96,32},{1,65},{33,97},{65,1},{97,33},{2,66}... | collective-permute-start | bytes 24584 | tf_op jit(solution)/shard_map/ppermute | solution.py:185
  150.6 1.4 collective-permute-start.27
  152.1 14.5 %collective-permute-done.25 = f32[8,256]{1,0:T(8,128)S(1)} collective-permute-done((f32[8,256]{1,0:T(8,128)S(1)}, f32[8,256]{1,0:T(8,128)S(1)}, u32[]{:S(2)}, u32[]{:S(2)}) %collective-permute-start.25) | collective-permute-done | bytes 8224 | tf_op jit(solution)/shard_map/ppermute | solution.py:185
  166.5 4.8 %collective-permute-done.26 = f32[8,256]{1,0:T(8,128)S(1)} collective-permute-done((f32[8,256]{1,0:T(8,128)S(1)}, f32[8,256]{1,0:T(8,128)S(1)}, u32[]{:S(2)}, u32[]{:S(2)}) %collective-permute-start.26) | collective-permute-done | bytes 8224 | tf_op jit(solution)/shard_map/ppermute | solution.py:185
  171.5 1.2 all-to-all-done.1
  173.4 1.1 copy.20
  (78 shorter events, 6.2 us)
Async XLA Ops:
  0.6 24.1 %copy-start.10 = (bf16[64,2048]{1,0:T(8,128)(2,1)S(1)}, bf16[64,2048]{1,0:T(8,128)(2,1)}, u32[]{:S(2)}) copy-start(bf16[64,2048]{1,0:T(8,128)(2,1)} %param.7) | copy-start | bytes 786436
  2.3 12.3 %collective-permute-start.8 = (bf16[1,32,2176]{2,1,0:T(8,128)(2,1)S(1)}, bf16[1,32,2176]{2,1,0:T(8,128)(2,1)S(1)}, u32[]{:S(2)}, u32[]{:S(2)}) collective-permute-start(bf16[1,32,2176]{2,1,0:T(8,128)(2,1)S(1)} %pad_maximum_fusion.2), channel_id=1, source_target_pairs={{0,4},{4,0},{1,5},{5,1},{2,6},{6,2},{3,7},{7,3},{8,12},{12,8},{9,1... | collective-permute-start | bytes 417800 | tf_op jit(solution)/shard_map/ppermute | solution.py:204
  6.2 12.7 %collective-permute-start = (bf16[32,640]{1,0:T(8,128)(2,1)S(1)}, bf16[32,640]{1,0:T(8,128)(2,1)S(1)}, u32[]{:S(2)}, u32[]{:S(2)}) collective-permute-start(bf16[32,640]{1,0:T(8,128)(2,1)S(1)} %get-tuple-element.45), channel_id=1, source_target_pairs={{0,0},{1,32},{2,64},{3,96},{4,128},{5,160},{6,192},{7,224},{8,8},{... | collective-permute-start | bytes 122888 | tf_op jit(solution)/shard_map/ppermute | solution.py:208
  14.6 4.4 %collective-permute-start.1 = (bf16[32,640]{1,0:T(8,128)(2,1)S(1)}, bf16[32,640]{1,0:T(8,128)(2,1)S(1)}, u32[]{:S(2)}, u32[]{:S(2)}) collective-permute-start(bf16[32,640]{1,0:T(8,128)(2,1)S(1)} %get-tuple-element.44), channel_id=1, source_target_pairs={{0,128},{1,160},{2,192},{3,224},{4,0},{5,32},{6,64},{7,96},{8,136}... | collective-permute-start | bytes 122888 | tf_op jit(solution)/shard_map/ppermute | solution.py:209
  15.6 23.5 %collective-permute-start.9 = (bf16[2,32,2176]{2,1,0:T(8,128)(2,1)S(1)}, bf16[2,32,2176]{2,1,0:T(8,128)(2,1)S(1)}, u32[]{:S(2)}, u32[]{:S(2)}) collective-permute-start(bf16[2,32,2176]{2,1,0:T(8,128)(2,1)S(1)} %pad_maximum_fusion.1.here), channel_id=1, source_target_pairs={{0,32},{32,64},{64,96},{96,128},{128,160},{160,192},{192,224},{224... | collective-permute-start | bytes 835592 | tf_op jit(solution)/shard_map/ppermute | solution.py:189
  17.7 22.0 %collective-permute-start.12 = (bf16[2,32,2176]{2,1,0:T(8,128)(2,1)S(1)}, bf16[2,32,2176]{2,1,0:T(8,128)(2,1)S(1)}, u32[]{:S(2)}, u32[]{:S(2)}) collective-permute-start(bf16[2,32,2176]{2,1,0:T(8,128)(2,1)S(1)} %pad_maximum_fusion.1.here), channel_id=1, source_target_pairs={{0,224},{32,0},{64,32},{96,64},{128,96},{160,128},{192,160},{224,1... | collective-permute-start | bytes 835592 | tf_op jit(solution)/shard_map/ppermute | solution.py:189
  19.0 15.2 %collective-permute-start.2 = (bf16[64,640]{1,0:T(8,128)(2,1)S(1)}, bf16[64,640]{1,0:T(8,128)(2,1)S(1)}, u32[]{:S(2)}, u32[]{:S(2)}) collective-permute-start(bf16[64,640]{1,0:T(8,128)(2,1)S(1)} %get-tuple-element.40), channel_id=1, source_target_pairs={{0,8},{8,16},{16,24},{24,0},{1,9},{9,17},{17,25},{25,1},{2,10},{10... | collective-permute-start | bytes 245768 | tf_op jit(solution)/shard_map/ppermute | solution.py:196
  20.5 13.6 %collective-permute-start.3 = (bf16[64,640]{1,0:T(8,128)(2,1)S(1)}, bf16[64,640]{1,0:T(8,128)(2,1)S(1)}, u32[]{:S(2)}, u32[]{:S(2)}) collective-permute-start(bf16[64,640]{1,0:T(8,128)(2,1)S(1)} %get-tuple-element.40), channel_id=1, source_target_pairs={{0,16},{8,24},{16,0},{24,8},{1,17},{9,25},{17,1},{25,9},{2,18},{10... | collective-permute-start | bytes 245768 | tf_op jit(solution)/shard_map/ppermute | solution.py:196
  23.3 10.9 %collective-permute-start.4 = (bf16[64,640]{1,0:T(8,128)(2,1)S(1)}, bf16[64,640]{1,0:T(8,128)(2,1)S(1)}, u32[]{:S(2)}, u32[]{:S(2)}) collective-permute-start(bf16[64,640]{1,0:T(8,128)(2,1)S(1)} %get-tuple-element.40), channel_id=1, source_target_pairs={{0,24},{8,0},{16,8},{24,16},{1,25},{9,1},{17,9},{25,17},{2,26},{10... | collective-permute-start | bytes 245768 | tf_op jit(solution)/shard_map/ppermute | solution.py:196
  26.3 50.4 %all-to-all-start = ((bf16[32,64,256]{2,1,0:T(8,128)(2,1)}), bf16[32,64,256]{2,1,0:T(8,128)(2,1)}, u32[]{:S(2)}, u32[]{:S(2)}) async-start(bf16[32,64,256]{2,1,0:T(8,128)(2,1)} %bitcast.10), calls=%async_computation | async-start | bytes 2097152 | tf_op jit(solution)/shard_map/all_to_all | solution.py:213
  34.2 30.8 %collective-permute-start.5 = (bf16[256,640]{1,0:T(8,128)(2,1)S(1)}, bf16[256,640]{1,0:T(8,128)(2,1)S(1)}, u32[]{:S(2)}, u32[]{:S(2)}) collective-permute-start(bf16[256,640]{1,0:T(8,128)(2,1)S(1)} %pad_maximum_fusion), channel_id=1, source_target_pairs={{0,4},{4,2},{2,6},{6,0},{1,5},{5,3},{3,7},{7,1},{8,12},{12,10},{10... | collective-permute-start | bytes 983048 | tf_op jit(solution)/shard_map/ppermute | solution.py:196
  34.5 30.7 %collective-permute-start.6 = (bf16[256,640]{1,0:T(8,128)(2,1)S(1)}, bf16[256,640]{1,0:T(8,128)(2,1)S(1)}, u32[]{:S(2)}, u32[]{:S(2)}) collective-permute-start(bf16[256,640]{1,0:T(8,128)(2,1)S(1)} %pad_maximum_fusion), channel_id=1, source_target_pairs={{0,2},{4,6},{2,0},{6,4},{1,3},{5,7},{3,1},{7,5},{8,10},{12,14},{10... | collective-permute-start | bytes 983048 | tf_op jit(solution)/shard_map/ppermute | solution.py:196
  36.7 28.5 %collective-permute-start.7 = (bf16[256,640]{1,0:T(8,128)(2,1)S(1)}, bf16[256,640]{1,0:T(8,128)(2,1)S(1)}, u32[]{:S(2)}, u32[]{:S(2)}) collective-permute-start(bf16[256,640]{1,0:T(8,128)(2,1)S(1)} %pad_maximum_fusion), channel_id=1, source_target_pairs={{0,6},{4,0},{2,4},{6,2},{1,7},{5,1},{3,5},{7,3},{8,14},{12,8},{10,... | collective-permute-start | bytes 983048 | tf_op jit(solution)/shard_map/ppermute | solution.py:196
  39.2 18.6 %collective-permute-start.10 = (bf16[2,32,2176]{2,1,0:T(8,128)(2,1)S(1)}, bf16[2,32,2176]{2,1,0:T(8,128)(2,1)S(1)}, u32[]{:S(2)}, u32[]{:S(2)}) collective-permute-start(bf16[2,32,2176]{2,1,0:T(8,128)(2,1)S(1)} %collective-permute-done.9.back1), channel_id=1, source_target_pairs={{0,32},{32,64},{64,96},{96,128},{128,160},{160,192},{192,224},{224... | collective-permute-start | bytes 835592 | tf_op jit(solution)/shard_map/ppermute | solution.py:189
  39.7 25.3 %collective-permute-start.13 = (bf16[2,32,2176]{2,1,0:T(8,128)(2,1)S(1)}, bf16[2,32,2176]{2,1,0:T(8,128)(2,1)S(1)}, u32[]{:S(2)}, u32[]{:S(2)}) collective-permute-start(bf16[2,32,2176]{2,1,0:T(8,128)(2,1)S(1)} %collective-permute-done.12.on1), channel_id=1, source_target_pairs={{0,224},{32,0},{64,32},{96,64},{128,96},{160,128},{192,160},{224,1... | collective-permute-start | bytes 835592 | tf_op jit(solution)/shard_map/ppermute | solution.py:189
  57.8 13.4 %copy-start.2 = (bf16[2,32,2176]{2,1,0:T(8,128)(2,1)}, bf16[2,32,2176]{2,1,0:T(8,128)(2,1)S(1)}, u32[]{:S(2)}) copy-start(bf16[2,32,2176]{2,1,0:T(8,128)(2,1)S(1)} %collective-permute-done.10.back2) | copy-start | bytes 835588
  57.8 13.4 %collective-permute-start.11 = (bf16[2,32,2176]{2,1,0:T(8,128)(2,1)S(1)}, bf16[2,32,2176]{2,1,0:T(8,128)(2,1)S(1)}, u32[]{:S(2)}, u32[]{:S(2)}) collective-permute-start(bf16[2,32,2176]{2,1,0:T(8,128)(2,1)S(1)} %collective-permute-done.10.back2), channel_id=1, source_target_pairs={{0,32},{32,64},{64,96},{96,128},{128,160},{160,192},{192,224},{224... | collective-permute-start | bytes 835592 | tf_op jit(solution)/shard_map/ppermute | solution.py:189
  65.0 6.2 %copy-start.4 = (bf16[2,32,2176]{2,1,0:T(8,128)(2,1)}, bf16[2,32,2176]{2,1,0:T(8,128)(2,1)S(1)}, u32[]{:S(2)}) copy-start(bf16[2,32,2176]{2,1,0:T(8,128)(2,1)S(1)} %collective-permute-done.13.on2) | copy-start | bytes 835588
  65.1 9.1 %collective-permute-start.14 = (bf16[2,32,2176]{2,1,0:T(8,128)(2,1)S(1)}, bf16[2,32,2176]{2,1,0:T(8,128)(2,1)S(1)}, u32[]{:S(2)}, u32[]{:S(2)}) collective-permute-start(bf16[2,32,2176]{2,1,0:T(8,128)(2,1)S(1)} %collective-permute-done.13.on2), channel_id=1, source_target_pairs={{0,224},{32,0},{64,32},{96,64},{128,96},{160,128},{192,160},{224,1... | collective-permute-start | bytes 835592 | tf_op jit(solution)/shard_map/ppermute | solution.py:189
  71.2 2.9 %copy-start.6 = (bf16[2,32,2176]{2,1,0:T(8,128)(2,1)}, bf16[2,32,2176]{2,1,0:T(8,128)(2,1)S(1)}, u32[]{:S(2)}) copy-start(bf16[2,32,2176]{2,1,0:T(8,128)(2,1)S(1)} %collective-permute-done.11.back3) | copy-start | bytes 835588
  74.1 0.7 copy-start.8
  74.9 3.0 %collective-permute-start.15 = (bf16[1024,640]{1,0:T(8,128)(2,1)S(1)}, bf16[1024,640]{1,0:T(8,128)(2,1)S(1)}, u32[]{:S(2)}, u32[]{:S(2)}) collective-permute-start(bf16[1024,640]{1,0:T(8,128)(2,1)S(1)} %constant_dynamic-update-slice_fusion.own), channel_id=1, source_target_pairs={{0,1},{1,0},{2,3},{3,2},{4,5},{5,4},{6,7},{7,6},{8,9},{9,8},{10,11... | collective-permute-start | bytes 3932168 | tf_op jit(solution)/shard_map/ppermute | solution.py:222
  74.9 10.6 %collective-permute-start.17 = (bf16[2,32,2176]{2,1,0:T(8,128)(2,1)}, bf16[2,32,2176]{2,1,0:T(8,128)(2,1)}, u32[]{:S(2)}, u32[]{:S(2)}) collective-permute-start(bf16[2,32,2176]{2,1,0:T(8,128)(2,1)} %copy-done.6), channel_id=1, source_target_pairs={{0,32},{32,64},{64,96},{96,128},{128,160},{160,192},{192,224},{224... | collective-permute-start | bytes 835592 | tf_op jit(solution)/shard_map/ppermute | solution.py:189
  77.9 11.3 %copy-start.3 = (bf16[2,32,2176]{2,1,0:T(8,128)(2,1)S(1)}, bf16[2,32,2176]{2,1,0:T(8,128)(2,1)}, u32[]{:S(2)}) copy-start(bf16[2,32,2176]{2,1,0:T(8,128)(2,1)} %copy-done.2) | copy-start | bytes 835588
  77.9 11.3 %copy-start.5 = (bf16[2,32,2176]{2,1,0:T(8,128)(2,1)S(1)}, bf16[2,32,2176]{2,1,0:T(8,128)(2,1)}, u32[]{:S(2)}) copy-start(bf16[2,32,2176]{2,1,0:T(8,128)(2,1)} %copy-done.4) | copy-start | bytes 835588
  77.9 11.3 %copy-start.7 = (bf16[2,32,2176]{2,1,0:T(8,128)(2,1)S(1)}, bf16[2,32,2176]{2,1,0:T(8,128)(2,1)}, u32[]{:S(2)}) copy-start(bf16[2,32,2176]{2,1,0:T(8,128)(2,1)} %copy-done.6) | copy-start | bytes 835588
  77.9 11.3 %copy-start.9 = (bf16[2,32,2176]{2,1,0:T(8,128)(2,1)S(1)}, bf16[2,32,2176]{2,1,0:T(8,128)(2,1)}, u32[]{:S(2)}) copy-start(bf16[2,32,2176]{2,1,0:T(8,128)(2,1)} %copy-done.8) | copy-start | bytes 835588
  80.8 8.4 %collective-permute-start.16 = (f32[256,256]{1,0:T(8,128)S(1)}, f32[256,256]{1,0:T(8,128)S(1)}, u32[]{:S(2)}, u32[]{:S(2)}) collective-permute-start(f32[256,256]{1,0:T(8,128)S(1)} %get-tuple-element.20), channel_id=1, source_target_pairs={{0,4},{4,0},{1,5},{5,1},{2,6},{6,2},{3,7},{7,3},{8,12},{12,8},{9,1... | collective-permute-start | bytes 786440 | tf_op jit(solution)/shard_map/ppermute | solution.py:232
  92.7 16.1 %copy-start = (f32[64,2048]{1,0:T(8,128)S(1)}, f32[64,2048]{1,0:T(8,128)}, u32[]{:S(2)}) copy-start(f32[64,2048]{1,0:T(8,128)} %moment1.1) | copy-start | bytes 1572868
  92.7 16.1 %copy-start.1 = (f32[64,2048]{1,0:T(8,128)S(1)}, f32[64,2048]{1,0:T(8,128)}, u32[]{:S(2)}) copy-start(f32[64,2048]{1,0:T(8,128)} %moment2.1) | copy-start | bytes 1572868
  92.7 10.1 %collective-permute-start.18 = (f16[64,2176]{1,0:T(8,128)(2,1)S(1)}, f16[64,2176]{1,0:T(8,128)(2,1)S(1)}, u32[]{:S(2)}, u32[]{:S(2)}) collective-permute-start(f16[64,2176]{1,0:T(8,128)(2,1)S(1)} %get-tuple-element.43), channel_id=1, source_target_pairs={{0,8},{8,16},{16,24},{24,0},{1,9},{9,17},{17,25},{25,1},{2,10},{10... | collective-permute-start | bytes 835592 | tf_op jit(solution)/shard_map/ppermute | solution.py:185
  93.8 14.8 %collective-permute-start.19 = (f16[64,2176]{1,0:T(8,128)(2,1)S(1)}, f16[64,2176]{1,0:T(8,128)(2,1)S(1)}, u32[]{:S(2)}, u32[]{:S(2)}) collective-permute-start(f16[64,2176]{1,0:T(8,128)(2,1)S(1)} %get-tuple-element.42), channel_id=1, source_target_pairs={{0,16},{8,24},{16,0},{24,8},{1,17},{9,25},{17,1},{25,9},{2,18},{10... | collective-permute-start | bytes 835592 | tf_op jit(solution)/shard_map/ppermute | solution.py:185
  96.8 11.9 %collective-permute-start.20 = (f16[64,2176]{1,0:T(8,128)(2,1)S(1)}, f16[64,2176]{1,0:T(8,128)(2,1)S(1)}, u32[]{:S(2)}, u32[]{:S(2)}) collective-permute-start(f16[64,2176]{1,0:T(8,128)(2,1)S(1)} %get-tuple-element.41), channel_id=1, source_target_pairs={{0,24},{8,0},{16,8},{24,16},{1,25},{9,1},{17,9},{25,17},{2,26},{10... | collective-permute-start | bytes 835592 | tf_op jit(solution)/shard_map/ppermute | solution.py:185
  110.3 9.3 %collective-permute-start.21 = (f16[64,2176]{1,0:T(8,128)(2,1)S(1)}, f16[64,2176]{1,0:T(8,128)(2,1)S(1)}, u32[]{:S(2)}, u32[]{:S(2)}) collective-permute-start(f16[64,2176]{1,0:T(8,128)(2,1)S(1)} %convert_element_type.36), channel_id=1, source_target_pairs={{0,8},{8,16},{16,24},{24,0},{1,9},{9,17},{17,25},{25,1},{2,10},{10... | collective-permute-start | bytes 835592 | tf_op jit(solution)/shard_map/ppermute | solution.py:185
  111.8 14.9 %collective-permute-start.22 = (f16[64,2176]{1,0:T(8,128)(2,1)S(1)}, f16[64,2176]{1,0:T(8,128)(2,1)S(1)}, u32[]{:S(2)}, u32[]{:S(2)}) collective-permute-start(f16[64,2176]{1,0:T(8,128)(2,1)S(1)} %convert_element_type.36), channel_id=1, source_target_pairs={{0,16},{8,24},{16,0},{24,8},{1,17},{9,25},{17,1},{25,9},{2,18},{10... | collective-permute-start | bytes 835592 | tf_op jit(solution)/shard_map/ppermute | solution.py:185
  114.2 12.6 %collective-permute-start.23 = (f16[64,2176]{1,0:T(8,128)(2,1)S(1)}, f16[64,2176]{1,0:T(8,128)(2,1)S(1)}, u32[]{:S(2)}, u32[]{:S(2)}) collective-permute-start(f16[64,2176]{1,0:T(8,128)(2,1)S(1)} %convert_element_type.36), channel_id=1, source_target_pairs={{0,24},{8,0},{16,8},{24,16},{1,25},{9,1},{17,9},{25,17},{2,26},{10... | collective-permute-start | bytes 835592 | tf_op jit(solution)/shard_map/ppermute | solution.py:185
  128.1 7.6 %collective-permute-start.24 = (f32[264,256]{1,0:T(8,128)S(1)}, f32[264,256]{1,0:T(8,128)S(1)}, u32[]{:S(2)}, u32[]{:S(2)}) collective-permute-start(f32[264,256]{1,0:T(8,128)S(1)} %get-tuple-element.27), channel_id=1, source_target_pairs={{0,4},{4,0},{1,5},{5,1},{2,6},{6,2},{3,7},{7,3},{8,12},{12,8},{9,1... | collective-permute-start | bytes 811016 | tf_op jit(solution)/shard_map/ppermute | solution.py:255
  138.9 33.8 %all-to-all-start.1 = ((f16[32,64,256]{2,1,0:T(8,128)(2,1)}), f16[32,64,256]{2,1,0:T(8,128)(2,1)S(1)}, u32[]{:S(2)}, u32[]{:S(2)}) async-start(f16[32,64,256]{2,1,0:T(8,128)(2,1)} %bitcast.12), calls=%async_computation.1 | async-start | bytes 2097152 | tf_op jit(solution)/shard_map/all_to_all | solution.py:267
  146.4 20.1 %collective-permute-start.25 = (f32[8,256]{1,0:T(8,128)S(1)}, f32[8,256]{1,0:T(8,128)S(1)}, u32[]{:S(2)}, u32[]{:S(2)}) collective-permute-start(f32[8,256]{1,0:T(8,128)S(1)} %get-tuple-element.30), channel_id=1, source_target_pairs={{0,32},{32,64},{64,96},{96,0},{1,33},{33,65},{65,97},{97,1},{2,34}... | collective-permute-start | bytes 24584 | tf_op jit(solution)/shard_map/ppermute | solution.py:185
  148.2 23.2 %collective-permute-start.26 = (f32[8,256]{1,0:T(8,128)S(1)}, f32[8,256]{1,0:T(8,128)S(1)}, u32[]{:S(2)}, u32[]{:S(2)}) collective-permute-start(f32[8,256]{1,0:T(8,128)S(1)} %get-tuple-element.30), channel_id=1, source_target_pairs={{0,64},{32,96},{64,0},{96,32},{1,65},{33,97},{65,1},{97,33},{2,66}... | collective-permute-start | bytes 24584 | tf_op jit(solution)/shard_map/ppermute | solution.py:185
  150.6 20.8 %collective-permute-start.27 = (f32[8,256]{1,0:T(8,128)S(1)}, f32[8,256]{1,0:T(8,128)S(1)}, u32[]{:S(2)}, u32[]{:S(2)}) collective-permute-start(f32[8,256]{1,0:T(8,128)S(1)} %get-tuple-element.30), channel_id=1, source_target_pairs={{0,96},{32,0},{64,32},{96,64},{1,97},{33,1},{65,33},{97,65},{2,98}... | collective-permute-start | bytes 24584 | tf_op jit(solution)/shard_map/ppermute | solution.py:185

commit v5 on v4

--- a/solution.py
+++ b/solution.py
@@ -105,7 +105,7 @@
         theirs[s * ROWS:(s + 1) * ROWS, :] = total[pl.ds(pl.multiple_of((2 * x + 1 - l) * ROWS, ROWS), ROWS), :]
 
 
-def right_kernel(place, mine, theirs, here, back1, back2, back3, on1, on2, on3, far, message, right, sems):
+def order_kernel(place, here, back1, back2, back3, on1, on2, on3, far, right, sems):
     z = place[3]
     copies = []
     for index, (block, shift) in enumerate(zip((here, on1, on2, on3, far, back3, back2, back1), range(8))):
@@ -115,6 +115,9 @@
         copy.start()
     for copy in copies:
         copy.wait()
+
+
+def right_kernel(mine, theirs, right, message):
     own_half = mine[...] * row_scales(right.at[0])
     other_half = theirs[...] * row_scales(right.at[1])
     bound = jnp.sum(jnp.abs(own_half) + jnp.abs(other_half), axis=1, keepdims=True)
@@ -230,14 +233,15 @@
         (place, left_own, left_other, columns),
     )
     theirs = lax.ppermute(theirs, "l", SWAP)
-    message, right = call(
-        right_kernel,
-        [(4 * ROWS, WIDTH + LANES), (2, SLICE, WIDTH + LANES)],
+    (right,) = call(
+        order_kernel,
+        [(2, SLICE, WIDTH + LANES)],
         [pltpu.SemaphoreType.DMA((8,))],
         1,
-        (place, mine, theirs, right, back1, back2, back3, on1, on2, on3, far),
+        (place, right, back1, back2, back3, on1, on2, on3, far),
         8,
     )
+    (message,) = call(right_kernel, [(4 * ROWS, WIDTH + LANES)], operands=(mine, theirs, right))
     got = [shifted(message[s * ROWS:(s + 1) * ROWS].astype(F16), "x", s).astype(F32) for s in range(1, 4)]
     first_new, second_new, message = call(
         moment_kernel,

time: 175 us -> 173 us (0.989)
  waiting for transfers between devices: 82.5 us -> 80.7 us
    pallas_call x5 -> x6, Pallas kernels: 10.8 us -> 10.8 us  [call(): pl.pallas_call(kernel, out_shape=tuple((jax.ShapeDtypeStruct(shape, BF16...]
  transfers between devices with their start and end apart: 30 -> 30, of which waited for: 14 -> 14; matrix products, arithmetic and copies ran while one was open for 3% -> 3% of each run, Pallas kernels for 2% -> 3%
where the time goes in v5:
time: 173 us
  waiting for transfers between devices  80.7 us (47%)
  starting transfers between devices  69.7 us (40%)
  Pallas kernels  10.8 us (6%)
  local copies, waits for them, and re-layouts  5.74 us (3%)
  other arithmetic  4.72 us (3%)
    ppermute x9, waiting for transfers between devices, shifted(): return lax.ppermute(value, axis, [(i, (i + shift) % 4) for i in range(4)])  40.6 us
    ppermute x7, waiting for transfers between devices, around(): lax.ppermute(value, ('zh', 'zl'), [(i, (i + shift) % 8) for i in range(8)])  28.5 us
    ppermute x9, starting transfers between devices, shifted(): return lax.ppermute(value, axis, [(i, (i + shift) % 4) for i in range(4)])  16.6 us
    ppermute x7, starting transfers between devices, around(): lax.ppermute(value, ('zh', 'zl'), [(i, (i + shift) % 8) for i in range(8)])  15.5 us
    pallas_call x6, Pallas kernels, call(): pl.pallas_call(kernel, out_shape=tuple((jax.ShapeDtypeStruct(shape, BF16...  10.8 us
    ppermute x6, starting transfers between devices, ring_gather(): lax.ppermute(value, axes, [(names[i], names[(i + shift) % size]) for i in...  10.7 us
    ppermute x2, waiting for transfers between devices, body(): theirs = lax.ppermute(theirs, 'l', SWAP)  9.15 us
    ppermute x1, starting transfers between devices, body(): got1 = lax.ppermute(jnp.where(l == 0, pieces[0], pieces[1]), AXES, first)  8.38 us
  transfers between devices with their start and end apart: 30, of which 14 were waited for; matrix products, arithmetic and copies ran while one was open for 3% of the time, Pallas kernels for 3%

profile of v5, /device:TPU:8, one launch (start us, length us, event | category | flops | bytes accessed | tf_op | source)
XLA Modules:
  0.0 172.7 jit_solution(9653109240203572767)
XLA Ops:
  1.4 0.9 pad_maximum_fusion.2
  2.3 2.3 %collective-permute-start.8 = (bf16[1,32,2176]{2,1,0:T(8,128)(2,1)S(1)}, bf16[1,32,2176]{2,1,0:T(8,128)(2,1)S(1)}, u32[]{:S(2)}, u32[]{:S(2)}) collective-permute-start(bf16[1,32,2176]{2,1,0:T(8,128)(2,1)S(1)} %pad_maximum_fusion.2), channel_id=1, source_target_pairs={{0,4},{4,0},{1,5},{5,1},{2,6},{6,2},{3,7},{7,3},{8,12},{12,8},{9,1... | collective-permute-start | bytes 417800 | tf_op jit(solution)/shard_map/ppermute | solution.py:207
  6.2 8.4 %collective-permute-start = (bf16[32,640]{1,0:T(8,128)(2,1)S(1)}, bf16[32,640]{1,0:T(8,128)(2,1)S(1)}, u32[]{:S(2)}, u32[]{:S(2)}) collective-permute-start(bf16[32,640]{1,0:T(8,128)(2,1)S(1)} %get-tuple-element.41), channel_id=1, source_target_pairs={{0,0},{1,32},{2,64},{3,96},{4,128},{5,160},{6,192},{7,224},{8,8},{... | collective-permute-start | bytes 122888 | tf_op jit(solution)/shard_map/ppermute | solution.py:211
  14.7 0.9 pad_maximum_fusion.1.here
  15.6 2.1 %collective-permute-start.9 = (bf16[2,32,2176]{2,1,0:T(8,128)(2,1)S(1)}, bf16[2,32,2176]{2,1,0:T(8,128)(2,1)S(1)}, u32[]{:S(2)}, u32[]{:S(2)}) collective-permute-start(bf16[2,32,2176]{2,1,0:T(8,128)(2,1)S(1)} %pad_maximum_fusion.1.here), channel_id=1, source_target_pairs={{0,32},{32,64},{64,96},{96,128},{128,160},{160,192},{192,224},{224... | collective-permute-start | bytes 835592 | tf_op jit(solution)/shard_map/ppermute | solution.py:192
  17.7 1.2 collective-permute-start.12
  19.0 1.6 collective-permute-start.2
  20.5 2.7 %collective-permute-start.3 = (bf16[64,640]{1,0:T(8,128)(2,1)S(1)}, bf16[64,640]{1,0:T(8,128)(2,1)S(1)}, u32[]{:S(2)}, u32[]{:S(2)}) collective-permute-start(bf16[64,640]{1,0:T(8,128)(2,1)S(1)} %get-tuple-element.36), channel_id=1, source_target_pairs={{0,16},{8,24},{16,0},{24,8},{1,17},{9,25},{17,1},{25,9},{2,18},{10... | collective-permute-start | bytes 245768 | tf_op jit(solution)/shard_map/ppermute | solution.py:199
  23.3 1.4 collective-permute-start.4
  25.2 1.1 broadcast_in_dim.77
  26.3 7.8 %all-to-all-start = ((bf16[32,64,256]{2,1,0:T(8,128)(2,1)}), bf16[32,64,256]{2,1,0:T(8,128)(2,1)}, u32[]{:S(2)}, u32[]{:S(2)}) async-start(bf16[32,64,256]{2,1,0:T(8,128)(2,1)} %bitcast.10), calls=%async_computation | async-start | bytes 2097152 | tf_op jit(solution)/shard_map/all_to_all | solution.py:216
  34.5 2.2 %collective-permute-start.6 = (bf16[256,640]{1,0:T(8,128)(2,1)S(1)}, bf16[256,640]{1,0:T(8,128)(2,1)S(1)}, u32[]{:S(2)}, u32[]{:S(2)}) collective-permute-start(bf16[256,640]{1,0:T(8,128)(2,1)S(1)} %pad_maximum_fusion), channel_id=1, source_target_pairs={{0,2},{4,6},{2,0},{6,4},{1,3},{5,7},{3,1},{7,5},{8,10},{12,14},{10... | collective-permute-start | bytes 983048 | tf_op jit(solution)/shard_map/ppermute | solution.py:199
  36.7 2.5 %collective-permute-start.7 = (bf16[256,640]{1,0:T(8,128)(2,1)S(1)}, bf16[256,640]{1,0:T(8,128)(2,1)S(1)}, u32[]{:S(2)}, u32[]{:S(2)}) collective-permute-start(bf16[256,640]{1,0:T(8,128)(2,1)S(1)} %pad_maximum_fusion), channel_id=1, source_target_pairs={{0,6},{4,0},{2,4},{6,2},{1,7},{5,1},{3,5},{7,3},{8,14},{12,8},{10,... | collective-permute-start | bytes 983048 | tf_op jit(solution)/shard_map/ppermute | solution.py:199
  39.7 2.7 %collective-permute-start.13 = (bf16[2,32,2176]{2,1,0:T(8,128)(2,1)S(1)}, bf16[2,32,2176]{2,1,0:T(8,128)(2,1)S(1)}, u32[]{:S(2)}, u32[]{:S(2)}) collective-permute-start(bf16[2,32,2176]{2,1,0:T(8,128)(2,1)S(1)} %collective-permute-done.12.on1), channel_id=1, source_target_pairs={{0,224},{32,0},{64,32},{96,64},{128,96},{160,128},{192,160},{224,1... | collective-permute-start | bytes 835592 | tf_op jit(solution)/shard_map/ppermute | solution.py:192
  42.4 15.4 %collective-permute-done.10.back2 = bf16[2,32,2176]{2,1,0:T(8,128)(2,1)S(1)} collective-permute-done((bf16[2,32,2176]{2,1,0:T(8,128)(2,1)S(1)}, bf16[2,32,2176]{2,1,0:T(8,128)(2,1)S(1)}, u32[]{:S(2)}, u32[]{:S(2)}) %collective-permute-start.10) | collective-permute-done | bytes 278560 | tf_op jit(solution)/shard_map/ppermute | solution.py:192
  57.8 7.2 %collective-permute-start.11 = (bf16[2,32,2176]{2,1,0:T(8,128)(2,1)S(1)}, bf16[2,32,2176]{2,1,0:T(8,128)(2,1)S(1)}, u32[]{:S(2)}, u32[]{:S(2)}) collective-permute-start(bf16[2,32,2176]{2,1,0:T(8,128)(2,1)S(1)} %collective-permute-done.10.back2), channel_id=1, source_target_pairs={{0,32},{32,64},{64,96},{96,128},{128,160},{160,192},{192,224},{224... | collective-permute-start | bytes 835592 | tf_op jit(solution)/shard_map/ppermute | solution.py:192
  65.2 6.0 %collective-permute-done.11.back3 = bf16[2,32,2176]{2,1,0:T(8,128)(2,1)S(1)} collective-permute-done((bf16[2,32,2176]{2,1,0:T(8,128)(2,1)S(1)}, bf16[2,32,2176]{2,1,0:T(8,128)(2,1)S(1)}, u32[]{:S(2)}, u32[]{:S(2)}) %collective-permute-start.11) | collective-permute-done | bytes 278560 | tf_op jit(solution)/shard_map/ppermute | solution.py:192
  71.2 2.9 %collective-permute-done.14.on3 = bf16[2,32,2176]{2,1,0:T(8,128)(2,1)S(1)} collective-permute-done((bf16[2,32,2176]{2,1,0:T(8,128)(2,1)S(1)}, bf16[2,32,2176]{2,1,0:T(8,128)(2,1)S(1)}, u32[]{:S(2)}, u32[]{:S(2)}) %collective-permute-start.14) | collective-permute-done | bytes 278560 | tf_op jit(solution)/shard_map/ppermute | solution.py:192
  74.9 1.7 %collective-permute-start.17 = (bf16[2,32,2176]{2,1,0:T(8,128)(2,1)}, bf16[2,32,2176]{2,1,0:T(8,128)(2,1)}, u32[]{:S(2)}, u32[]{:S(2)}) collective-permute-start(bf16[2,32,2176]{2,1,0:T(8,128)(2,1)} %copy-done.6), channel_id=1, source_target_pairs={{0,32},{32,64},{64,96},{96,128},{128,160},{160,192},{192,224},{224... | collective-permute-start | bytes 835592 | tf_op jit(solution)/shard_map/ppermute | solution.py:192
  76.7 1.2 collective-permute-done.15.other
  77.9 2.8 %shard_map.94 = (f32[256,256]{1,0:T(8,128)S(1)}, f32[256,256]{1,0:T(8,128)S(1)}) custom-call(s32[4]{0:T(128)S(1)} %pad_add_fusion.place, bf16[1024,640]{1,0:T(8,128)(2,1)S(1)} %constant_dynamic-update-slice_fusion.own, bf16[1024,640]{1,0:T(8,128)(2,1)S(1)} %collective-permute-done.15.other, bf16[2048,256]{1,0:T(8,128)(2,1)} %bitcast.11.columns), custom_call_target="tpu_custom_call" | custom-call | tf_op jit(solution)/shard_map/pallas_call | solution.py:65
  81.2 4.2 %collective-permute-done.17.far = bf16[2,32,2176]{2,1,0:T(8,128)(2,1)} collective-permute-done((bf16[2,32,2176]{2,1,0:T(8,128)(2,1)}, bf16[2,32,2176]{2,1,0:T(8,128)(2,1)}, u32[]{:S(2)}, u32[]{:S(2)}) %collective-permute-start.17) | collective-permute-done | bytes 278560 | tf_op jit(solution)/shard_map/ppermute | solution.py:192
  85.5 1.7 shard_map.95.right
  87.2 2.0 %collective-permute-done.16.theirs = f32[256,256]{1,0:T(8,128)S(1)} collective-permute-done((f32[256,256]{1,0:T(8,128)S(1)}, f32[256,256]{1,0:T(8,128)S(1)}, u32[]{:S(2)}, u32[]{:S(2)}) %collective-permute-start.16) | collective-permute-done | bytes 262176 | tf_op jit(solution)/shard_map/ppermute | solution.py:235
  89.2 1.4 shard_map.96.own
  90.9 1.2 collective-permute-start.18
  92.1 3.0 %collective-permute-start.19 = (f16[64,2176]{1,0:T(8,128)(2,1)S(1)}, f16[64,2176]{1,0:T(8,128)(2,1)S(1)}, u32[]{:S(2)}, u32[]{:S(2)}) collective-permute-start(f16[64,2176]{1,0:T(8,128)(2,1)S(1)} %get-tuple-element.38), channel_id=1, source_target_pairs={{0,16},{8,24},{16,0},{24,8},{1,17},{9,25},{17,1},{25,9},{2,18},{10... | collective-permute-start | bytes 835592 | tf_op jit(solution)/shard_map/ppermute | solution.py:188
  95.0 1.5 collective-permute-start.20
  96.5 4.4 %collective-permute-done.18 = f16[64,2176]{1,0:T(8,128)(2,1)S(1)} collective-permute-done((f16[64,2176]{1,0:T(8,128)(2,1)S(1)}, f16[64,2176]{1,0:T(8,128)(2,1)S(1)}, u32[]{:S(2)}, u32[]{:S(2)}) %collective-permute-start.18) | collective-permute-done | bytes 278560 | tf_op jit(solution)/shard_map/ppermute | solution.py:188
  101.0 5.8 %collective-permute-done.19 = f16[64,2176]{1,0:T(8,128)(2,1)S(1)} collective-permute-done((f16[64,2176]{1,0:T(8,128)(2,1)S(1)}, f16[64,2176]{1,0:T(8,128)(2,1)S(1)}, u32[]{:S(2)}, u32[]{:S(2)}) %collective-permute-start.19) | collective-permute-done | bytes 278560 | tf_op jit(solution)/shard_map/ppermute | solution.py:188
  107.0 1.5 shard_map.97
  108.5 1.5 collective-permute-start.21
  110.0 2.4 %collective-permute-start.22 = (f16[64,2176]{1,0:T(8,128)(2,1)S(1)}, f16[64,2176]{1,0:T(8,128)(2,1)S(1)}, u32[]{:S(2)}, u32[]{:S(2)}) collective-permute-start(f16[64,2176]{1,0:T(8,128)(2,1)S(1)} %convert_element_type.36), channel_id=1, source_target_pairs={{0,16},{8,24},{16,0},{24,8},{1,17},{9,25},{17,1},{25,9},{2,18},{10... | collective-permute-start | bytes 835592 | tf_op jit(solution)/shard_map/ppermute | solution.py:188
  112.4 1.5 collective-permute-start.23
  113.9 3.9 %collective-permute-done.21 = f16[64,2176]{1,0:T(8,128)(2,1)S(1)} collective-permute-done((f16[64,2176]{1,0:T(8,128)(2,1)S(1)}, f16[64,2176]{1,0:T(8,128)(2,1)S(1)}, u32[]{:S(2)}, u32[]{:S(2)}) %collective-permute-start.21) | collective-permute-done | bytes 278560 | tf_op jit(solution)/shard_map/ppermute | solution.py:188
  117.9 7.1 %collective-permute-done.22 = f16[64,2176]{1,0:T(8,128)(2,1)S(1)} collective-permute-done((f16[64,2176]{1,0:T(8,128)(2,1)S(1)}, f16[64,2176]{1,0:T(8,128)(2,1)S(1)}, u32[]{:S(2)}, u32[]{:S(2)}) %collective-permute-start.22) | collective-permute-done | bytes 278560 | tf_op jit(solution)/shard_map/ppermute | solution.py:188
  125.1 1.3 shard_map.98
  126.8 7.2 %collective-permute-done.24.theirs = f32[264,256]{1,0:T(8,128)S(1)} collective-permute-done((f32[264,256]{1,0:T(8,128)S(1)}, f32[264,256]{1,0:T(8,128)S(1)}, u32[]{:S(2)}, u32[]{:S(2)}) %collective-permute-start.24) | collective-permute-done | bytes 270368 | tf_op jit(solution)/shard_map/ppermute | solution.py:259
  134.0 2.0 %shard_map.99 = (f32[2048,256]{1,0:T(8,128)S(1)}, f32[8,256]{1,0:T(8,128)S(1)}) custom-call(s32[4]{0:T(128)S(1)} %pad_add_fusion.place, bf16[1024,640]{1,0:T(8,128)(2,1)S(1)} %constant_dynamic-update-slice_fusion.own, bf16[1024,640]{1,0:T(8,128)(2,1)S(1)} %collective-permute-done.15.other, f32[256,256]{1,0:T(8,128)S(1)} %get-tuple-element.22.mine, ...), custom_call_target="tpu_custom_call" | custom-call | tf_op jit(solution)/shard_map/pallas_call | solution.py:65
  136.0 1.2 convert_element_type.40
  137.2 7.4 %all-to-all-start.1 = ((f16[32,64,256]{2,1,0:T(8,128)(2,1)}), f16[32,64,256]{2,1,0:T(8,128)(2,1)S(1)}, u32[]{:S(2)}, u32[]{:S(2)}) async-start(f16[32,64,256]{2,1,0:T(8,128)(2,1)} %bitcast.12), calls=%async_computation.1 | async-start | bytes 2097152 | tf_op jit(solution)/shard_map/all_to_all | solution.py:271
  144.7 1.8 %collective-permute-start.25 = (f32[8,256]{1,0:T(8,128)S(1)}, f32[8,256]{1,0:T(8,128)S(1)}, u32[]{:S(2)}, u32[]{:S(2)}) collective-permute-start(f32[8,256]{1,0:T(8,128)S(1)} %get-tuple-element.26), channel_id=1, source_target_pairs={{0,32},{32,64},{64,96},{96,0},{1,33},{33,65},{65,97},{97,1},{2,34}... | collective-permute-start | bytes 24584 | tf_op jit(solution)/shard_map/ppermute | solution.py:188
  146.4 2.4 %collective-permute-start.26 = (f32[8,256]{1,0:T(8,128)S(1)}, f32[8,256]{1,0:T(8,128)S(1)}, u32[]{:S(2)}, u32[]{:S(2)}) collective-permute-start(f32[8,256]{1,0:T(8,128)S(1)} %get-tuple-element.26), channel_id=1, source_target_pairs={{0,64},{32,96},{64,0},{96,32},{1,65},{33,97},{65,1},{97,33},{2,66}... | collective-permute-start | bytes 24584 | tf_op jit(solution)/shard_map/ppermute | solution.py:188
  148.8 1.4 collective-permute-start.27
  150.3 14.5 %collective-permute-done.25 = f32[8,256]{1,0:T(8,128)S(1)} collective-permute-done((f32[8,256]{1,0:T(8,128)S(1)}, f32[8,256]{1,0:T(8,128)S(1)}, u32[]{:S(2)}, u32[]{:S(2)}) %collective-permute-start.25) | collective-permute-done | bytes 8224 | tf_op jit(solution)/shard_map/ppermute | solution.py:188
  164.8 4.8 %collective-permute-done.26 = f32[8,256]{1,0:T(8,128)S(1)} collective-permute-done((f32[8,256]{1,0:T(8,128)S(1)}, f32[8,256]{1,0:T(8,128)S(1)}, u32[]{:S(2)}, u32[]{:S(2)}) %collective-permute-start.26) | collective-permute-done | bytes 8224 | tf_op jit(solution)/shard_map/ppermute | solution.py:188
  169.7 1.2 all-to-all-done.1
  171.6 1.1 copy.20
  (79 shorter events, 7.1 us)
Async XLA Ops:
  0.6 24.1 %copy-start.10 = (bf16[64,2048]{1,0:T(8,128)(2,1)S(1)}, bf16[64,2048]{1,0:T(8,128)(2,1)}, u32[]{:S(2)}) copy-start(bf16[64,2048]{1,0:T(8,128)(2,1)} %param.7) | copy-start | bytes 786436
  2.3 12.3 %collective-permute-start.8 = (bf16[1,32,2176]{2,1,0:T(8,128)(2,1)S(1)}, bf16[1,32,2176]{2,1,0:T(8,128)(2,1)S(1)}, u32[]{:S(2)}, u32[]{:S(2)}) collective-permute-start(bf16[1,32,2176]{2,1,0:T(8,128)(2,1)S(1)} %pad_maximum_fusion.2), channel_id=1, source_target_pairs={{0,4},{4,0},{1,5},{5,1},{2,6},{6,2},{3,7},{7,3},{8,12},{12,8},{9,1... | collective-permute-start | bytes 417800 | tf_op jit(solution)/shard_map/ppermute | solution.py:207
  6.2 12.7 %collective-permute-start = (bf16[32,640]{1,0:T(8,128)(2,1)S(1)}, bf16[32,640]{1,0:T(8,128)(2,1)S(1)}, u32[]{:S(2)}, u32[]{:S(2)}) collective-permute-start(bf16[32,640]{1,0:T(8,128)(2,1)S(1)} %get-tuple-element.41), channel_id=1, source_target_pairs={{0,0},{1,32},{2,64},{3,96},{4,128},{5,160},{6,192},{7,224},{8,8},{... | collective-permute-start | bytes 122888 | tf_op jit(solution)/shard_map/ppermute | solution.py:211
  14.6 4.4 %collective-permute-start.1 = (bf16[32,640]{1,0:T(8,128)(2,1)S(1)}, bf16[32,640]{1,0:T(8,128)(2,1)S(1)}, u32[]{:S(2)}, u32[]{:S(2)}) collective-permute-start(bf16[32,640]{1,0:T(8,128)(2,1)S(1)} %get-tuple-element.40), channel_id=1, source_target_pairs={{0,128},{1,160},{2,192},{3,224},{4,0},{5,32},{6,64},{7,96},{8,136}... | collective-permute-start | bytes 122888 | tf_op jit(solution)/shard_map/ppermute | solution.py:212
  15.6 23.5 %collective-permute-start.9 = (bf16[2,32,2176]{2,1,0:T(8,128)(2,1)S(1)}, bf16[2,32,2176]{2,1,0:T(8,128)(2,1)S(1)}, u32[]{:S(2)}, u32[]{:S(2)}) collective-permute-start(bf16[2,32,2176]{2,1,0:T(8,128)(2,1)S(1)} %pad_maximum_fusion.1.here), channel_id=1, source_target_pairs={{0,32},{32,64},{64,96},{96,128},{128,160},{160,192},{192,224},{224... | collective-permute-start | bytes 835592 | tf_op jit(solution)/shard_map/ppermute | solution.py:192
  17.7 22.0 %collective-permute-start.12 = (bf16[2,32,2176]{2,1,0:T(8,128)(2,1)S(1)}, bf16[2,32,2176]{2,1,0:T(8,128)(2,1)S(1)}, u32[]{:S(2)}, u32[]{:S(2)}) collective-permute-start(bf16[2,32,2176]{2,1,0:T(8,128)(2,1)S(1)} %pad_maximum_fusion.1.here), channel_id=1, source_target_pairs={{0,224},{32,0},{64,32},{96,64},{128,96},{160,128},{192,160},{224,1... | collective-permute-start | bytes 835592 | tf_op jit(solution)/shard_map/ppermute | solution.py:192
  19.0 15.2 %collective-permute-start.2 = (bf16[64,640]{1,0:T(8,128)(2,1)S(1)}, bf16[64,640]{1,0:T(8,128)(2,1)S(1)}, u32[]{:S(2)}, u32[]{:S(2)}) collective-permute-start(bf16[64,640]{1,0:T(8,128)(2,1)S(1)} %get-tuple-element.36), channel_id=1, source_target_pairs={{0,8},{8,16},{16,24},{24,0},{1,9},{9,17},{17,25},{25,1},{2,10},{10... | collective-permute-start | bytes 245768 | tf_op jit(solution)/shard_map/ppermute | solution.py:199
  20.5 13.6 %collective-permute-start.3 = (bf16[64,640]{1,0:T(8,128)(2,1)S(1)}, bf16[64,640]{1,0:T(8,128)(2,1)S(1)}, u32[]{:S(2)}, u32[]{:S(2)}) collective-permute-start(bf16[64,640]{1,0:T(8,128)(2,1)S(1)} %get-tuple-element.36), channel_id=1, source_target_pairs={{0,16},{8,24},{16,0},{24,8},{1,17},{9,25},{17,1},{25,9},{2,18},{10... | collective-permute-start | bytes 245768 | tf_op jit(solution)/shard_map/ppermute | solution.py:199
  23.3 10.9 %collective-permute-start.4 = (bf16[64,640]{1,0:T(8,128)(2,1)S(1)}, bf16[64,640]{1,0:T(8,128)(2,1)S(1)}, u32[]{:S(2)}, u32[]{:S(2)}) collective-permute-start(bf16[64,640]{1,0:T(8,128)(2,1)S(1)} %get-tuple-element.36), channel_id=1, source_target_pairs={{0,24},{8,0},{16,8},{24,16},{1,25},{9,1},{17,9},{25,17},{2,26},{10... | collective-permute-start | bytes 245768 | tf_op jit(solution)/shard_map/ppermute | solution.py:199
  26.3 50.4 %all-to-all-start = ((bf16[32,64,256]{2,1,0:T(8,128)(2,1)}), bf16[32,64,256]{2,1,0:T(8,128)(2,1)}, u32[]{:S(2)}, u32[]{:S(2)}) async-start(bf16[32,64,256]{2,1,0:T(8,128)(2,1)} %bitcast.10), calls=%async_computation | async-start | bytes 2097152 | tf_op jit(solution)/shard_map/all_to_all | solution.py:216
  34.2 30.8 %collective-permute-start.5 = (bf16[256,640]{1,0:T(8,128)(2,1)S(1)}, bf16[256,640]{1,0:T(8,128)(2,1)S(1)}, u32[]{:S(2)}, u32[]{:S(2)}) collective-permute-start(bf16[256,640]{1,0:T(8,128)(2,1)S(1)} %pad_maximum_fusion), channel_id=1, source_target_pairs={{0,4},{4,2},{2,6},{6,0},{1,5},{5,3},{3,7},{7,1},{8,12},{12,10},{10... | collective-permute-start | bytes 983048 | tf_op jit(solution)/shard_map/ppermute | solution.py:199
  34.5 30.7 %collective-permute-start.6 = (bf16[256,640]{1,0:T(8,128)(2,1)S(1)}, bf16[256,640]{1,0:T(8,128)(2,1)S(1)}, u32[]{:S(2)}, u32[]{:S(2)}) collective-permute-start(bf16[256,640]{1,0:T(8,128)(2,1)S(1)} %pad_maximum_fusion), channel_id=1, source_target_pairs={{0,2},{4,6},{2,0},{6,4},{1,3},{5,7},{3,1},{7,5},{8,10},{12,14},{10... | collective-permute-start | bytes 983048 | tf_op jit(solution)/shard_map/ppermute | solution.py:199
  36.7 28.5 %collective-permute-start.7 = (bf16[256,640]{1,0:T(8,128)(2,1)S(1)}, bf16[256,640]{1,0:T(8,128)(2,1)S(1)}, u32[]{:S(2)}, u32[]{:S(2)}) collective-permute-start(bf16[256,640]{1,0:T(8,128)(2,1)S(1)} %pad_maximum_fusion), channel_id=1, source_target_pairs={{0,6},{4,0},{2,4},{6,2},{1,7},{5,1},{3,5},{7,3},{8,14},{12,8},{10,... | collective-permute-start | bytes 983048 | tf_op jit(solution)/shard_map/ppermute | solution.py:199
  39.1 18.7 %collective-permute-start.10 = (bf16[2,32,2176]{2,1,0:T(8,128)(2,1)S(1)}, bf16[2,32,2176]{2,1,0:T(8,128)(2,1)S(1)}, u32[]{:S(2)}, u32[]{:S(2)}) collective-permute-start(bf16[2,32,2176]{2,1,0:T(8,128)(2,1)S(1)} %collective-permute-done.9.back1), channel_id=1, source_target_pairs={{0,32},{32,64},{64,96},{96,128},{128,160},{160,192},{192,224},{224... | collective-permute-start | bytes 835592 | tf_op jit(solution)/shard_map/ppermute | solution.py:192
  39.7 25.3 %collective-permute-start.13 = (bf16[2,32,2176]{2,1,0:T(8,128)(2,1)S(1)}, bf16[2,32,2176]{2,1,0:T(8,128)(2,1)S(1)}, u32[]{:S(2)}, u32[]{:S(2)}) collective-permute-start(bf16[2,32,2176]{2,1,0:T(8,128)(2,1)S(1)} %collective-permute-done.12.on1), channel_id=1, source_target_pairs={{0,224},{32,0},{64,32},{96,64},{128,96},{160,128},{192,160},{224,1... | collective-permute-start | bytes 835592 | tf_op jit(solution)/shard_map/ppermute | solution.py:192
  57.8 13.4 %copy-start.2 = (bf16[2,32,2176]{2,1,0:T(8,128)(2,1)}, bf16[2,32,2176]{2,1,0:T(8,128)(2,1)S(1)}, u32[]{:S(2)}) copy-start(bf16[2,32,2176]{2,1,0:T(8,128)(2,1)S(1)} %collective-permute-done.10.back2) | copy-start | bytes 835588
  57.8 13.4 %collective-permute-start.11 = (bf16[2,32,2176]{2,1,0:T(8,128)(2,1)S(1)}, bf16[2,32,2176]{2,1,0:T(8,128)(2,1)S(1)}, u32[]{:S(2)}, u32[]{:S(2)}) collective-permute-start(bf16[2,32,2176]{2,1,0:T(8,128)(2,1)S(1)} %collective-permute-done.10.back2), channel_id=1, source_target_pairs={{0,32},{32,64},{64,96},{96,128},{128,160},{160,192},{192,224},{224... | collective-permute-start | bytes 835592 | tf_op jit(solution)/shard_map/ppermute | solution.py:192
  65.1 6.2 %copy-start.4 = (bf16[2,32,2176]{2,1,0:T(8,128)(2,1)}, bf16[2,32,2176]{2,1,0:T(8,128)(2,1)S(1)}, u32[]{:S(2)}) copy-start(bf16[2,32,2176]{2,1,0:T(8,128)(2,1)S(1)} %collective-permute-done.13.on2) | copy-start | bytes 835588
  65.1 9.1 %collective-permute-start.14 = (bf16[2,32,2176]{2,1,0:T(8,128)(2,1)S(1)}, bf16[2,32,2176]{2,1,0:T(8,128)(2,1)S(1)}, u32[]{:S(2)}, u32[]{:S(2)}) collective-permute-start(bf16[2,32,2176]{2,1,0:T(8,128)(2,1)S(1)} %collective-permute-done.13.on2), channel_id=1, source_target_pairs={{0,224},{32,0},{64,32},{96,64},{128,96},{160,128},{192,160},{224,1... | collective-permute-start | bytes 835592 | tf_op jit(solution)/shard_map/ppermute | solution.py:192
  71.2 2.9 %copy-start.6 = (bf16[2,32,2176]{2,1,0:T(8,128)(2,1)}, bf16[2,32,2176]{2,1,0:T(8,128)(2,1)S(1)}, u32[]{:S(2)}) copy-start(bf16[2,32,2176]{2,1,0:T(8,128)(2,1)S(1)} %collective-permute-done.11.back3) | copy-start | bytes 835588
  74.1 0.7 copy-start.8
  74.9 3.0 %collective-permute-start.15 = (bf16[1024,640]{1,0:T(8,128)(2,1)S(1)}, bf16[1024,640]{1,0:T(8,128)(2,1)S(1)}, u32[]{:S(2)}, u32[]{:S(2)}) collective-permute-start(bf16[1024,640]{1,0:T(8,128)(2,1)S(1)} %constant_dynamic-update-slice_fusion.own), channel_id=1, source_target_pairs={{0,1},{1,0},{2,3},{3,2},{4,5},{5,4},{6,7},{7,6},{8,9},{9,8},{10,11... | collective-permute-start | bytes 3932168 | tf_op jit(solution)/shard_map/ppermute | solution.py:225
  74.9 10.6 %collective-permute-start.17 = (bf16[2,32,2176]{2,1,0:T(8,128)(2,1)}, bf16[2,32,2176]{2,1,0:T(8,128)(2,1)}, u32[]{:S(2)}, u32[]{:S(2)}) collective-permute-start(bf16[2,32,2176]{2,1,0:T(8,128)(2,1)} %copy-done.6), channel_id=1, source_target_pairs={{0,32},{32,64},{64,96},{96,128},{128,160},{160,192},{192,224},{224... | collective-permute-start | bytes 835592 | tf_op jit(solution)/shard_map/ppermute | solution.py:192
  77.9 7.6 %copy-start.3 = (bf16[2,32,2176]{2,1,0:T(8,128)(2,1)S(1)}, bf16[2,32,2176]{2,1,0:T(8,128)(2,1)}, u32[]{:S(2)}) copy-start(bf16[2,32,2176]{2,1,0:T(8,128)(2,1)} %copy-done.2) | copy-start | bytes 835588
  77.9 7.6 %copy-start.5 = (bf16[2,32,2176]{2,1,0:T(8,128)(2,1)S(1)}, bf16[2,32,2176]{2,1,0:T(8,128)(2,1)}, u32[]{:S(2)}) copy-start(bf16[2,32,2176]{2,1,0:T(8,128)(2,1)} %copy-done.4) | copy-start | bytes 835588
  77.9 7.6 %copy-start.7 = (bf16[2,32,2176]{2,1,0:T(8,128)(2,1)S(1)}, bf16[2,32,2176]{2,1,0:T(8,128)(2,1)}, u32[]{:S(2)}) copy-start(bf16[2,32,2176]{2,1,0:T(8,128)(2,1)} %copy-done.6) | copy-start | bytes 835588
  77.9 7.6 %copy-start.9 = (bf16[2,32,2176]{2,1,0:T(8,128)(2,1)S(1)}, bf16[2,32,2176]{2,1,0:T(8,128)(2,1)}, u32[]{:S(2)}) copy-start(bf16[2,32,2176]{2,1,0:T(8,128)(2,1)} %copy-done.8) | copy-start | bytes 835588
  80.8 8.4 %collective-permute-start.16 = (f32[256,256]{1,0:T(8,128)S(1)}, f32[256,256]{1,0:T(8,128)S(1)}, u32[]{:S(2)}, u32[]{:S(2)}) collective-permute-start(f32[256,256]{1,0:T(8,128)S(1)} %get-tuple-element.18), channel_id=1, source_target_pairs={{0,4},{4,0},{1,5},{5,1},{2,6},{6,2},{3,7},{7,3},{8,12},{12,8},{9,1... | collective-permute-start | bytes 786440 | tf_op jit(solution)/shard_map/ppermute | solution.py:235
  90.9 16.1 %copy-start = (f32[64,2048]{1,0:T(8,128)S(1)}, f32[64,2048]{1,0:T(8,128)}, u32[]{:S(2)}) copy-start(f32[64,2048]{1,0:T(8,128)} %moment1.1) | copy-start | bytes 1572868
  90.9 16.1 %copy-start.1 = (f32[64,2048]{1,0:T(8,128)S(1)}, f32[64,2048]{1,0:T(8,128)}, u32[]{:S(2)}) copy-start(f32[64,2048]{1,0:T(8,128)} %moment2.1) | copy-start | bytes 1572868
  90.9 10.1 %collective-permute-start.18 = (f16[64,2176]{1,0:T(8,128)(2,1)S(1)}, f16[64,2176]{1,0:T(8,128)(2,1)S(1)}, u32[]{:S(2)}, u32[]{:S(2)}) collective-permute-start(f16[64,2176]{1,0:T(8,128)(2,1)S(1)} %get-tuple-element.39), channel_id=1, source_target_pairs={{0,8},{8,16},{16,24},{24,0},{1,9},{9,17},{17,25},{25,1},{2,10},{10... | collective-permute-start | bytes 835592 | tf_op jit(solution)/shard_map/ppermute | solution.py:188
  92.1 14.8 %collective-permute-start.19 = (f16[64,2176]{1,0:T(8,128)(2,1)S(1)}, f16[64,2176]{1,0:T(8,128)(2,1)S(1)}, u32[]{:S(2)}, u32[]{:S(2)}) collective-permute-start(f16[64,2176]{1,0:T(8,128)(2,1)S(1)} %get-tuple-element.38), channel_id=1, source_target_pairs={{0,16},{8,24},{16,0},{24,8},{1,17},{9,25},{17,1},{25,9},{2,18},{10... | collective-permute-start | bytes 835592 | tf_op jit(solution)/shard_map/ppermute | solution.py:188
  95.0 11.9 %collective-permute-start.20 = (f16[64,2176]{1,0:T(8,128)(2,1)S(1)}, f16[64,2176]{1,0:T(8,128)(2,1)S(1)}, u32[]{:S(2)}, u32[]{:S(2)}) collective-permute-start(f16[64,2176]{1,0:T(8,128)(2,1)S(1)} %get-tuple-element.37), channel_id=1, source_target_pairs={{0,24},{8,0},{16,8},{24,16},{1,25},{9,1},{17,9},{25,17},{2,26},{10... | collective-permute-start | bytes 835592 | tf_op jit(solution)/shard_map/ppermute | solution.py:188
  108.5 9.3 %collective-permute-start.21 = (f16[64,2176]{1,0:T(8,128)(2,1)S(1)}, f16[64,2176]{1,0:T(8,128)(2,1)S(1)}, u32[]{:S(2)}, u32[]{:S(2)}) collective-permute-start(f16[64,2176]{1,0:T(8,128)(2,1)S(1)} %convert_element_type.36), channel_id=1, source_target_pairs={{0,8},{8,16},{16,24},{24,0},{1,9},{9,17},{17,25},{25,1},{2,10},{10... | collective-permute-start | bytes 835592 | tf_op jit(solution)/shard_map/ppermute | solution.py:188
  110.0 14.9 %collective-permute-start.22 = (f16[64,2176]{1,0:T(8,128)(2,1)S(1)}, f16[64,2176]{1,0:T(8,128)(2,1)S(1)}, u32[]{:S(2)}, u32[]{:S(2)}) collective-permute-start(f16[64,2176]{1,0:T(8,128)(2,1)S(1)} %convert_element_type.36), channel_id=1, source_target_pairs={{0,16},{8,24},{16,0},{24,8},{1,17},{9,25},{17,1},{25,9},{2,18},{10... | collective-permute-start | bytes 835592 | tf_op jit(solution)/shard_map/ppermute | solution.py:188
  112.4 12.6 %collective-permute-start.23 = (f16[64,2176]{1,0:T(8,128)(2,1)S(1)}, f16[64,2176]{1,0:T(8,128)(2,1)S(1)}, u32[]{:S(2)}, u32[]{:S(2)}) collective-permute-start(f16[64,2176]{1,0:T(8,128)(2,1)S(1)} %convert_element_type.36), channel_id=1, source_target_pairs={{0,24},{8,0},{16,8},{24,16},{1,25},{9,1},{17,9},{25,17},{2,26},{10... | collective-permute-start | bytes 835592 | tf_op jit(solution)/shard_map/ppermute | solution.py:188
  126.3 7.6 %collective-permute-start.24 = (f32[264,256]{1,0:T(8,128)S(1)}, f32[264,256]{1,0:T(8,128)S(1)}, u32[]{:S(2)}, u32[]{:S(2)}) collective-permute-start(f32[264,256]{1,0:T(8,128)S(1)} %get-tuple-element.23), channel_id=1, source_target_pairs={{0,4},{4,0},{1,5},{5,1},{2,6},{6,2},{3,7},{7,3},{8,12},{12,8},{9,1... | collective-permute-start | bytes 811016 | tf_op jit(solution)/shard_map/ppermute | solution.py:259
  137.2 33.8 %all-to-all-start.1 = ((f16[32,64,256]{2,1,0:T(8,128)(2,1)}), f16[32,64,256]{2,1,0:T(8,128)(2,1)S(1)}, u32[]{:S(2)}, u32[]{:S(2)}) async-start(f16[32,64,256]{2,1,0:T(8,128)(2,1)} %bitcast.12), calls=%async_computation.1 | async-start | bytes 2097152 | tf_op jit(solution)/shard_map/all_to_all | solution.py:271
  144.7 20.1 %collective-permute-start.25 = (f32[8,256]{1,0:T(8,128)S(1)}, f32[8,256]{1,0:T(8,128)S(1)}, u32[]{:S(2)}, u32[]{:S(2)}) collective-permute-start(f32[8,256]{1,0:T(8,128)S(1)} %get-tuple-element.26), channel_id=1, source_target_pairs={{0,32},{32,64},{64,96},{96,0},{1,33},{33,65},{65,97},{97,1},{2,34}... | collective-permute-start | bytes 24584 | tf_op jit(solution)/shard_map/ppermute | solution.py:188
  146.4 23.2 %collective-permute-start.26 = (f32[8,256]{1,0:T(8,128)S(1)}, f32[8,256]{1,0:T(8,128)S(1)}, u32[]{:S(2)}, u32[]{:S(2)}) collective-permute-start(f32[8,256]{1,0:T(8,128)S(1)} %get-tuple-element.26), channel_id=1, source_target_pairs={{0,64},{32,96},{64,0},{96,32},{1,65},{33,97},{65,1},{97,33},{2,66}... | collective-permute-start | bytes 24584 | tf_op jit(solution)/shard_map/ppermute | solution.py:188
  148.8 20.8 %collective-permute-start.27 = (f32[8,256]{1,0:T(8,128)S(1)}, f32[8,256]{1,0:T(8,128)S(1)}, u32[]{:S(2)}, u32[]{:S(2)}) collective-permute-start(f32[8,256]{1,0:T(8,128)S(1)} %get-tuple-element.26), channel_id=1, source_target_pairs={{0,96},{32,0},{64,32},{96,64},{1,97},{33,1},{65,33},{97,65},{2,98}... | collective-permute-start | bytes 24584 | tf_op jit(solution)/shard_map/ppermute | solution.py:188

commit v6 on v5

--- a/solution.py
+++ b/solution.py
@@ -242,14 +242,15 @@
         8,
     )
     (message,) = call(right_kernel, [(4 * ROWS, WIDTH + LANES)], operands=(mine, theirs, right))
-    got = [shifted(message[s * ROWS:(s + 1) * ROWS].astype(F16), "x", s).astype(F32) for s in range(1, 4)]
+    got = [shifted(message[s * ROWS:(s + 1) * ROWS].astype(F16), "x", s).astype(F32) for s in (2, 1, 3)]
     first_new, second_new, message = call(
         moment_kernel,
         [(ROWS, WIDTH)] * 2 + [(ROWS, WIDTH + LANES)],
         operands=(message, *got, moment1, moment2),
     )
     narrow = message.astype(F16)
-    got = [shifted(narrow, "x", s).astype(F32) for s in range(1, 4)]
+    got = [shifted(narrow, "x", s).astype(F32) for s in (2, 1, 3)]
+    got = [got[1], got[0], got[2]]
     mine, theirs, top = call(
         back_kernel,
         [(4 * ROWS, SLICE), (4 * ROWS + 8, SLICE), (8, SLICE)],

time: 173 us -> 173 us (level)
  transfers between devices with their start and end apart: 30 -> 30, of which waited for: 14 -> 15; matrix products, arithmetic and copies ran while one was open for 3% -> 3% of each run, Pallas kernels for 3% -> 3%
where the time goes in v6:
time: 173 us
  waiting for transfers between devices  79.8 us (46%)
  starting transfers between devices  70.7 us (41%)
  Pallas kernels  10.8 us (6%)
  local copies, waits for them, and re-layouts  5.74 us (3%)
  other arithmetic  4.72 us (3%)
    ppermute x9, waiting for transfers between devices, shifted(): return lax.ppermute(value, axis, [(i, (i + shift) % 4) for i in range(4)])  40.2 us
    ppermute x7, waiting for transfers between devices, around(): lax.ppermute(value, ('zh', 'zl'), [(i, (i + shift) % 8) for i in range(8)])  28.5 us
    ppermute x9, starting transfers between devices, shifted(): return lax.ppermute(value, axis, [(i, (i + shift) % 4) for i in range(4)])  16.5 us
    ppermute x7, starting transfers between devices, around(): lax.ppermute(value, ('zh', 'zl'), [(i, (i + shift) % 8) for i in range(8)])  15.5 us
    pallas_call x6, Pallas kernels, call(): pl.pallas_call(kernel, out_shape=tuple((jax.ShapeDtypeStruct(shape, BF16...  10.8 us
    ppermute x6, starting transfers between devices, ring_gather(): lax.ppermute(value, axes, [(names[i], names[(i + shift) % size]) for i in...  10.7 us
    ppermute x2, waiting for transfers between devices, body(): theirs = lax.ppermute(theirs, 'l', SWAP)  8.65 us
    ppermute x1, starting transfers between devices, body(): got1 = lax.ppermute(jnp.where(l == 0, pieces[0], pieces[1]), AXES, first)  8.38 us
  transfers between devices with their start and end apart: 30, of which 15 were waited for; matrix products, arithmetic and copies ran while one was open for 3% of the time, Pallas kernels for 3%

profile of v6, /device:TPU:8, one launch (start us, length us, event | category | flops | bytes accessed | tf_op | source)
XLA Modules:
  0.0 172.7 jit_solution(826266068372022460)
XLA Ops:
  0.6 0.8 broadcast_in_dim.75
  1.4 0.9 pad_maximum_fusion.2
  2.3 2.3 %collective-permute-start.8 = (bf16[1,32,2176]{2,1,0:T(8,128)(2,1)S(1)}, bf16[1,32,2176]{2,1,0:T(8,128)(2,1)S(1)}, u32[]{:S(2)}, u32[]{:S(2)}) collective-permute-start(bf16[1,32,2176]{2,1,0:T(8,128)(2,1)S(1)} %pad_maximum_fusion.2), channel_id=1, source_target_pairs={{0,4},{4,0},{1,5},{5,1},{2,6},{6,2},{3,7},{7,3},{8,12},{12,8},{9,1... | collective-permute-start | bytes 417800 | tf_op jit(solution)/shard_map/ppermute | solution.py:207
  5.3 0.9 select_bitcast_fusion
  6.2 8.4 %collective-permute-start = (bf16[32,640]{1,0:T(8,128)(2,1)S(1)}, bf16[32,640]{1,0:T(8,128)(2,1)S(1)}, u32[]{:S(2)}, u32[]{:S(2)}) collective-permute-start(bf16[32,640]{1,0:T(8,128)(2,1)S(1)} %get-tuple-element.41), channel_id=1, source_target_pairs={{0,0},{1,32},{2,64},{3,96},{4,128},{5,160},{6,192},{7,224},{8,8},{... | collective-permute-start | bytes 122888 | tf_op jit(solution)/shard_map/ppermute | solution.py:211
  14.7 0.9 pad_maximum_fusion.1.here
  15.6 2.1 %collective-permute-start.9 = (bf16[2,32,2176]{2,1,0:T(8,128)(2,1)S(1)}, bf16[2,32,2176]{2,1,0:T(8,128)(2,1)S(1)}, u32[]{:S(2)}, u32[]{:S(2)}) collective-permute-start(bf16[2,32,2176]{2,1,0:T(8,128)(2,1)S(1)} %pad_maximum_fusion.1.here), channel_id=1, source_target_pairs={{0,32},{32,64},{64,96},{96,128},{128,160},{160,192},{192,224},{224... | collective-permute-start | bytes 835592 | tf_op jit(solution)/shard_map/ppermute | solution.py:192
  17.7 1.2 collective-permute-start.12
  19.0 1.6 collective-permute-start.2
  20.5 2.7 %collective-permute-start.3 = (bf16[64,640]{1,0:T(8,128)(2,1)S(1)}, bf16[64,640]{1,0:T(8,128)(2,1)S(1)}, u32[]{:S(2)}, u32[]{:S(2)}) collective-permute-start(bf16[64,640]{1,0:T(8,128)(2,1)S(1)} %get-tuple-element.36), channel_id=1, source_target_pairs={{0,16},{8,24},{16,0},{24,8},{1,17},{9,25},{17,1},{25,9},{2,18},{10... | collective-permute-start | bytes 245768 | tf_op jit(solution)/shard_map/ppermute | solution.py:199
  23.3 1.4 collective-permute-start.4
  25.2 1.1 broadcast_in_dim.77
  26.3 7.8 %all-to-all-start = ((bf16[32,64,256]{2,1,0:T(8,128)(2,1)}), bf16[32,64,256]{2,1,0:T(8,128)(2,1)}, u32[]{:S(2)}, u32[]{:S(2)}) async-start(bf16[32,64,256]{2,1,0:T(8,128)(2,1)} %bitcast.10), calls=%async_computation | async-start | bytes 2097152 | tf_op jit(solution)/shard_map/all_to_all | solution.py:216
  34.5 2.2 %collective-permute-start.6 = (bf16[256,640]{1,0:T(8,128)(2,1)S(1)}, bf16[256,640]{1,0:T(8,128)(2,1)S(1)}, u32[]{:S(2)}, u32[]{:S(2)}) collective-permute-start(bf16[256,640]{1,0:T(8,128)(2,1)S(1)} %pad_maximum_fusion), channel_id=1, source_target_pairs={{0,2},{4,6},{2,0},{6,4},{1,3},{5,7},{3,1},{7,5},{8,10},{12,14},{10... | collective-permute-start | bytes 983048 | tf_op jit(solution)/shard_map/ppermute | solution.py:199
  36.7 2.5 %collective-permute-start.7 = (bf16[256,640]{1,0:T(8,128)(2,1)S(1)}, bf16[256,640]{1,0:T(8,128)(2,1)S(1)}, u32[]{:S(2)}, u32[]{:S(2)}) collective-permute-start(bf16[256,640]{1,0:T(8,128)(2,1)S(1)} %pad_maximum_fusion), channel_id=1, source_target_pairs={{0,6},{4,0},{2,4},{6,2},{1,7},{5,1},{3,5},{7,3},{8,14},{12,8},{10,... | collective-permute-start | bytes 983048 | tf_op jit(solution)/shard_map/ppermute | solution.py:199
  39.7 2.7 %collective-permute-start.13 = (bf16[2,32,2176]{2,1,0:T(8,128)(2,1)S(1)}, bf16[2,32,2176]{2,1,0:T(8,128)(2,1)S(1)}, u32[]{:S(2)}, u32[]{:S(2)}) collective-permute-start(bf16[2,32,2176]{2,1,0:T(8,128)(2,1)S(1)} %collective-permute-done.12.on1), channel_id=1, source_target_pairs={{0,224},{32,0},{64,32},{96,64},{128,96},{160,128},{192,160},{224,1... | collective-permute-start | bytes 835592 | tf_op jit(solution)/shard_map/ppermute | solution.py:192
  42.4 15.4 %collective-permute-done.10.back2 = bf16[2,32,2176]{2,1,0:T(8,128)(2,1)S(1)} collective-permute-done((bf16[2,32,2176]{2,1,0:T(8,128)(2,1)S(1)}, bf16[2,32,2176]{2,1,0:T(8,128)(2,1)S(1)}, u32[]{:S(2)}, u32[]{:S(2)}) %collective-permute-start.10) | collective-permute-done | bytes 278560 | tf_op jit(solution)/shard_map/ppermute | solution.py:192
  57.8 7.2 %collective-permute-start.11 = (bf16[2,32,2176]{2,1,0:T(8,128)(2,1)S(1)}, bf16[2,32,2176]{2,1,0:T(8,128)(2,1)S(1)}, u32[]{:S(2)}, u32[]{:S(2)}) collective-permute-start(bf16[2,32,2176]{2,1,0:T(8,128)(2,1)S(1)} %collective-permute-done.10.back2), channel_id=1, source_target_pairs={{0,32},{32,64},{64,96},{96,128},{128,160},{160,192},{192,224},{224... | collective-permute-start | bytes 835592 | tf_op jit(solution)/shard_map/ppermute | solution.py:192
  65.2 6.0 %collective-permute-done.11.back3 = bf16[2,32,2176]{2,1,0:T(8,128)(2,1)S(1)} collective-permute-done((bf16[2,32,2176]{2,1,0:T(8,128)(2,1)S(1)}, bf16[2,32,2176]{2,1,0:T(8,128)(2,1)S(1)}, u32[]{:S(2)}, u32[]{:S(2)}) %collective-permute-start.11) | collective-permute-done | bytes 278560 | tf_op jit(solution)/shard_map/ppermute | solution.py:192
  71.2 2.9 %collective-permute-done.14.on3 = bf16[2,32,2176]{2,1,0:T(8,128)(2,1)S(1)} collective-permute-done((bf16[2,32,2176]{2,1,0:T(8,128)(2,1)S(1)}, bf16[2,32,2176]{2,1,0:T(8,128)(2,1)S(1)}, u32[]{:S(2)}, u32[]{:S(2)}) %collective-permute-start.14) | collective-permute-done | bytes 278560 | tf_op jit(solution)/shard_map/ppermute | solution.py:192
  74.9 1.7 %collective-permute-start.17 = (bf16[2,32,2176]{2,1,0:T(8,128)(2,1)}, bf16[2,32,2176]{2,1,0:T(8,128)(2,1)}, u32[]{:S(2)}, u32[]{:S(2)}) collective-permute-start(bf16[2,32,2176]{2,1,0:T(8,128)(2,1)} %copy-done.6), channel_id=1, source_target_pairs={{0,32},{32,64},{64,96},{96,128},{128,160},{160,192},{192,224},{224... | collective-permute-start | bytes 835592 | tf_op jit(solution)/shard_map/ppermute | solution.py:192
  76.7 1.2 collective-permute-done.15.other
  77.9 2.8 %shard_map.94 = (f32[256,256]{1,0:T(8,128)S(1)}, f32[256,256]{1,0:T(8,128)S(1)}) custom-call(s32[4]{0:T(128)S(1)} %pad_add_fusion.place, bf16[1024,640]{1,0:T(8,128)(2,1)S(1)} %constant_dynamic-update-slice_fusion.own, bf16[1024,640]{1,0:T(8,128)(2,1)S(1)} %collective-permute-done.15.other, bf16[2048,256]{1,0:T(8,128)(2,1)} %bitcast.11.columns), custom_call_target="tpu_custom_call" | custom-call | tf_op jit(solution)/shard_map/pallas_call | solution.py:65
  81.2 4.2 %collective-permute-done.17.far = bf16[2,32,2176]{2,1,0:T(8,128)(2,1)} collective-permute-done((bf16[2,32,2176]{2,1,0:T(8,128)(2,1)}, bf16[2,32,2176]{2,1,0:T(8,128)(2,1)}, u32[]{:S(2)}, u32[]{:S(2)}) %collective-permute-start.17) | collective-permute-done | bytes 278560 | tf_op jit(solution)/shard_map/ppermute | solution.py:192
  85.5 1.7 shard_map.95.right
  87.2 2.0 %collective-permute-done.16.theirs = f32[256,256]{1,0:T(8,128)S(1)} collective-permute-done((f32[256,256]{1,0:T(8,128)S(1)}, f32[256,256]{1,0:T(8,128)S(1)}, u32[]{:S(2)}, u32[]{:S(2)}) %collective-permute-start.16) | collective-permute-done | bytes 262176 | tf_op jit(solution)/shard_map/ppermute | solution.py:235
  89.2 1.4 shard_map.96.own
  90.9 3.0 %collective-permute-start.18 = (f16[64,2176]{1,0:T(8,128)(2,1)S(1)}, f16[64,2176]{1,0:T(8,128)(2,1)S(1)}, u32[]{:S(2)}, u32[]{:S(2)}) collective-permute-start(f16[64,2176]{1,0:T(8,128)(2,1)S(1)} %get-tuple-element.39), channel_id=1, source_target_pairs={{0,16},{8,24},{16,0},{24,8},{1,17},{9,25},{17,1},{25,9},{2,18},{10... | collective-permute-start | bytes 835592 | tf_op jit(solution)/shard_map/ppermute | solution.py:188
  94.4 2.7 %collective-permute-start.20 = (f16[64,2176]{1,0:T(8,128)(2,1)S(1)}, f16[64,2176]{1,0:T(8,128)(2,1)S(1)}, u32[]{:S(2)}, u32[]{:S(2)}) collective-permute-start(f16[64,2176]{1,0:T(8,128)(2,1)S(1)} %get-tuple-element.37), channel_id=1, source_target_pairs={{0,24},{8,0},{16,8},{24,16},{1,25},{9,1},{17,9},{25,17},{2,26},{10... | collective-permute-start | bytes 835592 | tf_op jit(solution)/shard_map/ppermute | solution.py:188
  97.2 5.0 %collective-permute-done.18 = f16[64,2176]{1,0:T(8,128)(2,1)S(1)} collective-permute-done((f16[64,2176]{1,0:T(8,128)(2,1)S(1)}, f16[64,2176]{1,0:T(8,128)(2,1)S(1)}, u32[]{:S(2)}, u32[]{:S(2)}) %collective-permute-start.18) | collective-permute-done | bytes 278560 | tf_op jit(solution)/shard_map/ppermute | solution.py:188
  102.2 4.2 %collective-permute-done.19 = f16[64,2176]{1,0:T(8,128)(2,1)S(1)} collective-permute-done((f16[64,2176]{1,0:T(8,128)(2,1)S(1)}, f16[64,2176]{1,0:T(8,128)(2,1)S(1)}, u32[]{:S(2)}, u32[]{:S(2)}) %collective-permute-start.19) | collective-permute-done | bytes 278560 | tf_op jit(solution)/shard_map/ppermute | solution.py:188
  106.5 1.5 shard_map.97
  108.0 1.5 collective-permute-start.21
  109.5 2.5 %collective-permute-start.22 = (f16[64,2176]{1,0:T(8,128)(2,1)S(1)}, f16[64,2176]{1,0:T(8,128)(2,1)S(1)}, u32[]{:S(2)}, u32[]{:S(2)}) collective-permute-start(f16[64,2176]{1,0:T(8,128)(2,1)S(1)} %convert_element_type.36), channel_id=1, source_target_pairs={{0,16},{8,24},{16,0},{24,8},{1,17},{9,25},{17,1},{25,9},{2,18},{10... | collective-permute-start | bytes 835592 | tf_op jit(solution)/shard_map/ppermute | solution.py:188
  112.7 6.0 %collective-permute-done.21 = f16[64,2176]{1,0:T(8,128)(2,1)S(1)} collective-permute-done((f16[64,2176]{1,0:T(8,128)(2,1)S(1)}, f16[64,2176]{1,0:T(8,128)(2,1)S(1)}, u32[]{:S(2)}, u32[]{:S(2)}) %collective-permute-start.21) | collective-permute-done | bytes 278560 | tf_op jit(solution)/shard_map/ppermute | solution.py:188
  118.8 5.5 %collective-permute-done.22 = f16[64,2176]{1,0:T(8,128)(2,1)S(1)} collective-permute-done((f16[64,2176]{1,0:T(8,128)(2,1)S(1)}, f16[64,2176]{1,0:T(8,128)(2,1)S(1)}, u32[]{:S(2)}, u32[]{:S(2)}) %collective-permute-start.22) | collective-permute-done | bytes 278560 | tf_op jit(solution)/shard_map/ppermute | solution.py:188
  124.5 1.3 shard_map.98
  126.6 6.7 %collective-permute-done.24.theirs = f32[264,256]{1,0:T(8,128)S(1)} collective-permute-done((f32[264,256]{1,0:T(8,128)S(1)}, f32[264,256]{1,0:T(8,128)S(1)}, u32[]{:S(2)}, u32[]{:S(2)}) %collective-permute-start.24) | collective-permute-done | bytes 270368 | tf_op jit(solution)/shard_map/ppermute | solution.py:260
  133.2 2.0 %shard_map.99 = (f32[2048,256]{1,0:T(8,128)S(1)}, f32[8,256]{1,0:T(8,128)S(1)}) custom-call(s32[4]{0:T(128)S(1)} %pad_add_fusion.place, bf16[1024,640]{1,0:T(8,128)(2,1)S(1)} %constant_dynamic-update-slice_fusion.own, bf16[1024,640]{1,0:T(8,128)(2,1)S(1)} %collective-permute-done.15.other, f32[256,256]{1,0:T(8,128)S(1)} %get-tuple-element.22.mine, ...), custom_call_target="tpu_custom_call" | custom-call | tf_op jit(solution)/shard_map/pallas_call | solution.py:65
  135.2 1.2 convert_element_type.40
  136.4 8.2 %all-to-all-start.1 = ((f16[32,64,256]{2,1,0:T(8,128)(2,1)}), f16[32,64,256]{2,1,0:T(8,128)(2,1)S(1)}, u32[]{:S(2)}, u32[]{:S(2)}) async-start(f16[32,64,256]{2,1,0:T(8,128)(2,1)} %bitcast.12), calls=%async_computation.1 | async-start | bytes 2097152 | tf_op jit(solution)/shard_map/all_to_all | solution.py:272
  144.6 1.8 %collective-permute-start.25 = (f32[8,256]{1,0:T(8,128)S(1)}, f32[8,256]{1,0:T(8,128)S(1)}, u32[]{:S(2)}, u32[]{:S(2)}) collective-permute-start(f32[8,256]{1,0:T(8,128)S(1)} %get-tuple-element.26), channel_id=1, source_target_pairs={{0,32},{32,64},{64,96},{96,0},{1,33},{33,65},{65,97},{97,1},{2,34}... | collective-permute-start | bytes 24584 | tf_op jit(solution)/shard_map/ppermute | solution.py:188
  146.4 2.4 %collective-permute-start.26 = (f32[8,256]{1,0:T(8,128)S(1)}, f32[8,256]{1,0:T(8,128)S(1)}, u32[]{:S(2)}, u32[]{:S(2)}) collective-permute-start(f32[8,256]{1,0:T(8,128)S(1)} %get-tuple-element.26), channel_id=1, source_target_pairs={{0,64},{32,96},{64,0},{96,32},{1,65},{33,97},{65,1},{97,33},{2,66}... | collective-permute-start | bytes 24584 | tf_op jit(solution)/shard_map/ppermute | solution.py:188
  148.8 1.4 collective-permute-start.27
  150.2 14.5 %collective-permute-done.25 = f32[8,256]{1,0:T(8,128)S(1)} collective-permute-done((f32[8,256]{1,0:T(8,128)S(1)}, f32[8,256]{1,0:T(8,128)S(1)}, u32[]{:S(2)}, u32[]{:S(2)}) %collective-permute-start.25) | collective-permute-done | bytes 8224 | tf_op jit(solution)/shard_map/ppermute | solution.py:188
  164.7 4.8 %collective-permute-done.26 = f32[8,256]{1,0:T(8,128)S(1)} collective-permute-done((f32[8,256]{1,0:T(8,128)S(1)}, f32[8,256]{1,0:T(8,128)S(1)}, u32[]{:S(2)}, u32[]{:S(2)}) %collective-permute-start.26) | collective-permute-done | bytes 8224 | tf_op jit(solution)/shard_map/ppermute | solution.py:188
  169.7 1.2 all-to-all-done.1
  171.6 1.1 copy.20
  (79 shorter events, 7.0 us)
Async XLA Ops:
  0.6 24.1 %copy-start.10 = (bf16[64,2048]{1,0:T(8,128)(2,1)S(1)}, bf16[64,2048]{1,0:T(8,128)(2,1)}, u32[]{:S(2)}) copy-start(bf16[64,2048]{1,0:T(8,128)(2,1)} %param.7) | copy-start | bytes 786436
  2.3 12.3 %collective-permute-start.8 = (bf16[1,32,2176]{2,1,0:T(8,128)(2,1)S(1)}, bf16[1,32,2176]{2,1,0:T(8,128)(2,1)S(1)}, u32[]{:S(2)}, u32[]{:S(2)}) collective-permute-start(bf16[1,32,2176]{2,1,0:T(8,128)(2,1)S(1)} %pad_maximum_fusion.2), channel_id=1, source_target_pairs={{0,4},{4,0},{1,5},{5,1},{2,6},{6,2},{3,7},{7,3},{8,12},{12,8},{9,1... | collective-permute-start | bytes 417800 | tf_op jit(solution)/shard_map/ppermute | solution.py:207
  6.2 12.7 %collective-permute-start = (bf16[32,640]{1,0:T(8,128)(2,1)S(1)}, bf16[32,640]{1,0:T(8,128)(2,1)S(1)}, u32[]{:S(2)}, u32[]{:S(2)}) collective-permute-start(bf16[32,640]{1,0:T(8,128)(2,1)S(1)} %get-tuple-element.41), channel_id=1, source_target_pairs={{0,0},{1,32},{2,64},{3,96},{4,128},{5,160},{6,192},{7,224},{8,8},{... | collective-permute-start | bytes 122888 | tf_op jit(solution)/shard_map/ppermute | solution.py:211
  14.6 4.4 %collective-permute-start.1 = (bf16[32,640]{1,0:T(8,128)(2,1)S(1)}, bf16[32,640]{1,0:T(8,128)(2,1)S(1)}, u32[]{:S(2)}, u32[]{:S(2)}) collective-permute-start(bf16[32,640]{1,0:T(8,128)(2,1)S(1)} %get-tuple-element.40), channel_id=1, source_target_pairs={{0,128},{1,160},{2,192},{3,224},{4,0},{5,32},{6,64},{7,96},{8,136}... | collective-permute-start | bytes 122888 | tf_op jit(solution)/shard_map/ppermute | solution.py:212
  15.6 23.5 %collective-permute-start.9 = (bf16[2,32,2176]{2,1,0:T(8,128)(2,1)S(1)}, bf16[2,32,2176]{2,1,0:T(8,128)(2,1)S(1)}, u32[]{:S(2)}, u32[]{:S(2)}) collective-permute-start(bf16[2,32,2176]{2,1,0:T(8,128)(2,1)S(1)} %pad_maximum_fusion.1.here), channel_id=1, source_target_pairs={{0,32},{32,64},{64,96},{96,128},{128,160},{160,192},{192,224},{224... | collective-permute-start | bytes 835592 | tf_op jit(solution)/shard_map/ppermute | solution.py:192
  17.7 22.0 %collective-permute-start.12 = (bf16[2,32,2176]{2,1,0:T(8,128)(2,1)S(1)}, bf16[2,32,2176]{2,1,0:T(8,128)(2,1)S(1)}, u32[]{:S(2)}, u32[]{:S(2)}) collective-permute-start(bf16[2,32,2176]{2,1,0:T(8,128)(2,1)S(1)} %pad_maximum_fusion.1.here), channel_id=1, source_target_pairs={{0,224},{32,0},{64,32},{96,64},{128,96},{160,128},{192,160},{224,1... | collective-permute-start | bytes 835592 | tf_op jit(solution)/shard_map/ppermute | solution.py:192
  19.0 15.2 %collective-permute-start.2 = (bf16[64,640]{1,0:T(8,128)(2,1)S(1)}, bf16[64,640]{1,0:T(8,128)(2,1)S(1)}, u32[]{:S(2)}, u32[]{:S(2)}) collective-permute-start(bf16[64,640]{1,0:T(8,128)(2,1)S(1)} %get-tuple-element.36), channel_id=1, source_target_pairs={{0,8},{8,16},{16,24},{24,0},{1,9},{9,17},{17,25},{25,1},{2,10},{10... | collective-permute-start | bytes 245768 | tf_op jit(solution)/shard_map/ppermute | solution.py:199
  20.5 13.6 %collective-permute-start.3 = (bf16[64,640]{1,0:T(8,128)(2,1)S(1)}, bf16[64,640]{1,0:T(8,128)(2,1)S(1)}, u32[]{:S(2)}, u32[]{:S(2)}) collective-permute-start(bf16[64,640]{1,0:T(8,128)(2,1)S(1)} %get-tuple-element.36), channel_id=1, source_target_pairs={{0,16},{8,24},{16,0},{24,8},{1,17},{9,25},{17,1},{25,9},{2,18},{10... | collective-permute-start | bytes 245768 | tf_op jit(solution)/shard_map/ppermute | solution.py:199
  23.3 10.9 %collective-permute-start.4 = (bf16[64,640]{1,0:T(8,128)(2,1)S(1)}, bf16[64,640]{1,0:T(8,128)(2,1)S(1)}, u32[]{:S(2)}, u32[]{:S(2)}) collective-permute-start(bf16[64,640]{1,0:T(8,128)(2,1)S(1)} %get-tuple-element.36), channel_id=1, source_target_pairs={{0,24},{8,0},{16,8},{24,16},{1,25},{9,1},{17,9},{25,17},{2,26},{10... | collective-permute-start | bytes 245768 | tf_op jit(solution)/shard_map/ppermute | solution.py:199
  26.3 50.4 %all-to-all-start = ((bf16[32,64,256]{2,1,0:T(8,128)(2,1)}), bf16[32,64,256]{2,1,0:T(8,128)(2,1)}, u32[]{:S(2)}, u32[]{:S(2)}) async-start(bf16[32,64,256]{2,1,0:T(8,128)(2,1)} %bitcast.10), calls=%async_computation | async-start | bytes 2097152 | tf_op jit(solution)/shard_map/all_to_all | solution.py:216
  34.2 30.8 %collective-permute-start.5 = (bf16[256,640]{1,0:T(8,128)(2,1)S(1)}, bf16[256,640]{1,0:T(8,128)(2,1)S(1)}, u32[]{:S(2)}, u32[]{:S(2)}) collective-permute-start(bf16[256,640]{1,0:T(8,128)(2,1)S(1)} %pad_maximum_fusion), channel_id=1, source_target_pairs={{0,4},{4,2},{2,6},{6,0},{1,5},{5,3},{3,7},{7,1},{8,12},{12,10},{10... | collective-permute-start | bytes 983048 | tf_op jit(solution)/shard_map/ppermute | solution.py:199
  34.5 30.7 %collective-permute-start.6 = (bf16[256,640]{1,0:T(8,128)(2,1)S(1)}, bf16[256,640]{1,0:T(8,128)(2,1)S(1)}, u32[]{:S(2)}, u32[]{:S(2)}) collective-permute-start(bf16[256,640]{1,0:T(8,128)(2,1)S(1)} %pad_maximum_fusion), channel_id=1, source_target_pairs={{0,2},{4,6},{2,0},{6,4},{1,3},{5,7},{3,1},{7,5},{8,10},{12,14},{10... | collective-permute-start | bytes 983048 | tf_op jit(solution)/shard_map/ppermute | solution.py:199
  36.7 28.5 %collective-permute-start.7 = (bf16[256,640]{1,0:T(8,128)(2,1)S(1)}, bf16[256,640]{1,0:T(8,128)(2,1)S(1)}, u32[]{:S(2)}, u32[]{:S(2)}) collective-permute-start(bf16[256,640]{1,0:T(8,128)(2,1)S(1)} %pad_maximum_fusion), channel_id=1, source_target_pairs={{0,6},{4,0},{2,4},{6,2},{1,7},{5,1},{3,5},{7,3},{8,14},{12,8},{10,... | collective-permute-start | bytes 983048 | tf_op jit(solution)/shard_map/ppermute | solution.py:199
  39.1 18.7 %collective-permute-start.10 = (bf16[2,32,2176]{2,1,0:T(8,128)(2,1)S(1)}, bf16[2,32,2176]{2,1,0:T(8,128)(2,1)S(1)}, u32[]{:S(2)}, u32[]{:S(2)}) collective-permute-start(bf16[2,32,2176]{2,1,0:T(8,128)(2,1)S(1)} %collective-permute-done.9.back1), channel_id=1, source_target_pairs={{0,32},{32,64},{64,96},{96,128},{128,160},{160,192},{192,224},{224... | collective-permute-start | bytes 835592 | tf_op jit(solution)/shard_map/ppermute | solution.py:192
  39.7 25.3 %collective-permute-start.13 = (bf16[2,32,2176]{2,1,0:T(8,128)(2,1)S(1)}, bf16[2,32,2176]{2,1,0:T(8,128)(2,1)S(1)}, u32[]{:S(2)}, u32[]{:S(2)}) collective-permute-start(bf16[2,32,2176]{2,1,0:T(8,128)(2,1)S(1)} %collective-permute-done.12.on1), channel_id=1, source_target_pairs={{0,224},{32,0},{64,32},{96,64},{128,96},{160,128},{192,160},{224,1... | collective-permute-start | bytes 835592 | tf_op jit(solution)/shard_map/ppermute | solution.py:192
  57.8 13.4 %copy-start.2 = (bf16[2,32,2176]{2,1,0:T(8,128)(2,1)}, bf16[2,32,2176]{2,1,0:T(8,128)(2,1)S(1)}, u32[]{:S(2)}) copy-start(bf16[2,32,2176]{2,1,0:T(8,128)(2,1)S(1)} %collective-permute-done.10.back2) | copy-start | bytes 835588
  57.8 13.4 %collective-permute-start.11 = (bf16[2,32,2176]{2,1,0:T(8,128)(2,1)S(1)}, bf16[2,32,2176]{2,1,0:T(8,128)(2,1)S(1)}, u32[]{:S(2)}, u32[]{:S(2)}) collective-permute-start(bf16[2,32,2176]{2,1,0:T(8,128)(2,1)S(1)} %collective-permute-done.10.back2), channel_id=1, source_target_pairs={{0,32},{32,64},{64,96},{96,128},{128,160},{160,192},{192,224},{224... | collective-permute-start | bytes 835592 | tf_op jit(solution)/shard_map/ppermute | solution.py:192
  65.1 6.2 %copy-start.4 = (bf16[2,32,2176]{2,1,0:T(8,128)(2,1)}, bf16[2,32,2176]{2,1,0:T(8,128)(2,1)S(1)}, u32[]{:S(2)}) copy-start(bf16[2,32,2176]{2,1,0:T(8,128)(2,1)S(1)} %collective-permute-done.13.on2) | copy-start | bytes 835588
  65.1 9.1 %collective-permute-start.14 = (bf16[2,32,2176]{2,1,0:T(8,128)(2,1)S(1)}, bf16[2,32,2176]{2,1,0:T(8,128)(2,1)S(1)}, u32[]{:S(2)}, u32[]{:S(2)}) collective-permute-start(bf16[2,32,2176]{2,1,0:T(8,128)(2,1)S(1)} %collective-permute-done.13.on2), channel_id=1, source_target_pairs={{0,224},{32,0},{64,32},{96,64},{128,96},{160,128},{192,160},{224,1... | collective-permute-start | bytes 835592 | tf_op jit(solution)/shard_map/ppermute | solution.py:192
  71.2 2.9 %copy-start.6 = (bf16[2,32,2176]{2,1,0:T(8,128)(2,1)}, bf16[2,32,2176]{2,1,0:T(8,128)(2,1)S(1)}, u32[]{:S(2)}) copy-start(bf16[2,32,2176]{2,1,0:T(8,128)(2,1)S(1)} %collective-permute-done.11.back3) | copy-start | bytes 835588
  74.1 0.7 copy-start.8
  74.9 3.0 %collective-permute-start.15 = (bf16[1024,640]{1,0:T(8,128)(2,1)S(1)}, bf16[1024,640]{1,0:T(8,128)(2,1)S(1)}, u32[]{:S(2)}, u32[]{:S(2)}) collective-permute-start(bf16[1024,640]{1,0:T(8,128)(2,1)S(1)} %constant_dynamic-update-slice_fusion.own), channel_id=1, source_target_pairs={{0,1},{1,0},{2,3},{3,2},{4,5},{5,4},{6,7},{7,6},{8,9},{9,8},{10,11... | collective-permute-start | bytes 3932168 | tf_op jit(solution)/shard_map/ppermute | solution.py:225
  74.9 10.6 %collective-permute-start.17 = (bf16[2,32,2176]{2,1,0:T(8,128)(2,1)}, bf16[2,32,2176]{2,1,0:T(8,128)(2,1)}, u32[]{:S(2)}, u32[]{:S(2)}) collective-permute-start(bf16[2,32,2176]{2,1,0:T(8,128)(2,1)} %copy-done.6), channel_id=1, source_target_pairs={{0,32},{32,64},{64,96},{96,128},{128,160},{160,192},{192,224},{224... | collective-permute-start | bytes 835592 | tf_op jit(solution)/shard_map/ppermute | solution.py:192
  77.9 7.6 %copy-start.3 = (bf16[2,32,2176]{2,1,0:T(8,128)(2,1)S(1)}, bf16[2,32,2176]{2,1,0:T(8,128)(2,1)}, u32[]{:S(2)}) copy-start(bf16[2,32,2176]{2,1,0:T(8,128)(2,1)} %copy-done.2) | copy-start | bytes 835588
  77.9 7.6 %copy-start.5 = (bf16[2,32,2176]{2,1,0:T(8,128)(2,1)S(1)}, bf16[2,32,2176]{2,1,0:T(8,128)(2,1)}, u32[]{:S(2)}) copy-start(bf16[2,32,2176]{2,1,0:T(8,128)(2,1)} %copy-done.4) | copy-start | bytes 835588
  77.9 7.6 %copy-start.7 = (bf16[2,32,2176]{2,1,0:T(8,128)(2,1)S(1)}, bf16[2,32,2176]{2,1,0:T(8,128)(2,1)}, u32[]{:S(2)}) copy-start(bf16[2,32,2176]{2,1,0:T(8,128)(2,1)} %copy-done.6) | copy-start | bytes 835588
  77.9 7.6 %copy-start.9 = (bf16[2,32,2176]{2,1,0:T(8,128)(2,1)S(1)}, bf16[2,32,2176]{2,1,0:T(8,128)(2,1)}, u32[]{:S(2)}) copy-start(bf16[2,32,2176]{2,1,0:T(8,128)(2,1)} %copy-done.8) | copy-start | bytes 835588
  80.8 8.4 %collective-permute-start.16 = (f32[256,256]{1,0:T(8,128)S(1)}, f32[256,256]{1,0:T(8,128)S(1)}, u32[]{:S(2)}, u32[]{:S(2)}) collective-permute-start(f32[256,256]{1,0:T(8,128)S(1)} %get-tuple-element.18), channel_id=1, source_target_pairs={{0,4},{4,0},{1,5},{5,1},{2,6},{6,2},{3,7},{7,3},{8,12},{12,8},{9,1... | collective-permute-start | bytes 786440 | tf_op jit(solution)/shard_map/ppermute | solution.py:235
  90.9 15.6 %copy-start = (f32[64,2048]{1,0:T(8,128)S(1)}, f32[64,2048]{1,0:T(8,128)}, u32[]{:S(2)}) copy-start(f32[64,2048]{1,0:T(8,128)} %moment1.1) | copy-start | bytes 1572868
  90.9 15.5 %copy-start.1 = (f32[64,2048]{1,0:T(8,128)S(1)}, f32[64,2048]{1,0:T(8,128)}, u32[]{:S(2)}) copy-start(f32[64,2048]{1,0:T(8,128)} %moment2.1) | copy-start | bytes 1572868
  90.9 11.2 %collective-permute-start.18 = (f16[64,2176]{1,0:T(8,128)(2,1)S(1)}, f16[64,2176]{1,0:T(8,128)(2,1)S(1)}, u32[]{:S(2)}, u32[]{:S(2)}) collective-permute-start(f16[64,2176]{1,0:T(8,128)(2,1)S(1)} %get-tuple-element.39), channel_id=1, source_target_pairs={{0,16},{8,24},{16,0},{24,8},{1,17},{9,25},{17,1},{25,9},{2,18},{10... | collective-permute-start | bytes 835592 | tf_op jit(solution)/shard_map/ppermute | solution.py:188
  93.9 12.4 %collective-permute-start.19 = (f16[64,2176]{1,0:T(8,128)(2,1)S(1)}, f16[64,2176]{1,0:T(8,128)(2,1)S(1)}, u32[]{:S(2)}, u32[]{:S(2)}) collective-permute-start(f16[64,2176]{1,0:T(8,128)(2,1)S(1)} %get-tuple-element.38), channel_id=1, source_target_pairs={{0,8},{8,16},{16,24},{24,0},{1,9},{9,17},{17,25},{25,1},{2,10},{10... | collective-permute-start | bytes 835592 | tf_op jit(solution)/shard_map/ppermute | solution.py:188
  94.4 11.9 %collective-permute-start.20 = (f16[64,2176]{1,0:T(8,128)(2,1)S(1)}, f16[64,2176]{1,0:T(8,128)(2,1)S(1)}, u32[]{:S(2)}, u32[]{:S(2)}) collective-permute-start(f16[64,2176]{1,0:T(8,128)(2,1)S(1)} %get-tuple-element.37), channel_id=1, source_target_pairs={{0,24},{8,0},{16,8},{24,16},{1,25},{9,1},{17,9},{25,17},{2,26},{10... | collective-permute-start | bytes 835592 | tf_op jit(solution)/shard_map/ppermute | solution.py:188
  108.0 10.7 %collective-permute-start.21 = (f16[64,2176]{1,0:T(8,128)(2,1)S(1)}, f16[64,2176]{1,0:T(8,128)(2,1)S(1)}, u32[]{:S(2)}, u32[]{:S(2)}) collective-permute-start(f16[64,2176]{1,0:T(8,128)(2,1)S(1)} %convert_element_type.36), channel_id=1, source_target_pairs={{0,8},{8,16},{16,24},{24,0},{1,9},{9,17},{17,25},{25,1},{2,10},{10... | collective-permute-start | bytes 835592 | tf_op jit(solution)/shard_map/ppermute | solution.py:188
  109.5 14.7 %collective-permute-start.22 = (f16[64,2176]{1,0:T(8,128)(2,1)S(1)}, f16[64,2176]{1,0:T(8,128)(2,1)S(1)}, u32[]{:S(2)}, u32[]{:S(2)}) collective-permute-start(f16[64,2176]{1,0:T(8,128)(2,1)S(1)} %convert_element_type.36), channel_id=1, source_target_pairs={{0,16},{8,24},{16,0},{24,8},{1,17},{9,25},{17,1},{25,9},{2,18},{10... | collective-permute-start | bytes 835592 | tf_op jit(solution)/shard_map/ppermute | solution.py:188
  112.1 12.4 %collective-permute-start.23 = (f16[64,2176]{1,0:T(8,128)(2,1)S(1)}, f16[64,2176]{1,0:T(8,128)(2,1)S(1)}, u32[]{:S(2)}, u32[]{:S(2)}) collective-permute-start(f16[64,2176]{1,0:T(8,128)(2,1)S(1)} %convert_element_type.36), channel_id=1, source_target_pairs={{0,24},{8,0},{16,8},{24,16},{1,25},{9,1},{17,9},{25,17},{2,26},{10... | collective-permute-start | bytes 835592 | tf_op jit(solution)/shard_map/ppermute | solution.py:188
  125.8 7.4 %collective-permute-start.24 = (f32[264,256]{1,0:T(8,128)S(1)}, f32[264,256]{1,0:T(8,128)S(1)}, u32[]{:S(2)}, u32[]{:S(2)}) collective-permute-start(f32[264,256]{1,0:T(8,128)S(1)} %get-tuple-element.23), channel_id=1, source_target_pairs={{0,4},{4,0},{1,5},{5,1},{2,6},{6,2},{3,7},{7,3},{8,12},{12,8},{9,1... | collective-permute-start | bytes 811016 | tf_op jit(solution)/shard_map/ppermute | solution.py:260
  136.4 34.5 %all-to-all-start.1 = ((f16[32,64,256]{2,1,0:T(8,128)(2,1)}), f16[32,64,256]{2,1,0:T(8,128)(2,1)S(1)}, u32[]{:S(2)}, u32[]{:S(2)}) async-start(f16[32,64,256]{2,1,0:T(8,128)(2,1)} %bitcast.12), calls=%async_computation.1 | async-start | bytes 2097152 | tf_op jit(solution)/shard_map/all_to_all | solution.py:272
  144.6 20.1 %collective-permute-start.25 = (f32[8,256]{1,0:T(8,128)S(1)}, f32[8,256]{1,0:T(8,128)S(1)}, u32[]{:S(2)}, u32[]{:S(2)}) collective-permute-start(f32[8,256]{1,0:T(8,128)S(1)} %get-tuple-element.26), channel_id=1, source_target_pairs={{0,32},{32,64},{64,96},{96,0},{1,33},{33,65},{65,97},{97,1},{2,34}... | collective-permute-start | bytes 24584 | tf_op jit(solution)/shard_map/ppermute | solution.py:188
  146.4 23.2 %collective-permute-start.26 = (f32[8,256]{1,0:T(8,128)S(1)}, f32[8,256]{1,0:T(8,128)S(1)}, u32[]{:S(2)}, u32[]{:S(2)}) collective-permute-start(f32[8,256]{1,0:T(8,128)S(1)} %get-tuple-element.26), channel_id=1, source_target_pairs={{0,64},{32,96},{64,0},{96,32},{1,65},{33,97},{65,1},{97,33},{2,66}... | collective-permute-start | bytes 24584 | tf_op jit(solution)/shard_map/ppermute | solution.py:188
  148.8 20.8 %collective-permute-start.27 = (f32[8,256]{1,0:T(8,128)S(1)}, f32[8,256]{1,0:T(8,128)S(1)}, u32[]{:S(2)}, u32[]{:S(2)}) collective-permute-start(f32[8,256]{1,0:T(8,128)S(1)} %get-tuple-element.26), channel_id=1, source_target_pairs={{0,96},{32,0},{64,32},{96,64},{1,97},{33,1},{65,33},{97,65},{2,98}... | collective-permute-start | bytes 24584 | tf_op jit(solution)/shard_map/ppermute | solution.py:188
